TPU v7x, 32 devices: a whole 2x2x4 slice. The times are simulated.
32 devices in a mesh: tok: 8 (over z, y), tp: 4 (over x, core).
Axes of the slice: x: 2, y: 2, z: 4, core: 2. Of those that a mesh axis runs over, the one named last changes fastest.
Arguments:
- inputs: bfloat16 [6144, 2304], P('tok'), may hold values from -7 to 7
- seq_lengths: int32 [4], replicated, may hold values from 1024 to 2048, as said below
- gain_attn_in: bfloat16 [2304], P('tok'), may hold values from 0.5 to 1.5
- gain_attn_out: bfloat16 [2304], P('tok'), may hold values from 0.5 to 1.5
- gain_ffn_in: bfloat16 [2304], P('tok'), may hold values from 0.5 to 1.5
- gain_ffn_out: bfloat16 [2304], P('tok'), may hold values from 0.5 to 1.5
- w_query: bfloat16 [2304, 2048], P('tok', 'tp'), may hold values from -2 to 2
- w_key: bfloat16 [2304, 1024], P('tok', 'tp'), may hold values from -2 to 2
- w_value: bfloat16 [2304, 1024], P('tok', 'tp'), may hold values from -0.125 to 0.125
- w_out: bfloat16 [2304, 2048], P('tok', 'tp'), may hold values from -0.125 to 0.125
- w_gate: bfloat16 [2304, 9216], P('tok', 'tp'), may hold values from -0.125 to 0.125
- w_up: bfloat16 [2304, 9216], P('tok', 'tp'), may hold values from -0.125 to 0.125
- w_down: bfloat16 [2304, 9216], P('tok', 'tp'), may hold values from -0.0625 to 0.0625
- out_grad: bfloat16 [6144, 2304], P('tok'), may hold values from -6 to 6
Outputs:
- layer_out: bfloat16 [6144, 2304], P('tok')
- input_grad: float32 [6144, 2304], P('tok')
- gain_attn_in_grad: float32 [2304], P('tok')
- gain_attn_out_grad: float32 [2304], P('tok')
- gain_ffn_in_grad: float32 [2304], P('tok')
- gain_ffn_out_grad: float32 [2304], P('tok')
- w_query_grad: float32 [2304, 2048], P('tok', 'tp')
- w_key_grad: float32 [2304, 1024], P('tok', 'tp')
- w_value_grad: float32 [2304, 1024], P('tok', 'tp')
- w_out_grad: float32 [2304, 2048], P('tok', 'tp')
- w_gate_grad: float32 [2304, 9216], P('tok', 'tp')
- w_up_grad: float32 [2304, 9216], P('tok', 'tp')
- w_down_grad: float32 [2304, 9216], P('tok', 'tp')
Inputs may be any that keep to these rules, and one draw needn't show every extreme that they name: `seq_lengths`: lengths of the 4 packed sequences in order; they sum to 6144, and entries 2k and 2k + 1 sum to 3072.
All inputs are finite; a program needn't handle non-finite values.
Results may differ from a plain program's by a relative error of at most 0.023.
Values may be sent and summed in bfloat16 or wider, within the bound.
A program may use at most 256 MiB of HBM per device.

v0:
```python
from functools import partial

import jax
import jax.numpy as jnp
from jax import lax
from jax.sharding import PartitionSpec as P

HEAD_DIM = 256
REACH = 3


softcap_limit = 50.0
norm_epsilon = 1e-06
rope_base = 10000.0
negative_fill = -1e30


def passed_along(array, axis, by):
    length = lax.axis_size(axis)
    pairs = [(i, i + by) for i in range(length) if 0 <= i + by < length]
    return lax.ppermute(array, axis, pairs)


def norm_apply(values, gain_vec):
    inverse = lax.rsqrt(jnp.mean(values * values, axis=-1, keepdims=True) + norm_epsilon)
    unit_vals = values * inverse
    return (unit_vals * gain_vec, unit_vals, inverse)


def norm_back(gradient, gain_vec, unit_vals, inverse):
    scaled = gradient * gain_vec
    input_part = inverse * (
        scaled - unit_vals * jnp.mean(scaled * unit_vals, axis=-1, keepdims=True)
    )
    return (input_part, jnp.sum(gradient * unit_vals, axis=0))


def token_places(seq_lengths, tok_index):
    starts = jnp.cumsum(seq_lengths) - seq_lengths
    passed = tok_index[:, None] >= starts[None, :]
    segment = jnp.sum(passed.astype(jnp.int32), axis=1) - 1
    seq_start = jnp.max(jnp.where(passed, starts[None, :], 0), axis=1)
    return (segment, tok_index - seq_start)


def rope_tables(position):
    half_dim = HEAD_DIM // 2
    freqs = rope_base ** (-2.0 * jnp.arange(half_dim).astype(jnp.float32) / HEAD_DIM)
    theta = position.astype(jnp.float32)[:, None] * freqs[None, :]
    return (jnp.cos(theta)[:, None, :], jnp.sin(theta)[:, None, :])


def rotate(values, cosine, sine_tab):
    half_dim = values.shape[-1] // 2
    front_half = values[..., :half_dim]
    back_half = values[..., half_dim:]
    return jnp.concatenate(
        [front_half * cosine - back_half * sine_tab, back_half * cosine + front_half * sine_tab],
        axis=-1,
    )


def rotate_back(values, cosine, sine_tab):
    half_dim = values.shape[-1] // 2
    front_half = values[..., :half_dim]
    back_half = values[..., half_dim:]
    return jnp.concatenate(
        [front_half * cosine + back_half * sine_tab, back_half * cosine - front_half * sine_tab],
        axis=-1,
    )


def fetch_window(kv_pair, offset):
    return passed_along((kv_pair[0], kv_pair[1]), "tok", offset)


def return_grads(kv_pair, offset):
    return (
        passed_along(kv_pair[0].astype(jnp.bfloat16), "tok", -offset).astype(jnp.float32),
        passed_along(kv_pair[1].astype(jnp.bfloat16), "tok", -offset).astype(jnp.float32),
    )


def contract_rows(left, right):
    return lax.dot_general(
        left, right, (((0,), (0,)), ((), ())), preferred_element_type=jnp.float32
    )


def contract_cols(left, right):
    return lax.dot_general(
        left, right, (((1,), (1,)), ((), ())), preferred_element_type=jnp.float32
    )


def local(
    inputs,
    seq_lengths,
    gain_attn_in,
    gain_attn_out,
    gain_ffn_in,
    gain_ffn_out,
    w_query,
    w_key,
    w_value,
    w_out,
    w_gate,
    w_up,
    w_down,
    out_grad,
):
    row_count = inputs.shape[0]
    head_cols = w_query.shape[1]
    kv_cols = w_key.shape[1]
    heads_local = head_cols // HEAD_DIM
    kv_local = kv_cols // HEAD_DIM
    group = heads_local // kv_local
    score_scale = HEAD_DIM ** (-0.5)
    tok_place = lax.axis_index("tok")
    own_index = tok_place * row_count + jnp.arange(row_count, dtype=jnp.int32)
    key_index = (tok_place - REACH) * row_count + jnp.arange(
        (REACH + 1) * row_count, dtype=jnp.int32
    )
    seg_query, pos_query = token_places(seq_lengths, own_index)
    seg_key, pos_key = token_places(seq_lengths, key_index)
    allowed = (seg_query[:, None] == seg_key[None, :]) & (pos_key[None, :] <= pos_query[:, None])
    cosine, sine_tab = rope_tables(pos_query)
    attn_mats = (
        lax.all_gather(w_query, "tok", axis=0, tiled=True),
        lax.all_gather(w_key, "tok", axis=0, tiled=True),
        lax.all_gather(w_value, "tok", axis=0, tiled=True),
        lax.all_gather(w_out, "tok", axis=0, tiled=True),
        lax.all_gather(gain_attn_in, "tok", axis=0, tiled=True),
        lax.all_gather(gain_attn_out, "tok", axis=0, tiled=True),
    )
    gain_one = attn_mats[4].astype(jnp.float32)
    gain_two = attn_mats[5].astype(jnp.float32)
    resid = inputs.astype(jnp.float32)
    normed_one, unit_one, inv_one = norm_apply(resid, gain_one)
    hidden_one = normed_one.astype(jnp.bfloat16)
    query_pre = jnp.dot(hidden_one, attn_mats[0], preferred_element_type=jnp.float32)
    key_pre = jnp.dot(hidden_one, attn_mats[1], preferred_element_type=jnp.float32)
    value_vec = jnp.dot(hidden_one, attn_mats[2], preferred_element_type=jnp.float32).astype(
        jnp.bfloat16
    )
    query_rot = rotate(
        query_pre.reshape(row_count, heads_local, HEAD_DIM), cosine, sine_tab
    ).astype(jnp.bfloat16)
    key_rot = (
        rotate(key_pre.reshape(row_count, kv_local, HEAD_DIM), cosine, sine_tab)
        .reshape(row_count, kv_cols)
        .astype(jnp.bfloat16)
    )
    key_parts = [key_rot]
    value_parts = [value_vec]
    for offset in range(1, REACH + 1):
        arrived = fetch_window((key_rot, value_vec), offset)
        key_parts.insert(0, arrived[0])
        value_parts.insert(0, arrived[1])
    key_grp = jnp.concatenate(key_parts, axis=0).reshape(-1, kv_local, HEAD_DIM)
    value_grp = jnp.concatenate(value_parts, axis=0).reshape(-1, kv_local, HEAD_DIM)
    query_grp = query_rot.reshape(row_count, kv_local, group, HEAD_DIM)

    def capped_scores():
        raw_scores = jnp.einsum(
            "qgjd,kgd->gjqk", query_grp, key_grp, preferred_element_type=jnp.float32
        )
        capped = softcap_limit * jnp.tanh(raw_scores * score_scale / softcap_limit)
        return (capped, jnp.where(allowed[None, None], capped, negative_fill))

    capped_fwd, masked_fwd = capped_scores()
    row_max = jnp.max(masked_fwd, axis=-1, keepdims=True)
    exponent = jnp.exp(masked_fwd - row_max)
    row_total = jnp.sum(exponent, axis=-1, keepdims=True)
    log_total = row_max + jnp.log(row_total)
    probs_low = (exponent / row_total).astype(jnp.bfloat16)
    attended = (
        jnp.einsum("gjqk,kgd->qgjd", probs_low, value_grp, preferred_element_type=jnp.float32)
        .reshape(row_count, head_cols)
        .astype(jnp.bfloat16)
    )
    attn_part = contract_cols(attended, attn_mats[3])
    attn_total = lax.psum(attn_part, "tp")
    normed_two, unit_two, inv_two = norm_apply(attn_total, gain_two)
    resid_mid = resid + normed_two
    ffn_mats = (
        lax.all_gather(w_gate, "tok", axis=0, tiled=True),
        lax.all_gather(w_up, "tok", axis=0, tiled=True),
        lax.all_gather(w_down, "tok", axis=0, tiled=True),
        lax.all_gather(gain_ffn_in, "tok", axis=0, tiled=True),
        lax.all_gather(gain_ffn_out, "tok", axis=0, tiled=True),
    )
    gain_three = ffn_mats[3].astype(jnp.float32)
    gain_four = ffn_mats[4].astype(jnp.float32)
    normed_three, unit_three, inv_three = norm_apply(resid_mid, gain_three)
    hidden_two = normed_three.astype(jnp.bfloat16)
    gate_vals = jnp.dot(hidden_two, ffn_mats[0], preferred_element_type=jnp.float32)
    up_vals = jnp.dot(hidden_two, ffn_mats[1], preferred_element_type=jnp.float32)
    gelu_tanh = partial(jax.nn.gelu, approximate=True)
    activated, gelu_pull = jax.vjp(gelu_tanh, gate_vals)
    inner = (activated * up_vals).astype(jnp.bfloat16)
    ffn_part = contract_cols(inner, ffn_mats[2])
    ffn_total = lax.psum(ffn_part, "tp")
    normed_four, unit_four, inv_four = norm_apply(ffn_total, gain_four)
    layer_out = (resid_mid + normed_four).astype(jnp.bfloat16)
    ffn_mats = (
        lax.all_gather(w_gate, "tok", axis=0, tiled=True),
        lax.all_gather(w_up, "tok", axis=0, tiled=True),
        lax.all_gather(w_down, "tok", axis=0, tiled=True),
        lax.all_gather(gain_ffn_in, "tok", axis=0, tiled=True),
        lax.all_gather(gain_ffn_out, "tok", axis=0, tiled=True),
    )
    grad_out = out_grad.astype(jnp.float32)
    d_ffn, grad_four = norm_back(grad_out, gain_four, unit_four, inv_four)
    d_ffn_low = d_ffn.astype(jnp.bfloat16)
    d_inner = jnp.dot(d_ffn_low, ffn_mats[2], preferred_element_type=jnp.float32)
    grad_down = contract_rows(d_ffn_low, inner)
    grad_upvals = (d_inner * activated).astype(jnp.bfloat16)
    grad_gatevals = gelu_pull(d_inner * up_vals)[0].astype(jnp.bfloat16)
    grad_gate = contract_rows(hidden_two, grad_gatevals)
    grad_upmat = contract_rows(hidden_two, grad_upvals)
    d_hidden_part = contract_cols(grad_gatevals, ffn_mats[0]) + contract_cols(
        grad_upvals, ffn_mats[1]
    )
    d_hidden_two = lax.psum(d_hidden_part, "tp")
    mid_add, grad_three = norm_back(d_hidden_two, gain_three, unit_three, inv_three)
    d_mid = grad_out + mid_add
    ffn_sums = (
        lax.psum_scatter(
            grad_gate.astype(jnp.bfloat16), "tok", scatter_dimension=0, tiled=True
        ).astype(jnp.float32),
        lax.psum_scatter(
            grad_upmat.astype(jnp.bfloat16), "tok", scatter_dimension=0, tiled=True
        ).astype(jnp.float32),
        lax.psum_scatter(
            grad_down.astype(jnp.bfloat16), "tok", scatter_dimension=0, tiled=True
        ).astype(jnp.float32),
        lax.psum_scatter(
            grad_three.astype(jnp.bfloat16), "tok", scatter_dimension=0, tiled=True
        ).astype(jnp.float32),
        lax.psum_scatter(
            grad_four.astype(jnp.bfloat16), "tok", scatter_dimension=0, tiled=True
        ).astype(jnp.float32),
    )
    attn_mats = (
        lax.all_gather(w_query, "tok", axis=0, tiled=True),
        lax.all_gather(w_key, "tok", axis=0, tiled=True),
        lax.all_gather(w_value, "tok", axis=0, tiled=True),
        lax.all_gather(w_out, "tok", axis=0, tiled=True),
        lax.all_gather(gain_attn_in, "tok", axis=0, tiled=True),
        lax.all_gather(gain_attn_out, "tok", axis=0, tiled=True),
    )
    d_attn, grad_two = norm_back(d_mid, gain_two, unit_two, inv_two)
    d_attn_low = d_attn.astype(jnp.bfloat16)
    grad_outmat = contract_rows(d_attn_low, attended)
    d_attended = jnp.dot(d_attn_low, attn_mats[3], preferred_element_type=jnp.float32).astype(
        jnp.bfloat16
    )
    d_att_grp = d_attended.reshape(row_count, kv_local, group, HEAD_DIM)
    capped_bwd, masked_bwd = capped_scores()
    probs = jnp.exp(masked_bwd - log_total)
    probs_back = probs.astype(jnp.bfloat16)
    d_probs = jnp.einsum("qgjd,kgd->gjqk", d_att_grp, value_grp, preferred_element_type=jnp.float32)
    d_value_win = jnp.einsum(
        "gjqk,qgjd->kgd", probs_back, d_att_grp, preferred_element_type=jnp.float32
    )
    row_delta = jnp.sum(probs * d_probs, axis=-1, keepdims=True)
    ratio_cap = capped_bwd / softcap_limit
    d_raw = (probs * (d_probs - row_delta) * (1.0 - ratio_cap * ratio_cap) * score_scale).astype(
        jnp.bfloat16
    )
    d_query_rot = jnp.einsum("gjqk,kgd->qgjd", d_raw, key_grp, preferred_element_type=jnp.float32)
    d_key_win = jnp.einsum("gjqk,qgjd->kgd", d_raw, query_grp, preferred_element_type=jnp.float32)
    d_key_slots = d_key_win.reshape(REACH + 1, row_count, kv_cols)
    d_value_slots = d_value_win.reshape(REACH + 1, row_count, kv_cols)
    key_total = d_key_slots[REACH]
    value_total = d_value_slots[REACH]
    for offset in range(1, REACH + 1):
        arrived = return_grads((d_key_slots[REACH - offset], d_value_slots[REACH - offset]), offset)
        key_total = key_total + arrived[0]
        value_total = value_total + arrived[1]
    d_query = (
        rotate_back(d_query_rot.reshape(row_count, heads_local, HEAD_DIM), cosine, sine_tab)
        .reshape(row_count, head_cols)
        .astype(jnp.bfloat16)
    )
    d_key = (
        rotate_back(key_total.reshape(row_count, kv_local, HEAD_DIM), cosine, sine_tab)
        .reshape(row_count, kv_cols)
        .astype(jnp.bfloat16)
    )
    d_value = value_total.astype(jnp.bfloat16)
    grad_query = contract_rows(hidden_one, d_query)
    grad_key = contract_rows(hidden_one, d_key)
    grad_value = contract_rows(hidden_one, d_value)
    d_hidden_one_part = (
        contract_cols(d_query, attn_mats[0])
        + contract_cols(d_key, attn_mats[1])
        + contract_cols(d_value, attn_mats[2])
    )
    d_hidden_one = lax.psum(d_hidden_one_part.astype(jnp.bfloat16), "tp").astype(jnp.float32)
    input_add, grad_one = norm_back(d_hidden_one, gain_one, unit_one, inv_one)
    input_grad = d_mid + input_add
    attn_sums = (
        lax.psum_scatter(
            grad_query.astype(jnp.bfloat16), "tok", scatter_dimension=0, tiled=True
        ).astype(jnp.float32),
        lax.psum_scatter(
            grad_key.astype(jnp.bfloat16), "tok", scatter_dimension=0, tiled=True
        ).astype(jnp.float32),
        lax.psum_scatter(
            grad_value.astype(jnp.bfloat16), "tok", scatter_dimension=0, tiled=True
        ).astype(jnp.float32),
        lax.psum_scatter(
            grad_outmat.astype(jnp.bfloat16), "tok", scatter_dimension=0, tiled=True
        ).astype(jnp.float32),
        lax.psum_scatter(
            grad_one.astype(jnp.bfloat16), "tok", scatter_dimension=0, tiled=True
        ).astype(jnp.float32),
        lax.psum_scatter(
            grad_two.astype(jnp.bfloat16), "tok", scatter_dimension=0, tiled=True
        ).astype(jnp.float32),
    )
    return (
        layer_out,
        input_grad,
        attn_sums[4],
        attn_sums[5],
        ffn_sums[3],
        ffn_sums[4],
        attn_sums[0],
        attn_sums[1],
        attn_sums[2],
        attn_sums[3],
        ffn_sums[0],
        ffn_sums[1],
        ffn_sums[2],
    )


def solution(mesh):
    in_specs = (
        P("tok", None),
        P(),
        P("tok"),
        P("tok"),
        P("tok"),
        P("tok"),
        P("tok", "tp"),
        P("tok", "tp"),
        P("tok", "tp"),
        P("tok", "tp"),
        P("tok", "tp"),
        P("tok", "tp"),
        P("tok", "tp"),
        P("tok", None),
    )
    out_specs = (
        P("tok", None),
        P("tok", None),
        P("tok"),
        P("tok"),
        P("tok"),
        P("tok"),
        P("tok", "tp"),
        P("tok", "tp"),
        P("tok", "tp"),
        P("tok", "tp"),
        P("tok", "tp"),
        P("tok", "tp"),
        P("tok", "tp"),
    )
    return jax.shard_map(local, mesh=mesh, in_specs=in_specs, out_specs=out_specs, check_vma=False)
```

profile of v0, /device:TPU:0, one launch (start us, length us, event | category | flops | bytes accessed | tf_op | source)
XLA Modules:
  0.0 2218.1 jit_solution(15859377549336782163)
XLA Ops:
  23.4 39.7 %all-reduce.9 = (bf16[2304]{0:T(1024)(128)(2,1)}, bf16[2304]{0:T(1024)(128)(2,1)}, bf16[2304]{0:T(1024)(128)(2,1)}, bf16[2304]{0:T(1024)(128)(2,1)}) all-reduce(bf16[2304]{0:T(1024)(128)(2,1)} %dynamic-update-slice, bf16[2304]{0:T(1024)(128)(2,1)} %copy-done.40, ...), channel_id=1, replica_groups=mesh['tok'=8,'tp'=4] {'tok'}, use_global_device_ids=true, to_apply=%add | all-reduce | flops 9216 | bytes 36864
  80.0 17.7 all-gather.10.cloned.1.call-done
  113.1 49.7 %all-gather.12.cloned.1.call-done = bf16[2304,512]{1,0:T(8,128)(2,1)} async-done(((bf16[288,512]{1,0:T(8,128)(2,1)}), bf16[2304,512]{1,0:T(8,128)(2,1)}) %all-gather.12.cloned.1.call-update) | async-done | bytes 2359312 | tf_op jit(solution)/shard_map/all_gather | solution.py:129
  204.6 24.7 %all-gather.14.cloned.1.call-done = bf16[2304,512]{1,0:T(8,128)(2,1)} async-done(((bf16[288,512]{1,0:T(8,128)(2,1)}), bf16[2304,512]{1,0:T(8,128)(2,1)}) %all-gather.14.cloned.1.call-update) | async-done | bytes 2359312 | tf_op jit(solution)/shard_map/all_gather | solution.py:132
  240.4 126.9 %all-reduce.15.cloned.1.call-done = f32[768,2304]{1,0:T(8,128)} async-done(((f32[768,2304]{1,0:T(8,128)}), f32[768,2304]{1,0:T(8,128)}) %all-reduce.15.cloned.1.call-update) | async-done | bytes 7077904 | tf_op jit(solution)/shard_map/psum | solution.py:183
  378.4 143.6 %all-gather.16.cloned.1.call-done = bf16[2304,2304]{1,0:T(8,128)(2,1)} async-done(((bf16[288,2304]{1,0:T(8,128)(2,1)}), bf16[2304,2304]{1,0:T(8,128)(2,1)}) %all-gather.16.cloned.1.call-update) | async-done | bytes 10616848 | tf_op jit(solution)/shard_map/all_gather | solution.py:187
  535.8 139.1 %all-gather.18.cloned.1.call-done = bf16[2304,2304]{1,0:T(8,128)(2,1)} async-done(((bf16[288,2304]{1,0:T(8,128)(2,1)}), bf16[2304,2304]{1,0:T(8,128)(2,1)}) %all-gather.18.cloned.1.call-update) | async-done | bytes 10616848 | tf_op jit(solution)/shard_map/all_gather | solution.py:188
  674.9 15.6 multiply_convert_fusion.2
  690.5 137.2 %all-gather.20.cloned.1.call-done = bf16[2304,2304]{1,0:T(8,128)(2,1)} async-done(((bf16[288,2304]{1,0:T(8,128)(2,1)}), bf16[2304,2304]{1,0:T(8,128)(2,1)}) %all-gather.20.cloned.1.call-update) | async-done | bytes 10616848 | tf_op jit(solution)/shard_map/all_gather | solution.py:189
  844.2 129.2 %all-reduce.17.cloned.1.call-done = f32[768,2304]{1,0:T(8,128)} async-done(((f32[768,2304]{1,0:T(8,128)}), f32[768,2304]{1,0:T(8,128)}) %all-reduce.17.cloned.1.call-update) | async-done | bytes 7077904 | tf_op jit(solution)/shard_map/psum | solution.py:203
  986.7 20.0 multiply_convert_fusion.1
  1006.7 15.1 fusion.115
  1021.8 16.0 convolution_add_fusion
  1039.2 131.4 %all-reduce.19.cloned.1.call-done = f32[768,2304]{1,0:T(8,128)} async-done(((f32[768,2304]{1,0:T(8,128)}), f32[768,2304]{1,0:T(8,128)}) %all-reduce.19.cloned.1.call-update) | async-done | bytes 7077904 | tf_op jit(solution)/shard_map/psum | solution.py:225
  1210.8 17.6 fusion.2
  1228.4 15.2 fusion.1
  1359.3 21.9 all-reduce.21.cloned.1.call-done
  1385.9 38.7 %all-reduce.8 = (bf16[2304]{0:T(1024)(128)(2,1)}, bf16[2304]{0:T(1024)(128)(2,1)}, bf16[2304]{0:T(1024)(128)(2,1)}, bf16[2304]{0:T(1024)(128)(2,1)}) all-reduce(bf16[2304]{0:T(1024)(128)(2,1)} %get-tuple-element.19, bf16[2304]{0:T(1024)(128)(2,1)} %get-tuple-element.15, ...), channel_id=2, replica_groups=mesh['tok'=8,'tp'=4] {'tok'}, use_global_device_ids=true, to_apply=%region_21.22.clone | all-reduce | flops 9216 | bytes 36864
  1450.4 65.4 %reduce-scatter.10.cloned.1.call-done = bf16[288,256]{1,0:T(8,128)(2,1)} async-done(((bf16[2304,256]{1,0:T(8,128)(2,1)}), bf16[288,256]{1,0:T(8,128)(2,1)}) %reduce-scatter.10.cloned.1.call-update) | async-done | bytes 147472 | tf_op jit(solution)/shard_map/reduce_scatter | solution.py:308
  1517.4 70.4 %reduce-scatter.14.cloned.1.call-done = bf16[288,512]{1,0:T(8,128)(2,1)} async-done(((bf16[2304,512]{1,0:T(8,128)(2,1)}), bf16[288,512]{1,0:T(8,128)(2,1)}) %reduce-scatter.14.cloned.1.call-update) | async-done | bytes 294928 | tf_op jit(solution)/shard_map/reduce_scatter | solution.py:314
  1589.7 70.1 %reduce-scatter.8.cloned.1.call-done = bf16[288,512]{1,0:T(8,128)(2,1)} async-done(((bf16[2304,512]{1,0:T(8,128)(2,1)}), bf16[288,512]{1,0:T(8,128)(2,1)}) %reduce-scatter.8.cloned.1.call-update) | async-done | bytes 294928 | tf_op jit(solution)/shard_map/reduce_scatter | solution.py:305
  1661.6 180.7 %reduce-scatter.18.cloned.1.call-done = bf16[288,2304]{1,0:T(8,128)(2,1)} async-done(((bf16[2304,2304]{1,0:T(8,128)(2,1)}), bf16[288,2304]{1,0:T(8,128)(2,1)}) %reduce-scatter.18.cloned.1.call-update) | async-done | bytes 1327120 | tf_op jit(solution)/shard_map/reduce_scatter | solution.py:232
  1845.3 180.0 %reduce-scatter.16.cloned.1.call-done = bf16[288,2304]{1,0:T(8,128)(2,1)} async-done(((bf16[2304,2304]{1,0:T(8,128)(2,1)}), bf16[288,2304]{1,0:T(8,128)(2,1)}) %reduce-scatter.16.cloned.1.call-update) | async-done | bytes 1327120 | tf_op jit(solution)/shard_map/reduce_scatter | solution.py:229
  2028.3 179.5 %reduce-scatter.20.cloned.1.call-done = bf16[288,2304]{1,0:T(8,128)(2,1)} async-done(((bf16[2304,2304]{1,0:T(8,128)(2,1)}), bf16[288,2304]{1,0:T(8,128)(2,1)}) %reduce-scatter.20.cloned.1.call-update) | async-done | bytes 1327120 | tf_op jit(solution)/shard_map/reduce_scatter | solution.py:235
  (262 shorter events, 355.7 us)
Async XLA Ops:
  7.9 89.8 %all-gather.10.cloned.1.call-start = ((), (), s32[]{:S(2)}) async-start(), calls=%async_computation.8 | async-start | bytes 1327104 | tf_op jit(solution)/shard_map/all_gather | solution.py:130
  8.7 154.2 %all-gather.12.cloned.1.call-start = ((), (), s32[]{:S(2)}) async-start(), calls=%async_computation.9 | async-start | bytes 2654208 | tf_op jit(solution)/shard_map/all_gather | solution.py:129
  9.4 219.9 %all-gather.14.cloned.1.call-start = ((), (), s32[]{:S(2)}) async-start(), calls=%async_computation.10 | async-start | bytes 2654208 | tf_op jit(solution)/shard_map/all_gather | solution.py:132
  10.0 357.3 %all-reduce.15.cloned.1.call-start = ((), (), s32[]{:S(2)}) async-start(), calls=%async_computation.11 | async-start | bytes 14155776 | tf_op jit(solution)/shard_map/psum | solution.py:183
  75.8 117.1 %collective-permute-start.2 = (bf16[768,256]{1,0:T(8,128)(2,1)}, bf16[768,256]{1,0:T(8,128)(2,1)}, u32[]{:S(2)}, u32[]{:S(2)}) collective-permute-start(bf16[768,256]{1,0:T(8,128)(2,1)} %convolution_convert_fusion.8), channel_id=1, source_target_pairs={{0,4},{4,8},{8,12},{12,16},{16,20},{20,24},{24,28},{1,5},{5,9},{9,... | collective-permute-start | bytes 1179656 | tf_op jit(solution)/shard_map/ppermute | solution.py:21
  77.9 115.0 %collective-permute-start.1 = (bf16[768,256]{1,0:T(8,128)(2,1)}, bf16[768,256]{1,0:T(8,128)(2,1)}, u32[]{:S(2)}, u32[]{:S(2)}) collective-permute-start(bf16[768,256]{1,0:T(8,128)(2,1)} %convolution_convert_fusion.8), channel_id=1, source_target_pairs={{0,8},{4,12},{8,16},{12,20},{16,24},{20,28},{1,9},{5,13},{9,17},{1... | collective-permute-start | bytes 1179656 | tf_op jit(solution)/shard_map/ppermute | solution.py:21
  102.8 65.9 %collective-permute-start.5 = (bf16[768,256]{0,1:T(8,128)(2,1)}, bf16[768,256]{0,1:T(8,128)(2,1)}, u32[]{:S(2)}, u32[]{:S(2)}) collective-permute-start(bf16[768,256]{0,1:T(8,128)(2,1)} %maximum_bitcast_fusion.6), channel_id=1, source_target_pairs={{0,4},{4,8},{8,12},{12,16},{16,20},{20,24},{24,28},{1,5},{5,9},{9,... | collective-permute-start | bytes 1179656 | tf_op jit(solution)/shard_map/ppermute | solution.py:21
  105.7 72.3 %collective-permute-start.4 = (bf16[768,256]{0,1:T(8,128)(2,1)}, bf16[768,256]{0,1:T(8,128)(2,1)}, u32[]{:S(2)}, u32[]{:S(2)}) collective-permute-start(bf16[768,256]{0,1:T(8,128)(2,1)} %maximum_bitcast_fusion.6), channel_id=1, source_target_pairs={{0,8},{4,12},{8,16},{12,20},{16,24},{20,28},{1,9},{5,13},{9,17},{1... | collective-permute-start | bytes 1179656 | tf_op jit(solution)/shard_map/ppermute | solution.py:21
  110.1 68.0 %collective-permute-start.3 = (bf16[768,256]{0,1:T(8,128)(2,1)}, bf16[768,256]{0,1:T(8,128)(2,1)}, u32[]{:S(2)}, u32[]{:S(2)}) collective-permute-start(bf16[768,256]{0,1:T(8,128)(2,1)} %maximum_bitcast_fusion.6), channel_id=1, source_target_pairs={{0,12},{4,16},{8,20},{12,24},{16,28},{1,13},{5,17},{9,21},{13,25},... | collective-permute-start | bytes 1179656 | tf_op jit(solution)/shard_map/ppermute | solution.py:21
  236.3 285.8 %all-gather.16.cloned.1.call-start = ((), (), s32[]{:S(2)}) async-start(), calls=%async_computation.12 | async-start | bytes 11943936 | tf_op jit(solution)/shard_map/all_gather | solution.py:187
  236.9 438.1 %all-gather.18.cloned.1.call-start = ((), (), s32[]{:S(2)}) async-start(), calls=%async_computation.13 | async-start | bytes 11943936 | tf_op jit(solution)/shard_map/all_gather | solution.py:188
  237.6 590.2 %all-gather.20.cloned.1.call-start = ((), (), s32[]{:S(2)}) async-start(), calls=%async_computation.14 | async-start | bytes 11943936 | tf_op jit(solution)/shard_map/all_gather | solution.py:189
  238.4 735.1 %all-reduce.17.cloned.1.call-start = ((), (), s32[]{:S(2)}) async-start(), calls=%async_computation.15 | async-start | bytes 14155776 | tf_op jit(solution)/shard_map/psum | solution.py:203
  842.7 327.9 %all-reduce.19.cloned.1.call-start = ((), (), s32[]{:S(2)}) async-start(), calls=%async_computation.16 | async-start | bytes 14155776 | tf_op jit(solution)/shard_map/psum | solution.py:225
  1037.8 343.3 %all-reduce.21.cloned.1.call-start = ((), (), s32[]{:S(2)}) async-start(), calls=%async_computation.17 | async-start | bytes 7077888 | tf_op jit(solution)/shard_map/psum | solution.py:301
  1208.2 76.9 %collective-permute-start.9 = (bf16[768,256]{0,1:T(8,128)(2,1)}, bf16[768,256]{0,1:T(8,128)(2,1)S(1)}, u32[]{:S(2)}, u32[]{:S(2)}) collective-permute-start(bf16[768,256]{0,1:T(8,128)(2,1)} %get-tuple-element.46), channel_id=1, source_target_pairs={{4,0},{8,4},{12,8},{16,12},{20,16},{24,20},{28,24},{5,1},{9,5},{13... | collective-permute-start | bytes 1179656 | tf_op jit(solution)/shard_map/ppermute | solution.py:21
  1209.5 75.7 %collective-permute-start.11 = (bf16[768,256]{0,1:T(8,128)(2,1)}, bf16[768,256]{0,1:T(8,128)(2,1)}, u32[]{:S(2)}, u32[]{:S(2)}) collective-permute-start(bf16[768,256]{0,1:T(8,128)(2,1)} %get-tuple-element.47), channel_id=1, source_target_pairs={{12,0},{16,4},{20,8},{24,12},{28,16},{13,1},{17,5},{21,9},{25,13},... | collective-permute-start | bytes 1179656 | tf_op jit(solution)/shard_map/ppermute | solution.py:21
  1299.1 149.7 %reduce-scatter.12.cloned.1.call-start = ((), (), s32[]{:S(2)}) async-start(), calls=%async_computation.20 | async-start | bytes 1327104 | tf_op jit(solution)/shard_map/reduce_scatter | solution.py:311
  1302.7 213.1 %reduce-scatter.10.cloned.1.call-start = ((), (), s32[]{:S(2)}) async-start(), calls=%async_computation.19 | async-start | bytes 1327104 | tf_op jit(solution)/shard_map/reduce_scatter | solution.py:308
  1306.2 281.6 %reduce-scatter.14.cloned.1.call-start = ((), (), s32[]{:S(2)}) async-start(), calls=%async_computation.21 | async-start | bytes 2654208 | tf_op jit(solution)/shard_map/reduce_scatter | solution.py:314
  1312.0 347.8 %reduce-scatter.8.cloned.1.call-start = ((), (), s32[]{:S(2)}) async-start(), calls=%async_computation.18 | async-start | bytes 2654208 | tf_op jit(solution)/shard_map/reduce_scatter | solution.py:305
  1317.1 525.2 %reduce-scatter.18.cloned.1.call-start = ((), (), s32[]{:S(2)}) async-start(), calls=%async_computation.23 | async-start | bytes 11943936 | tf_op jit(solution)/shard_map/reduce_scatter | solution.py:232
  1330.9 694.3 %reduce-scatter.16.cloned.1.call-start = ((), (), s32[]{:S(2)}) async-start(), calls=%async_computation.22 | async-start | bytes 11943936 | tf_op jit(solution)/shard_map/reduce_scatter | solution.py:229
  1344.7 863.2 %reduce-scatter.20.cloned.1.call-start = ((), (), s32[]{:S(2)}) async-start(), calls=%async_computation.24 | async-start | bytes 11943936 | tf_op jit(solution)/shard_map/reduce_scatter | solution.py:235
  (58 other events, 1397.7 us)
Sparse Core Ops, SparseCore 0:
  10.2 43.9 all-gather.7
  56.4 41.2 all-gather.9
  99.9 62.8 all-gather.11
  164.9 64.4 all-gather.13
  236.4 130.8 all-reduce.14
  369.3 152.6 all-gather.15
  524.2 150.6 all-gather.17
  677.1 150.6 all-gather.19
  842.8 130.5 all-reduce.16
  1038.0 132.5 all-reduce.18
  1299.3 81.8 all-reduce.20
  1384.4 64.3 reduce-scatter.11
  1452.8 62.9 reduce-scatter.9
  1519.7 68.0 reduce-scatter.13
  1591.8 67.9 reduce-scatter.7
  1663.2 179.0 reduce-scatter.17
  1846.2 179.0 reduce-scatter.15
  2028.7 179.0 reduce-scatter.19
where the time goes:
time: 2230 us; the launch traced here: 2220 us
  waiting for transfers between devices  1710 us (77%)
  matrix products  240 us (11%)
  other arithmetic  123 us (6%)
  blocking collectives  78.4 us (4%)
  starting transfers between devices  32.9 us (1%)
    reduce_scatter x1, waiting for transfers between devices, local(): lax.psum_scatter(grad_upmat.astype(jnp.bfloat16), 'tok', scatter_dimensio...  181 us
    reduce_scatter x1, waiting for transfers between devices, local(): lax.psum_scatter(grad_gate.astype(jnp.bfloat16), 'tok', scatter_dimension...  180 us
    reduce_scatter x1, waiting for transfers between devices, local(): lax.psum_scatter(grad_down.astype(jnp.bfloat16), 'tok', scatter_dimension...  180 us
    all_gather x1, waiting for transfers between devices, local(): lax.all_gather(w_gate, 'tok', axis=0, tiled=True)  144 us
    all_gather x1, waiting for transfers between devices, local(): lax.all_gather(w_up, 'tok', axis=0, tiled=True)  139 us
    all_gather x1, waiting for transfers between devices, local(): lax.all_gather(w_down, 'tok', axis=0, tiled=True)  137 us
    psum x1, waiting for transfers between devices, local(): d_hidden_two = lax.psum(d_hidden_part, 'tp')  131 us
    psum x1, waiting for transfers between devices, local(): ffn_total = lax.psum(ffn_part, 'tp')  129 us
  transfers between devices with their start and end apart: 30, of which 21 were waited for; matrix products, arithmetic and copies ran while one was open for 11% of the time, Pallas kernels for 0%

commit v1 on v0

v1 whole, which is shorter than its diff:
```python
from functools import partial

import jax
import jax.numpy as jnp
from jax import lax
from jax.sharding import PartitionSpec as P

HEAD_DIM = 256
QUAD = 4
REACH = 2

softcap_limit = 50.0
norm_epsilon = 1e-06
rope_base = 10000.0
negative_fill = -1e30

f32 = jnp.float32
bf16 = jnp.bfloat16


def norm_parts(values):
    inverse = lax.rsqrt(jnp.mean(values * values, axis=-1, keepdims=True) + norm_epsilon)
    return values * inverse, inverse


def norm_back(gradient, gain_vec, unit_vals, inverse):
    scaled = gradient * gain_vec
    input_part = inverse * (
        scaled - unit_vals * jnp.mean(scaled * unit_vals, axis=-1, keepdims=True)
    )
    return (input_part, jnp.sum(gradient * unit_vals, axis=0))


def token_places(seq_lengths, tok_index):
    count = seq_lengths.shape[0]
    before = jnp.arange(count)[:, None] > jnp.arange(count)[None, :]
    starts = jnp.sum(jnp.where(before, seq_lengths[None, :], 0), axis=1)
    passed = tok_index[:, None] >= starts[None, :]
    segment = jnp.sum(passed.astype(jnp.int32), axis=1) - 1
    seq_start = jnp.max(jnp.where(passed, starts[None, :], 0), axis=1)
    return (segment, tok_index - seq_start)


def rope_tables(position):
    half_dim = HEAD_DIM // 2
    freqs = rope_base ** (-2.0 * jnp.arange(half_dim).astype(f32) / HEAD_DIM)
    theta = position.astype(f32)[:, None] * freqs[None, :]
    return (jnp.cos(theta)[:, None, :], jnp.sin(theta)[:, None, :])


def rotate(values, cosine, sine_tab):
    half_dim = values.shape[-1] // 2
    front_half = values[..., :half_dim]
    back_half = values[..., half_dim:]
    return jnp.concatenate(
        [front_half * cosine - back_half * sine_tab, back_half * cosine + front_half * sine_tab],
        axis=-1,
    )


def contract_rows(left, right):
    return lax.dot_general(
        left, right, (((0,), (0,)), ((), ())), preferred_element_type=f32
    )


def contract_cols(left, right):
    return lax.dot_general(
        left, right, (((1,), (1,)), ((), ())), preferred_element_type=f32
    )


def pick(array, index, axis=0):
    return lax.dynamic_index_in_dim(array, index, axis, keepdims=False)


def put(buffer, block, index):
    return lax.dynamic_update_index_in_dim(buffer, block, index, 0)


def local(
    inputs,
    seq_lengths,
    gain_attn_in,
    gain_attn_out,
    gain_ffn_in,
    gain_ffn_out,
    w_query,
    w_key,
    w_value,
    w_out,
    w_gate,
    w_up,
    w_down,
    out_grad,
):
    n = lax.axis_size("tok")
    m = n // 4
    width = inputs.shape[1]
    rows = inputs.shape[0]
    part = rows // 4
    tok = lax.axis_index("tok")
    tpi = lax.axis_index("tp")
    z, y = tok // m, tok % m
    zlo, zhi = z % 2, z // 2
    x, core = tpi // 2, tpi % 2
    wrows = w_query.shape[0]
    head_cols = w_query.shape[1]
    kv_cols = w_key.shape[1]
    heads = head_cols // HEAD_DIM
    units = w_gate.shape[1]
    half = units // 2

    def over_tok(fn):
        pairs = [(t, fn(t)) for t in range(n)]
        return lambda a: lax.ppermute(a, "tok", pairs)

    def over_tp(fn):
        pairs = [(t, fn(t)) for t in range(4)]
        return lambda a: lax.ppermute(a, "tp", pairs)

    def z_shift(a, k):
        return over_tok(lambda t: ((t // m + k) % 4) * m + t % m)(a)

    def y_shift(a, k):
        return over_tok(lambda t: (t // m) * m + (t % m + k) % m)(a)

    to_zlo = over_tok(lambda t: ((t // m) ^ 1) * m + t % m)
    to_zhi = over_tok(lambda t: ((t // m) ^ 2) * m + t % m)
    to_core = over_tp(lambda t: t ^ 1)
    to_x = over_tp(lambda t: t ^ 2)

    def within_quad(a, by):
        pairs = [(t, t + by) for t in range(n) if 0 <= t + by < n and t // QUAD == (t + by) // QUAD]
        return lax.ppermute(a, "tok", pairs)

    def place_of(dz, dy):
        return ((z ^ dz) * m) + (y - dy) % m

    gains = jnp.stack([gain_attn_in, gain_attn_out, gain_ffn_in, gain_ffn_out])
    gains_all = lax.all_gather(gains, "tok", axis=1, tiled=True).astype(f32)
    gain_one, gain_two, gain_three, gain_four = (gains_all[i] for i in range(4))

    attn_own = jnp.concatenate([w_query, w_key, w_value, w_out], axis=1)
    attn_z = [attn_own] + [z_shift(attn_own, k) for k in range(1, 4)]
    attn_buf = jnp.zeros((n,) + attn_own.shape, bf16)
    for k in range(4):
        zs = (z - k) % 4
        attn_buf = put(attn_buf, attn_z[k], zs * m + y)
        for j in range(1, m):
            attn_buf = put(attn_buf, y_shift(attn_z[k], j), zs * m + (y - j) % m)
    attn_mat = attn_buf.reshape(width, -1)
    qkv_cols = head_cols + 2 * kv_cols
    qkv_mat = attn_mat[:, :qkv_cols]
    out_mat = attn_mat[:, qkv_cols:]

    def halves(a, index):
        return lax.dynamic_slice_in_dim(a, index * half, half, 1)

    gu_keep = jnp.concatenate([halves(w_gate, zlo), halves(w_up, zlo)], axis=1)
    gu_send = jnp.concatenate([halves(w_gate, 1 - zlo), halves(w_up, 1 - zlo)], axis=1)
    d_keep, d_send = halves(w_down, zlo), halves(w_down, 1 - zlo)
    gu_keep, gu_send, d_keep, d_send, attn_z = lax.optimization_barrier(
        (gu_keep, gu_send, d_keep, d_send, attn_z)
    )

    def ffn_gather(keep, send):
        buffer = jnp.zeros((n,) + keep.shape, bf16)
        for r, block in ((0, keep), (1, to_zlo(send))):
            for h in range(2):
                piece = block if h == 0 else to_zhi(block)
                buffer = put(buffer, piece, place_of(r + 2 * h, 0))
                for j in range(1, m):
                    buffer = put(buffer, y_shift(piece, j), place_of(r + 2 * h, j))
        return buffer.reshape(width, -1)

    gu_mat = ffn_gather(gu_keep, gu_send)
    down_mat = ffn_gather(d_keep, d_send)

    def own_slice(a):
        return lax.dynamic_slice_in_dim(a, tpi * part, part, 0)

    def gather_tp(a):
        buffer = jnp.zeros((4,) + a.shape, a.dtype)
        other = to_x(a)
        pair = to_core(jnp.stack([a, other]))
        for k, block in enumerate((a, pair[0], other, pair[1])):
            buffer = put(buffer, block, tpi ^ k)
        return buffer.reshape((-1,) + a.shape[1:])

    def gather_pair(a):
        a_z = to_zlo(a)
        a_x = to_x(a)
        a_xz = to_x(a_z)
        side = jnp.concatenate([a, a_z, a_x, a_xz])
        return jnp.concatenate([side, to_core(side)])

    def reduce_pair(compute):
        far = compute(1).astype(bf16)
        near = compute(0) + to_core(far).astype(f32)
        near = near.reshape(2, 2, part, width)
        z_part = near[0, 1] + to_x(near[1, 1].astype(bf16)).astype(f32)
        own = near[0, 0] + to_x(near[1, 0].astype(bf16)).astype(f32)
        return own + to_zlo(z_part.astype(bf16)).astype(f32)

    def reduce_tp(compute):
        far = compute(1 - core).astype(bf16)
        near = compute(core) + to_core(far).astype(f32)
        near = near.reshape(2, part, width)
        return pick(near, x) + to_x(pick(near, 1 - x).astype(bf16)).astype(f32)

    def core_rows(a, c):
        return pick(a.reshape(2, 2, part, a.shape[1]), c, 1).reshape(2 * part, a.shape[1])

    own_index = tok * rows + jnp.arange(rows, dtype=jnp.int32)
    key_index = (tok - REACH) * rows + jnp.arange((REACH + 1) * rows, dtype=jnp.int32)
    seg_query, pos_query = token_places(seq_lengths, own_index)
    seg_key, pos_key = token_places(seq_lengths, key_index)
    allowed = (seg_query[:, None] == seg_key[None, :]) & (pos_key[None, :] <= pos_query[:, None])
    cosine, sine_tab = rope_tables(pos_query)
    score_scale = HEAD_DIM ** (-0.5)

    unit_one_all, _ = norm_parts(inputs.astype(f32))
    hidden_one = (unit_one_all * gain_one).astype(bf16)
    qkv = jnp.dot(hidden_one, qkv_mat, preferred_element_type=f32)
    qk_rot = rotate(
        qkv[:, : head_cols + kv_cols].reshape(rows, -1, HEAD_DIM), cosine, sine_tab
    ).astype(bf16)
    query_rot = qk_rot[:, :heads]
    key_value = jnp.concatenate(
        [qk_rot[:, heads:].reshape(rows, kv_cols), qkv[:, head_cols + kv_cols :].astype(bf16)], axis=1
    )
    window = [within_quad(key_value, by) for by in range(REACH, 0, -1)] + [key_value]
    window = jnp.concatenate(window, axis=0)
    key_win, value_win = window[:, :kv_cols], window[:, kv_cols:]

    def capped_scores():
        raw = jnp.einsum("qjd,kd->jqk", query_rot, key_win, preferred_element_type=f32)
        capped = softcap_limit * jnp.tanh(raw * score_scale / softcap_limit)
        return (capped, jnp.where(allowed[None], capped, negative_fill))

    capped_fwd, masked_fwd = capped_scores()
    row_max = jnp.max(masked_fwd, axis=-1, keepdims=True)
    exponent = jnp.exp(masked_fwd - row_max)
    row_total = jnp.sum(exponent, axis=-1, keepdims=True)
    log_total = row_max + jnp.log(row_total)
    probs_low = (exponent / row_total).astype(bf16)
    attended = (
        jnp.einsum("jqk,kd->qjd", probs_low, value_win, preferred_element_type=f32)
        .reshape(rows, head_cols)
        .astype(bf16)
    )
    attn = reduce_tp(lambda c: contract_cols(core_rows(attended, c), out_mat))

    resid = own_slice(inputs).astype(f32)
    unit_two, inv_two = norm_parts(attn)
    resid_mid = resid + unit_two * gain_two
    unit_three, inv_three = norm_parts(resid_mid)
    hidden_two = gather_pair((unit_three * gain_three).astype(bf16))
    gate_up = jnp.dot(hidden_two, gu_mat, preferred_element_type=f32)
    gate_vals, up_vals = gate_up[:, :half], gate_up[:, half:]
    activated, gelu_pull = jax.vjp(partial(jax.nn.gelu, approximate=True), gate_vals)
    inner = (activated * up_vals).astype(bf16)
    ffn = reduce_pair(lambda k: contract_cols(jnp.split(inner, 2)[k], down_mat))
    unit_four, inv_four = norm_parts(ffn)
    layer_out = gather_tp((resid_mid + unit_four * gain_four).astype(bf16))

    grad_out = own_slice(out_grad).astype(f32)
    d_ffn, grad_four = norm_back(grad_out, gain_four, unit_four, inv_four)
    d_ffn_all = gather_pair(d_ffn.astype(bf16))
    d_inner = jnp.dot(d_ffn_all, down_mat, preferred_element_type=f32)

    def scatter_y(grad):
        blocks = grad.reshape(4, m, wrows, -1)
        total = pick(blocks, y, 1).astype(f32)
        for j in range(1, m):
            total = total + y_shift(pick(blocks, (y + j) % m, 1), j).astype(f32)
        return total

    def ffn_scatter(grad):
        total = scatter_y(grad.astype(bf16)).reshape(2, 2, wrows, -1)
        total = pick(total, zhi) + to_zhi(pick(total, 1 - zhi).astype(bf16)).astype(f32)
        return pick(total, zlo), to_zlo(pick(total, 1 - zlo).astype(bf16)).astype(f32)

    def sides(own, other):
        return jnp.where(
            zlo == 0,
            jnp.concatenate([own, other], axis=1),
            jnp.concatenate([other, own], axis=1),
        )

    out_down = sides(*ffn_scatter(contract_rows(d_ffn_all, inner)))
    grad_upvals = (d_inner * activated).astype(bf16)
    grad_gatevals = gelu_pull(d_inner * up_vals)[0].astype(bf16)
    grad_gu = jnp.concatenate([grad_gatevals, grad_upvals], axis=1)
    d_hidden_two = reduce_pair(lambda k: contract_cols(jnp.split(grad_gu, 2)[k], gu_mat))
    gu_own, gu_other = ffn_scatter(contract_rows(hidden_two, grad_gu))
    out_gate = sides(gu_own[:, :half], gu_other[:, :half])
    out_up = sides(gu_own[:, half:], gu_other[:, half:])

    mid_add, grad_three = norm_back(d_hidden_two, gain_three, unit_three, inv_three)
    d_mid = grad_out + mid_add

    d_attn, grad_two = norm_back(d_mid, gain_two, unit_two, inv_two)
    d_attn_low = gather_tp(d_attn.astype(bf16))

    def attn_scatter(grad):
        total = scatter_y(grad.astype(bf16))
        own = pick(total, z)
        for k in range(1, 4):
            own = own + z_shift(pick(total, (z + k) % 4).astype(bf16), k).astype(f32)
        return own

    out_wout = attn_scatter(contract_rows(d_attn_low, attended))
    d_attended = jnp.dot(d_attn_low, out_mat, preferred_element_type=f32).astype(bf16)
    d_att = d_attended.reshape(rows, heads, HEAD_DIM)
    capped_bwd, masked_bwd = capped_scores()
    probs = jnp.exp(masked_bwd - log_total)
    d_probs = jnp.einsum("qjd,kd->jqk", d_att, value_win, preferred_element_type=f32)
    d_value_win = jnp.einsum("jqk,qjd->kd", probs.astype(bf16), d_att, preferred_element_type=f32)
    row_delta = jnp.sum(probs * d_probs, axis=-1, keepdims=True)
    ratio_cap = capped_bwd / softcap_limit
    d_raw = (probs * (d_probs - row_delta) * (1.0 - ratio_cap * ratio_cap) * score_scale).astype(
        bf16
    )
    d_query_rot = jnp.einsum("jqk,kd->qjd", d_raw, key_win, preferred_element_type=f32)
    d_key_win = jnp.einsum("jqk,qjd->kd", d_raw, query_rot, preferred_element_type=f32)
    d_window = jnp.concatenate([d_key_win, d_value_win], axis=1).reshape(REACH + 1, rows, -1)
    d_kv = d_window[REACH]
    for by in range(1, REACH + 1):
        d_kv = d_kv + within_quad(d_window[REACH - by].astype(bf16), -by).astype(f32)
    d_query = rotate(d_query_rot, cosine, -sine_tab).reshape(rows, head_cols)
    d_key = rotate(d_kv[:, :kv_cols].reshape(rows, -1, HEAD_DIM), cosine, -sine_tab).reshape(
        rows, kv_cols
    )
    d_qkv = jnp.concatenate([d_query, d_key, d_kv[:, kv_cols:]], axis=1).astype(bf16)
    out_qkv = attn_scatter(contract_rows(hidden_one, d_qkv))
    d_hidden_one = reduce_tp(lambda c: contract_cols(core_rows(d_qkv, c), qkv_mat))
    unit_one, inv_one = norm_parts(resid)
    input_add, grad_one = norm_back(d_hidden_one, gain_one, unit_one, inv_one)
    input_grad = gather_tp(d_mid + input_add)

    gain_grads = lax.psum(jnp.stack([grad_one, grad_two, grad_three, grad_four]), ("tok", "tp"))
    gain_grads = lax.dynamic_slice_in_dim(gain_grads, tok * wrows, wrows, 1)
    return (
        layer_out,
        input_grad,
        gain_grads[0],
        gain_grads[1],
        gain_grads[2],
        gain_grads[3],
        out_qkv[:, :head_cols],
        out_qkv[:, head_cols : head_cols + kv_cols],
        out_qkv[:, head_cols + kv_cols :],
        out_wout,
        out_gate,
        out_up,
        out_down,
    )


def solution(mesh):
    weight = P("tok", "tp")
    in_specs = (P("tok", None), P()) + (P("tok"),) * 4 + (weight,) * 7 + (P("tok", None),)
    out_specs = (P("tok", None),) * 2 + (P("tok"),) * 4 + (weight,) * 7
    return jax.shard_map(local, mesh=mesh, in_specs=in_specs, out_specs=out_specs, check_vma=False)
```

time: 2230 us -> 1320 us (0.59)
  waiting for transfers between devices: 1710 us -> 589 us
  local copies, waits for them, and re-layouts: 16.1 us -> 129 us
  starting transfers between devices: 32.9 us -> 113 us
  blocking collectives: 78.4 us -> 158 us
  other arithmetic: 123 us -> 87.8 us
    reduce_scatter x7 -> x0, waiting for transfers between devices: 757 us -> none  [the longest x1 181 us: local(): lax.psum_scatter(grad_upmat.astype(jnp.bfloat16), 'tok', scatter_dimensio...]
    ppermute x12 -> x65, waiting for transfers between devices: 26.9 us -> 589 us  [the longest x39 382 us: over_tok(): return lambda a: lax.ppermute(a, 'tok', pairs)]
    all_gather x7 -> x0, waiting for transfers between devices: 512 us -> none  [the longest x1 144 us: local(): lax.all_gather(w_gate, 'tok', axis=0, tiled=True)]
    psum x4 -> x0, waiting for transfers between devices: 409 us -> none  [the longest x1 131 us: local(): d_hidden_two = lax.psum(d_hidden_part, 'tp')]
    all_gather x0 -> x1, blocking collectives: none -> 89.9 us  [local(): gains_all = lax.all_gather(gains, 'tok', axis=1, tiled=True).astype(f32)]
    ppermute x12 -> x65, starting transfers between devices: 31.8 us -> 113 us  [the longest x39 84.5 us: over_tok(): return lambda a: lax.ppermute(a, 'tok', pairs)]
    unnamed x2 -> x0, blocking collectives: 78.4 us -> none
    psum x0 -> x1, blocking collectives: none -> 67.9 us  [local(): lax.psum(jnp.stack([grad_one, grad_two, grad_three, grad_four]), ('tok',...]
  transfers between devices with their start and end apart: 30 -> 65, of which waited for: 21 -> 27; matrix products, arithmetic and copies ran while one was open for 11% -> 28% of each run, Pallas kernels for 0% -> 0%
where the time goes in v1:
time: 1320 us; the launch traced here: 1310 us
  waiting for transfers between devices  589 us (45%)
  matrix products  235 us (18%)
  blocking collectives  158 us (12%)
  local copies, waits for them, and re-layouts  129 us (10%)
  starting transfers between devices  113 us (9%)
  other arithmetic  87.8 us (7%)
    ppermute x39, waiting for transfers between devices, over_tok(): return lambda a: lax.ppermute(a, 'tok', pairs)  382 us
    ppermute x22, waiting for transfers between devices, over_tp(): return lambda a: lax.ppermute(a, 'tp', pairs)  148 us
    all_gather x1, blocking collectives, local(): gains_all = lax.all_gather(gains, 'tok', axis=1, tiled=True).astype(f32)  89.9 us
    ppermute x39, starting transfers between devices, over_tok(): return lambda a: lax.ppermute(a, 'tok', pairs)  84.5 us
    psum x1, blocking collectives, local(): lax.psum(jnp.stack([grad_one, grad_two, grad_three, grad_four]), ('tok',...  67.9 us
    dot_general x8, matrix products, contract_cols(): lax.dot_general(left, right, (((1,), (1,)), ((), ())), preferred_element_...  60 us
    ppermute x4, waiting for transfers between devices, within_quad(): return lax.ppermute(a, 'tok', pairs)  59.6 us
    dynamic_update_slice x33, local copies, waits for them, and re-layouts, put(): return lax.dynamic_update_index_in_dim(buffer, block, index, 0)  43 us
  transfers between devices with their start and end apart: 65, of which 27 were waited for; matrix products, arithmetic and copies ran while one was open for 28% of the time, Pallas kernels for 0%

profile of v1, /device:TPU:0, one launch (start us, length us, event | category | flops | bytes accessed | tf_op | source)
XLA Modules:
  0.0 1313.6 jit_solution(7451910992184512229)
XLA Ops:
  16.4 89.9 %all-gather = bf16[8,288,4]{1,2,0:T(4,128)(2,1)S(1)} all-gather(bf16[1,288,4]{1,2,0:T(4,128)(2,1)S(1)} %maximum_bitcast_fusion.1), channel_id=1, replica_groups=mesh['tok'=8,'tp'=4] {'tok'}, dimensions={0}, use_global_device_ids=true | all-gather | bytes 20736 | tf_op jit(solution)/shard_map/all_gather | solution.py:141
  139.5 57.1 %collective-permute-done.2 = bf16[288,1536]{1,0:T(8,128)(2,1)S(1)} collective-permute-done((bf16[288,1536]{1,0:T(8,128)(2,1)}, bf16[288,1536]{1,0:T(8,128)(2,1)S(1)}, u32[]{:S(2)}, u32[]{:S(2)}) %collective-permute-start.2) | collective-permute-done | bytes 884768 | tf_op jit(solution)/shard_map/ppermute | solution.py:116
  199.9 15.7 %collective-permute-done.4 = bf16[288,1536]{1,0:T(8,128)(2,1)S(1)} collective-permute-done((bf16[288,1536]{1,0:T(8,128)(2,1)}, bf16[288,1536]{1,0:T(8,128)(2,1)S(1)}, u32[]{:S(2)}, u32[]{:S(2)}) %collective-permute-start.4) | collective-permute-done | bytes 884768 | tf_op jit(solution)/shard_map/ppermute | solution.py:116
  262.2 20.6 %collective-permute-start.24 = (bf16[288,1152]{1,0:T(8,128)(2,1)}, bf16[288,1152]{1,0:T(8,128)(2,1)}, u32[]{:S(2)}, u32[]{:S(2)}) collective-permute-start(bf16[288,1152]{1,0:T(8,128)(2,1)} %collective-permute-done.23), channel_id=1, source_target_pairs={{0,4},{4,0},{8,12},{12,8},{16,20},{20,16},{24,28},{28,24},{1,5},{5... | collective-permute-start | bytes 1990664 | tf_op jit(solution)/shard_map/ppermute | solution.py:116
  342.9 70.2 %collective-permute-done.16 = bf16[288,2304]{1,0:T(8,128)(2,1)S(1)} collective-permute-done((bf16[288,2304]{1,0:T(8,128)(2,1)}, bf16[288,2304]{1,0:T(8,128)(2,1)S(1)}, u32[]{:S(2)}, u32[]{:S(2)}) %collective-permute-start.16) | collective-permute-done | bytes 1327136 | tf_op jit(solution)/shard_map/ppermute | solution.py:116
  439.6 18.5 %collective-permute-done.28 = bf16[288,1152]{1,0:T(8,128)(2,1)S(1)} collective-permute-done((bf16[288,1152]{1,0:T(8,128)(2,1)S(1)}, bf16[288,1152]{1,0:T(8,128)(2,1)S(1)}, u32[]{:S(2)}, u32[]{:S(2)}) %collective-permute-start.28) | collective-permute-done | bytes 663584 | tf_op jit(solution)/shard_map/ppermute | solution.py:116
  477.1 19.0 %collective-permute-done.13 = bf16[192,2304]{1,0:T(8,128)(2,1)S(1)} collective-permute-done((bf16[192,2304]{1,0:T(8,128)(2,1)S(1)}, bf16[192,2304]{1,0:T(8,128)(2,1)S(1)}, u32[]{:S(2)}, u32[]{:S(2)}) %collective-permute-start.13) | collective-permute-done | bytes 884768 | tf_op jit(solution)/shard_map/ppermute | solution.py:120
  499.9 29.7 %collective-permute-done.21 = bf16[288,2304]{1,0:T(8,128)(2,1)S(1)} collective-permute-done((bf16[288,2304]{1,0:T(8,128)(2,1)S(1)}, bf16[288,2304]{1,0:T(8,128)(2,1)S(1)}, u32[]{:S(2)}, u32[]{:S(2)}) %collective-permute-start.21) | collective-permute-done | bytes 1327136 | tf_op jit(solution)/shard_map/ppermute | solution.py:116
  535.7 19.2 %fusion.153 = f32[1536,2304]{1,0:T(8,128)S(1)} fusion(bf16[1536,2304]{1,0:T(8,128)(2,1)} %copy-done.61, bf16[2304,2304]{1,0:T(8,128)(2,1)S(1)} %bitcast.348), kind=kOutput, calls=%fused_computation.345 | convolution fusion | flops 16307453952 | bytes 31850496 | tf_op jit(solution)/shard_map/dot_general | solution.py:260
  585.2 20.5 %collective-permute-done.31 = bf16[192,2304]{1,0:T(8,128)(2,1)S(1)} collective-permute-done((bf16[192,2304]{1,0:T(8,128)(2,1)S(1)}, bf16[192,2304]{1,0:T(8,128)(2,1)S(1)}, u32[]{:S(2)}, u32[]{:S(2)}) %collective-permute-start.31) | collective-permute-done | bytes 884768 | tf_op jit(solution)/shard_map/ppermute | solution.py:120
  605.9 17.9 %collective-permute-done.30 = bf16[192,2304]{1,0:T(8,128)(2,1)S(1)} collective-permute-done((bf16[192,2304]{1,0:T(8,128)(2,1)S(1)}, bf16[192,2304]{1,0:T(8,128)(2,1)S(1)}, u32[]{:S(2)}, u32[]{:S(2)}) %collective-permute-start.30) | collective-permute-done | bytes 884768 | tf_op jit(solution)/shard_map/ppermute | solution.py:120
  630.7 17.4 %collective-permute-done.35 = bf16[192,2304]{1,0:T(8,128)(2,1)S(1)} collective-permute-done((bf16[192,2304]{1,0:T(8,128)(2,1)S(1)}, bf16[192,2304]{1,0:T(8,128)(2,1)S(1)}, u32[]{:S(2)}, u32[]{:S(2)}) %collective-permute-start.35) | collective-permute-done | bytes 884768 | tf_op jit(solution)/shard_map/ppermute | solution.py:116
  649.6 17.8 %collective-permute-done.37 = bf16[192,2304]{1,0:T(8,128)(2,1)S(1)} collective-permute-done((bf16[192,2304]{1,0:T(8,128)(2,1)S(1)}, bf16[192,2304]{1,0:T(8,128)(2,1)S(1)}, u32[]{:S(2)}, u32[]{:S(2)}) %collective-permute-start.37) | collective-permute-done | bytes 884768 | tf_op jit(solution)/shard_map/ppermute | solution.py:120
  703.5 21.9 %multiply_convert_fusion = (bf16[1536,1152]{1,0:T(8,128)(2,1)}, bf16[1536,1152]{1,0:T(8,128)(2,1)}) fusion(f32[1536,2304]{1,0:T(8,128)} %copy-done.4, bf16[1536,2304]{1,0:T(8,128)(2,1)} %constant_dynamic-update-slice_fusion.9, bf16[2304,1152]{1,0:T(8,128)(2,1)} %bitcast.40), kind=kOutput, calls=%fused_computation.40 | convolution fusion | flops 8196194304 | bytes 33619968 | tf_op jit(solution)/shard_map/dot_general | solution.py:271
  780.3 22.7 %convolution_convert_fusion = bf16[2304,2304]{1,0:T(8,128)(2,1)} fusion(bf16[1536,2304]{1,0:T(8,128)(2,1)} %copy-done.61, bf16[1536,1152]{1,0:T(8,128)(2,1)S(1)} %copy-done.83, bf16[1536,1152]{1,0:T(8,128)(2,1)} %get-tuple-element.61), kind=kOutput, calls=%fused_computation.1 | convolution fusion | flops 16326918144 | bytes 24772608 | tf_op jit(solution)/shard_map/dot_general | solution.py:62
  845.7 37.5 %collective-permute-done.63 = bf16[2,288,1152]{2,1,0:T(8,128)(2,1)S(1)} collective-permute-done((bf16[2,288,1152]{2,1,0:T(8,128)(2,1)S(1)}, bf16[2,288,1152]{2,1,0:T(8,128)(2,1)S(1)}, u32[]{:S(2)}, u32[]{:S(2)}) %collective-permute-start.63) | collective-permute-done | bytes 1327136 | tf_op jit(solution)/shard_map/ppermute | solution.py:116
  886.0 46.1 %collective-permute-done.59 = bf16[4,288,2304]{2,1,0:T(8,128)(2,1)} collective-permute-done((bf16[4,288,2304]{2,1,0:T(8,128)(2,1)}, bf16[4,288,2304]{2,1,0:T(8,128)(2,1)}, u32[]{:S(2)}, u32[]{:S(2)}) %collective-permute-start.59) | collective-permute-done | bytes 5308448 | tf_op jit(solution)/shard_map/ppermute | solution.py:116
  964.8 29.3 %convolution_bitcast_fusion = f32[2304,256]{0,1:T(8,128)} fusion(f32[2304,768,2]{1,0,2:T(8,128)} %fusion.84, f32[2304,768,2]{1,0,2:T(8,128)} %copy-done.3, f32[2,768]{1,0:T(2,128)} %log_add_fusion, pred[768,2304]{0,1:T(8,128)(4,1)S(1)} %copy-done.14, bf16[768,3,128]{2,0,1:T(8,128)(2,1)} %copy-done.37, bf16[768,3,128]{2,0,1:T(8,128)(2,1)} %copy-done.36), kind=kOutput, calls=%fused_computation.64 | convolution fusion | flops 1870139136 | bytes 33626112 | tf_op jit(solution)/shard_map/jqk,qjd->kd/dot_general | solution.py:327
  1000.6 28.4 %fusion.73 = f32[768,2,256]{0,2,1:T(8,128)} fusion(f32[2304,768,2]{1,0,2:T(8,128)} %fusion.84, f32[2304,768,2]{1,0,2:T(8,128)} %copy-done.3, f32[2,768]{1,0:T(2,128)} %log_add_fusion, pred[768,2304]{0,1:T(8,128)(4,1)S(1)} %copy-done.14, bf16[2304,512]{1,0:T(8,128)(2,1)} %copy-done.16), kind=kOutput, calls=%fused_computation.155 | convolution fusion | flops 1868566272 | bytes 62926848 | tf_op jit(solution)/shard_map/jqk,kd->qjd/dot_general | solution.py:326
  1032.9 58.5 %collective-permute-done.46 = bf16[768,512]{0,1:T(8,128)(2,1)} collective-permute-done((bf16[768,512]{0,1:T(8,128)(2,1)}, bf16[768,512]{0,1:T(8,128)(2,1)}, u32[]{:S(2)}, u32[]{:S(2)}) %collective-permute-start.46) | collective-permute-done | bytes 786464 | tf_op jit(solution)/shard_map/ppermute | solution.py:135
  1121.6 17.8 %collective-permute-done.48 = bf16[192,2304]{1,0:T(8,128)(2,1)S(1)} collective-permute-done((bf16[192,2304]{1,0:T(8,128)(2,1)S(1)}, bf16[192,2304]{1,0:T(8,128)(2,1)S(1)}, u32[]{:S(2)}, u32[]{:S(2)}) %collective-permute-start.48) | collective-permute-done | bytes 884768 | tf_op jit(solution)/shard_map/ppermute | solution.py:120
  1153.3 31.2 %collective-permute-done.49 = f32[192,2304]{1,0:T(8,128)S(1)} collective-permute-done((f32[192,2304]{1,0:T(8,128)S(1)}, f32[192,2304]{1,0:T(8,128)S(1)}, u32[]{:S(2)}, u32[]{:S(2)}) %collective-permute-start.49) | collective-permute-done | bytes 1769504 | tf_op jit(solution)/shard_map/ppermute | solution.py:120
  1194.8 28.8 %collective-permute-done.51 = bf16[4,288,1024]{2,1,0:T(8,128)(2,1)S(1)} collective-permute-done((bf16[4,288,1024]{2,1,0:T(8,128)(2,1)S(1)}, bf16[4,288,1024]{2,1,0:T(8,128)(2,1)S(1)}, u32[]{:S(2)}, u32[]{:S(2)}) %collective-permute-start.51) | collective-permute-done | bytes 2359328 | tf_op jit(solution)/shard_map/ppermute | solution.py:116
  1233.7 67.9 %psum.7 = f32[4,2304]{1,0:T(4,128)} all-reduce(f32[4,2304]{1,0:T(4,128)} %pad_maximum_fusion.15), channel_id=1, replica_groups=mesh['tok'=8,'tp'=4] {'tok','tp'}, use_global_device_ids=true, to_apply=%region_21.22 | all-reduce | flops 9216 | bytes 73728 | tf_op jit(solution)/shard_map/psum | solution.py:343
  (503 shorter events, 507.4 us)
Async XLA Ops:
  4.6 126.5 %collective-permute-start.1 = (bf16[288,1536]{1,0:T(8,128)(2,1)S(1)}, bf16[288,1536]{1,0:T(8,128)(2,1)}, u32[]{:S(2)}, u32[]{:S(2)}) collective-permute-start(bf16[288,1536]{1,0:T(8,128)(2,1)S(1)} %constant_dynamic-update-slice_fusion), channel_id=1, source_target_pairs={{0,8},{4,12},{8,16},{12,20},{16,24},{20,28},{24,0},{28,4},{1,9},{5... | collective-permute-start | bytes 2654216 | tf_op jit(solution)/shard_map/ppermute | solution.py:116
  7.7 123.4 %collective-permute-start.3 = (bf16[288,1536]{1,0:T(8,128)(2,1)S(1)}, bf16[288,1536]{1,0:T(8,128)(2,1)}, u32[]{:S(2)}, u32[]{:S(2)}) collective-permute-start(bf16[288,1536]{1,0:T(8,128)(2,1)S(1)} %constant_dynamic-update-slice_fusion), channel_id=1, source_target_pairs={{0,16},{4,20},{8,24},{12,28},{16,0},{20,4},{24,8},{28,12},{1,17},{... | collective-permute-start | bytes 2654216 | tf_op jit(solution)/shard_map/ppermute | solution.py:116
  10.3 120.8 %collective-permute-start.5 = (bf16[288,1536]{1,0:T(8,128)(2,1)S(1)}, bf16[288,1536]{1,0:T(8,128)(2,1)}, u32[]{:S(2)}, u32[]{:S(2)}) collective-permute-start(bf16[288,1536]{1,0:T(8,128)(2,1)S(1)} %constant_dynamic-update-slice_fusion), channel_id=1, source_target_pairs={{0,24},{4,28},{8,0},{12,4},{16,8},{20,12},{24,16},{28,20},{1,25},{... | collective-permute-start | bytes 2654216 | tf_op jit(solution)/shard_map/ppermute | solution.py:116
  11.6 121.7 %collective-permute-start = (bf16[288,1536]{1,0:T(8,128)(2,1)S(1)}, bf16[288,1536]{1,0:T(8,128)(2,1)}, u32[]{:S(2)}, u32[]{:S(2)}) collective-permute-start(bf16[288,1536]{1,0:T(8,128)(2,1)S(1)} %constant_dynamic-update-slice_fusion), channel_id=1, source_target_pairs={{0,4},{4,0},{8,12},{12,8},{16,20},{20,16},{24,28},{28,24},{1,5},{5... | collective-permute-start | bytes 2654216 | tf_op jit(solution)/shard_map/ppermute | solution.py:116
  131.1 173.2 %collective-permute-start.22 = (bf16[288,1152]{1,0:T(8,128)(2,1)}, bf16[288,1152]{1,0:T(8,128)(2,1)}, u32[]{:S(2)}, u32[]{:S(2)}) collective-permute-start(bf16[288,1152]{1,0:T(8,128)(2,1)} %get-tuple-element.19), channel_id=1, source_target_pairs={{0,4},{4,0},{8,12},{12,8},{16,20},{20,16},{24,28},{28,24},{1,5},{5... | collective-permute-start | bytes 1990664 | tf_op jit(solution)/shard_map/ppermute | solution.py:116
  131.2 127.4 %collective-permute-start.23 = (bf16[288,1152]{1,0:T(8,128)(2,1)}, bf16[288,1152]{1,0:T(8,128)(2,1)}, u32[]{:S(2)}, u32[]{:S(2)}) collective-permute-start(bf16[288,1152]{1,0:T(8,128)(2,1)} %get-tuple-element.19), channel_id=1, source_target_pairs={{0,16},{4,20},{8,24},{12,28},{16,0},{20,4},{24,8},{28,12},{1,17},{... | collective-permute-start | bytes 1990664 | tf_op jit(solution)/shard_map/ppermute | solution.py:116
  131.3 211.7 %collective-permute-start.15 = (bf16[288,2304]{1,0:T(8,128)(2,1)}, bf16[288,2304]{1,0:T(8,128)(2,1)}, u32[]{:S(2)}, u32[]{:S(2)}) collective-permute-start(bf16[288,2304]{1,0:T(8,128)(2,1)} %pad_maximum_fusion.9), channel_id=1, source_target_pairs={{0,4},{4,0},{8,12},{12,8},{16,20},{20,16},{24,28},{28,24},{1,5},{5... | collective-permute-start | bytes 3981320 | tf_op jit(solution)/shard_map/ppermute | solution.py:116
  133.3 82.2 %collective-permute-start.4 = (bf16[288,1536]{1,0:T(8,128)(2,1)}, bf16[288,1536]{1,0:T(8,128)(2,1)S(1)}, u32[]{:S(2)}, u32[]{:S(2)}) collective-permute-start(bf16[288,1536]{1,0:T(8,128)(2,1)} %collective-permute-done.3), channel_id=1, source_target_pairs={{0,4},{4,0},{8,12},{12,8},{16,20},{20,16},{24,28},{28,24},{1,5},{5... | collective-permute-start | bytes 2654216 | tf_op jit(solution)/shard_map/ppermute | solution.py:116
  258.6 69.9 %collective-permute-start.18 = (bf16[288,2304]{1,0:T(8,128)(2,1)}, bf16[288,2304]{1,0:T(8,128)(2,1)}, u32[]{:S(2)}, u32[]{:S(2)}) collective-permute-start(bf16[288,2304]{1,0:T(8,128)(2,1)} %pad_maximum_fusion.10), channel_id=1, source_target_pairs={{0,8},{4,12},{8,0},{12,4},{16,24},{20,28},{24,16},{28,20},{1,9},{5... | collective-permute-start | bytes 3981320 | tf_op jit(solution)/shard_map/ppermute | solution.py:116
  308.5 104.6 %collective-permute-start.16 = (bf16[288,2304]{1,0:T(8,128)(2,1)}, bf16[288,2304]{1,0:T(8,128)(2,1)S(1)}, u32[]{:S(2)}, u32[]{:S(2)}) collective-permute-start(bf16[288,2304]{1,0:T(8,128)(2,1)} %pad_maximum_fusion.9), channel_id=1, source_target_pairs={{0,16},{4,20},{8,24},{12,28},{16,0},{20,4},{24,8},{28,12},{1,17},{... | collective-permute-start | bytes 3981320 | tf_op jit(solution)/shard_map/ppermute | solution.py:116
  328.5 98.9 %collective-permute-start.27 = (bf16[288,1152]{1,0:T(8,128)(2,1)}, bf16[288,1152]{1,0:T(8,128)(2,1)S(1)}, u32[]{:S(2)}, u32[]{:S(2)}) collective-permute-start(bf16[288,1152]{1,0:T(8,128)(2,1)} %collective-permute-done.25), channel_id=1, source_target_pairs={{0,16},{4,20},{8,24},{12,28},{16,0},{20,4},{24,8},{28,12},{1,17},{... | collective-permute-start | bytes 1990664 | tf_op jit(solution)/shard_map/ppermute | solution.py:116
  328.5 171.1 %collective-permute-start.19 = (bf16[288,2304]{1,0:T(8,128)(2,1)}, bf16[288,2304]{1,0:T(8,128)(2,1)S(1)}, u32[]{:S(2)}, u32[]{:S(2)}) collective-permute-start(bf16[288,2304]{1,0:T(8,128)(2,1)} %collective-permute-done.18), channel_id=1, source_target_pairs={{0,4},{4,0},{8,12},{12,8},{16,20},{20,16},{24,28},{28,24},{1,5},{5... | collective-permute-start | bytes 3981320 | tf_op jit(solution)/shard_map/ppermute | solution.py:116
  340.5 91.7 %collective-permute-start.10 = (bf16[192,2304]{1,0:T(8,128)(2,1)S(1)}, bf16[192,2304]{1,0:T(8,128)(2,1)S(1)}, u32[]{:S(2)}, u32[]{:S(2)}) collective-permute-start(bf16[192,2304]{1,0:T(8,128)(2,1)S(1)} %fusion.86), channel_id=1, source_target_pairs={{0,2},{1,3},{2,0},{3,1},{4,6},{5,7},{6,4},{7,5},{8,10},{9,11},{10,... | collective-permute-start | bytes 2654216 | tf_op jit(solution)/shard_map/ppermute | solution.py:120
  342.9 155.1 %collective-permute-start.20 = (bf16[288,2304]{1,0:T(8,128)(2,1)}, bf16[288,2304]{1,0:T(8,128)(2,1)S(1)}, u32[]{:S(2)}, u32[]{:S(2)}) collective-permute-start(bf16[288,2304]{1,0:T(8,128)(2,1)} %collective-permute-done.18), channel_id=1, source_target_pairs={{0,16},{4,20},{8,24},{12,28},{16,0},{20,4},{24,8},{28,12},{1,17},{... | collective-permute-start | bytes 3981320 | tf_op jit(solution)/shard_map/ppermute | solution.py:116
  808.2 124.0 %collective-permute-start.59 = (bf16[4,288,2304]{2,1,0:T(8,128)(2,1)}, bf16[4,288,2304]{2,1,0:T(8,128)(2,1)}, u32[]{:S(2)}, u32[]{:S(2)}) collective-permute-start(bf16[4,288,2304]{2,1,0:T(8,128)(2,1)} %dynamic-slice_bitcast_fusion), channel_id=1, source_target_pairs={{0,4},{4,0},{8,12},{12,8},{16,20},{20,16},{24,28},{28,24},{1,5},{5... | collective-permute-start | bytes 15925256 | tf_op jit(solution)/shard_map/ppermute | solution.py:116
  886.0 220.1 %collective-permute-start.64 = (bf16[288,1152]{1,0:T(8,128)(2,1)}, bf16[288,1152]{1,0:T(8,128)(2,1)}, u32[]{:S(2)}, u32[]{:S(2)}) collective-permute-start(bf16[288,1152]{1,0:T(8,128)(2,1)} %fusion.88), channel_id=1, source_target_pairs={{0,8},{4,12},{8,0},{12,4},{16,24},{20,28},{24,16},{28,20},{1,9},{5... | collective-permute-start | bytes 1990664 | tf_op jit(solution)/shard_map/ppermute | solution.py:116
  939.1 170.2 %collective-permute-start.60 = (bf16[2,288,2304]{2,1,0:T(8,128)(2,1)}, bf16[2,288,2304]{2,1,0:T(8,128)(2,1)}, u32[]{:S(2)}, u32[]{:S(2)}) collective-permute-start(bf16[2,288,2304]{2,1,0:T(8,128)(2,1)} %fusion.33), channel_id=1, source_target_pairs={{0,16},{4,20},{8,24},{12,28},{16,0},{20,4},{24,8},{28,12},{1,17},{... | collective-permute-start | bytes 7962632 | tf_op jit(solution)/shard_map/ppermute | solution.py:116
  999.3 92.1 %collective-permute-start.46 = (bf16[768,512]{0,1:T(8,128)(2,1)}, bf16[768,512]{0,1:T(8,128)(2,1)}, u32[]{:S(2)}, u32[]{:S(2)}) collective-permute-start(bf16[768,512]{0,1:T(8,128)(2,1)} %get-tuple-element.80), channel_id=1, source_target_pairs={{8,0},{12,4},{24,16},{28,20},{9,1},{13,5},{25,17},{29,21},{10,2},{... | collective-permute-start | bytes 2359304 | tf_op jit(solution)/shard_map/ppermute | solution.py:135
  1112.9 75.6 %collective-permute-start.61 = (bf16[288,2304]{1,0:T(8,128)(2,1)}, bf16[288,2304]{1,0:T(8,128)(2,1)S(1)}, u32[]{:S(2)}, u32[]{:S(2)}) collective-permute-start(bf16[288,2304]{1,0:T(8,128)(2,1)} %fusion.78), channel_id=1, source_target_pairs={{0,8},{4,12},{8,0},{12,4},{16,24},{20,28},{24,16},{28,20},{1,9},{5... | collective-permute-start | bytes 3981320 | tf_op jit(solution)/shard_map/ppermute | solution.py:116
  1151.1 72.5 %collective-permute-start.51 = (bf16[4,288,1024]{2,1,0:T(8,128)(2,1)S(1)}, bf16[4,288,1024]{2,1,0:T(8,128)(2,1)S(1)}, u32[]{:S(2)}, u32[]{:S(2)}) collective-permute-start(bf16[4,288,1024]{2,1,0:T(8,128)(2,1)S(1)} %dynamic-slice_bitcast_fusion.3), channel_id=1, source_target_pairs={{0,4},{4,0},{8,12},{12,8},{16,20},{20,16},{24,28},{28,24},{1,5},{5... | collective-permute-start | bytes 7077896 | tf_op jit(solution)/shard_map/ppermute | solution.py:116
  1186.5 120.0 %collective-permute-start.50 = (f32[2,192,2304]{2,1,0:T(8,128)}, f32[2,192,2304]{2,1,0:T(8,128)}, u32[]{:S(2)}, u32[]{:S(2)}) collective-permute-start(f32[2,192,2304]{2,1,0:T(8,128)} %pad_maximum_fusion.5), channel_id=1, source_target_pairs={{0,1},{1,0},{2,3},{3,2},{4,5},{5,4},{6,7},{7,6},{8,9},{9,8},{10,11... | collective-permute-start | bytes 10616840 | tf_op jit(solution)/shard_map/ppermute | solution.py:120
  1228.2 75.0 %collective-permute-start.52 = (bf16[288,1024]{1,0:T(8,128)(2,1)}, bf16[288,1024]{1,0:T(8,128)(2,1)S(1)}, u32[]{:S(2)}, u32[]{:S(2)}) collective-permute-start(bf16[288,1024]{1,0:T(8,128)(2,1)} %get-tuple-element.62), channel_id=1, source_target_pairs={{0,8},{4,12},{8,16},{12,20},{16,24},{20,28},{24,0},{28,4},{1,9},{5... | collective-permute-start | bytes 1769480 | tf_op jit(solution)/shard_map/ppermute | solution.py:116
  1229.6 73.6 %collective-permute-start.53 = (bf16[288,1024]{1,0:T(8,128)(2,1)}, bf16[288,1024]{1,0:T(8,128)(2,1)S(1)}, u32[]{:S(2)}, u32[]{:S(2)}) collective-permute-start(bf16[288,1024]{1,0:T(8,128)(2,1)} %get-tuple-element.64), channel_id=1, source_target_pairs={{0,16},{4,20},{8,24},{12,28},{16,0},{20,4},{24,8},{28,12},{1,17},{... | collective-permute-start | bytes 1769480 | tf_op jit(solution)/shard_map/ppermute | solution.py:116
  1229.6 73.6 %collective-permute-start.54 = (bf16[288,1024]{1,0:T(8,128)(2,1)}, bf16[288,1024]{1,0:T(8,128)(2,1)S(1)}, u32[]{:S(2)}, u32[]{:S(2)}) collective-permute-start(bf16[288,1024]{1,0:T(8,128)(2,1)} %get-tuple-element.63), channel_id=1, source_target_pairs={{0,24},{4,28},{8,0},{12,4},{16,8},{20,12},{24,16},{28,20},{1,25},{... | collective-permute-start | bytes 1769480 | tf_op jit(solution)/shard_map/ppermute | solution.py:116
  (137 other events, 3639.1 us)

commit v2 on v1

v2 whole, which is shorter than its diff:
```python
from functools import partial

import jax
import jax.numpy as jnp
from jax import lax
from jax.experimental import pallas as pl
from jax.experimental.pallas import tpu as pltpu
from jax.sharding import PartitionSpec as P

HEAD_DIM = 256
QUAD = 4
REACH = 2

softcap_limit = 50.0
norm_epsilon = 1e-06
rope_base = 10000.0
negative_fill = -1e30

QKV_COST = 10_000_000_000
ATTEND_COST = 20_000_000_000
ATTEND_BACK_COST = 40_000_000_000

f32 = jnp.float32
bf16 = jnp.bfloat16


def norm_parts(values):
    inverse = lax.rsqrt(jnp.mean(values * values, axis=-1, keepdims=True) + norm_epsilon)
    return values * inverse, inverse


def norm_back(gradient, gain_vec, unit_vals, inverse):
    scaled = gradient * gain_vec
    input_part = inverse * (
        scaled - unit_vals * jnp.mean(scaled * unit_vals, axis=-1, keepdims=True)
    )
    return (input_part, jnp.sum(gradient * unit_vals, axis=0))


def sequence_start(seq_lengths, tok_index):
    count = seq_lengths.shape[0]
    before = jnp.arange(count)[:, None] > jnp.arange(count)[None, :]
    starts = jnp.sum(jnp.where(before, seq_lengths[None, :], 0), axis=1)
    passed = tok_index[:, None] >= starts[None, :]
    return jnp.max(jnp.where(passed, starts[None, :], 0), axis=1)


def rope_tables(position):
    half_dim = HEAD_DIM // 2
    freqs = rope_base ** (-2.0 * jnp.arange(half_dim).astype(f32) / HEAD_DIM)
    theta = position.astype(f32)[:, None] * freqs[None, :]
    return (jnp.cos(theta), jnp.sin(theta))


def contract_rows(left, right):
    return lax.dot_general(
        left, right, (((0,), (0,)), ((), ())), preferred_element_type=f32
    )


def contract_cols(left, right):
    return lax.dot_general(
        left, right, (((1,), (1,)), ((), ())), preferred_element_type=f32
    )


def rotate_in(values, cosine, sine_tab):
    half_dim = HEAD_DIM // 2
    front, back = values[:, :half_dim], values[:, half_dim:]
    return jnp.concatenate(
        [front * cosine - back * sine_tab, back * cosine + front * sine_tab], axis=1
    )


def qkv_kernel(heads, kv_heads, x_ref, gain_ref, w_ref, cos_ref, sin_ref, hidden_ref, q_ref, kv_ref):
    which = pl.program_id(0)

    @pl.when(which == 0)
    def _():
        values = x_ref[...].astype(f32)
        inverse = lax.rsqrt(jnp.mean(values * values, axis=1, keepdims=True) + norm_epsilon)
        hidden_ref[...] = (values * inverse * gain_ref[...]).astype(bf16)

    product = jnp.dot(
        hidden_ref[...], w_ref[...], preferred_element_type=f32
    )

    @pl.when(which < heads)
    def _():
        q_ref[...] = rotate_in(product, cos_ref[...], sin_ref[...]).astype(bf16)

    @pl.when((which >= heads) & (which < heads + kv_heads))
    def _():
        kv_ref[...] = rotate_in(product, cos_ref[...], sin_ref[...]).astype(bf16)

    @pl.when(which >= heads + kv_heads)
    def _():
        kv_ref[...] = product.astype(bf16)


def qkv_call(inputs, gain, mat, cosine, sine_tab, heads, kv_heads):
    rows, width = inputs.shape
    whole = lambda a: pl.BlockSpec(a.shape, lambda j: (0, 0))
    return pl.pallas_call(
        partial(qkv_kernel, heads, kv_heads),
        grid=(heads + 2 * kv_heads,),
        out_shape=(
            jax.ShapeDtypeStruct((rows, width), bf16),
            jax.ShapeDtypeStruct((rows, heads * HEAD_DIM), bf16),
            jax.ShapeDtypeStruct((rows, 2 * kv_heads * HEAD_DIM), bf16),
        ),
        in_specs=[
            whole(inputs),
            whole(gain),
            pl.BlockSpec((width, HEAD_DIM), lambda j: (0, j)),
            whole(cosine),
            whole(sine_tab),
        ],
        out_specs=(
            pl.BlockSpec((rows, width), lambda j: (0, 0)),
            pl.BlockSpec((rows, HEAD_DIM), lambda j: (0, jnp.minimum(j, heads - 1))),
            pl.BlockSpec((rows, HEAD_DIM), lambda j: (0, jnp.maximum(j - heads, 0))),
        ),
        compiler_params=pltpu.CompilerParams(vmem_limit_bytes=40 << 20),
        cost_estimate=pl.CostEstimate(flops=QKV_COST, bytes_accessed=0, transcendentals=0),
        name="qkv",
    )(inputs, gain, mat, cosine, sine_tab)


def scores_of(q, k_refs, low, first_row, kv_heads, head):
    rows, block = q.shape[0], k_refs[0].shape[0]
    last = len(k_refs) - 1
    query_at = last * block + first_row + lax.broadcasted_iota(jnp.int32, (rows, 1), 0)
    found = []
    for i, ref in enumerate(k_refs):
        raw = lax.dot_general(
            q, ref[...], (((1,), (1,)), ((), ())), preferred_element_type=f32
        )
        ratio = jnp.tanh(raw * (HEAD_DIM ** (-0.5) / softcap_limit))
        key_at = i * block + lax.broadcasted_iota(jnp.int32, (1, block), 1)
        found.append((ratio, (key_at >= low) & (key_at <= query_at)))
    return found


def attend_kernel(tile, q_ref, k2_ref, k1_ref, k0_ref, v2_ref, v1_ref, v0_ref, low_ref, o_ref, lse_ref):
    step = pl.program_id(1)
    k_refs, v_refs = (k2_ref, k1_ref, k0_ref), (v2_ref, v1_ref, v0_ref)
    found = scores_of(q_ref[...], k_refs, low_ref[...], step * tile, 1, 0)
    masked = [jnp.where(ok, softcap_limit * ratio, negative_fill) for ratio, ok in found]
    row_max = jnp.max(masked[0], axis=1, keepdims=True)
    for part in masked[1:]:
        row_max = jnp.maximum(row_max, jnp.max(part, axis=1, keepdims=True))
    exps = [jnp.exp(part - row_max) for part in masked]
    total = sum(jnp.sum(e, axis=1, keepdims=True) for e in exps)
    scale = 1.0 / total
    mixed = sum(
        jnp.dot((e * scale).astype(bf16), v[...], preferred_element_type=f32)
        for e, v in zip(exps, v_refs)
    )
    o_ref[...] = mixed.astype(bf16)
    lse_ref[0] = row_max + jnp.log(total)


def attend_call(query, window, low, heads, kv_heads):
    rows = query.shape[0]
    tile = rows // 3
    group = heads // kv_heads
    key = pl.BlockSpec((rows, HEAD_DIM), lambda h, i: (0, h // group))
    value = pl.BlockSpec((rows, HEAD_DIM), lambda h, i: (0, kv_heads + h // group))
    mine = pl.BlockSpec((tile, HEAD_DIM), lambda h, i: (i, h))
    return pl.pallas_call(
        partial(attend_kernel, tile),
        grid=(heads, rows // tile),
        out_shape=(
            jax.ShapeDtypeStruct(query.shape, bf16),
            jax.ShapeDtypeStruct((heads, rows, 1), f32),
        ),
        in_specs=[mine] + [key] * 3 + [value] * 3 + [pl.BlockSpec((tile, 1), lambda h, i: (i, 0))],
        out_specs=(mine, pl.BlockSpec((1, tile, 1), lambda h, i: (h, i, 0))),
        compiler_params=pltpu.CompilerParams(vmem_limit_bytes=48 << 20),
        cost_estimate=pl.CostEstimate(flops=ATTEND_COST, bytes_accessed=0, transcendentals=0),
        name="attend",
    )(query, *window, *window, low)


def attend_back_kernel(
    tile, q_ref, do_ref, k2_ref, k1_ref, k0_ref, v2_ref, v1_ref, v0_ref, low_ref, lse_ref, cos_ref, sin_ref,
    dq_ref, d2_ref, d1_ref, d0_ref, acc_ref,
):
    head, step = pl.program_id(0), pl.program_id(1)
    k_refs, v_refs = (k2_ref, k1_ref, k0_ref), (v2_ref, v1_ref, v0_ref)

    @pl.when((head == 0) & (step == 0))
    def _():
        acc_ref[...] = jnp.zeros_like(acc_ref)

    q, d_out = q_ref[...], do_ref[...]
    found = scores_of(q, k_refs, low_ref[...], step * tile, 1, 0)
    lse = lse_ref[0]
    probs = [jnp.where(ok, jnp.exp(softcap_limit * ratio - lse), 0.0) for ratio, ok in found]
    d_probs = [
        lax.dot_general(d_out, v[...], (((1,), (1,)), ((), ())), preferred_element_type=f32)
        for v in v_refs
    ]
    delta = sum(jnp.sum(p * d, axis=1, keepdims=True) for p, d in zip(probs, d_probs))
    d_query = 0.0
    for i, (p, d) in enumerate(zip(probs, d_probs)):
        ratio = found[i][0]
        d_raw = (p * (d - delta) * (1.0 - ratio * ratio) * (HEAD_DIM ** (-0.5))).astype(bf16)
        d_query += jnp.dot(d_raw, k_refs[i][...], preferred_element_type=f32)
        acc_ref[i, :, :HEAD_DIM] += contract_rows(d_raw, q)
        acc_ref[i, :, HEAD_DIM:] += contract_rows(p.astype(bf16), d_out)
    dq_ref[...] = rotate_in(d_query, cos_ref[...], -sin_ref[...]).astype(bf16)

    @pl.when((head == pl.num_programs(0) - 1) & (step == pl.num_programs(1) - 1))
    def _():
        d2_ref[...] = acc_ref[0].astype(bf16)
        d1_ref[...] = acc_ref[1].astype(bf16)
        d0_ref[...] = acc_ref[2]


def attend_back_call(query, d_out, window, low, lse, cosine, sine_tab, heads):
    rows = query.shape[0]
    tile = rows // 3
    key = pl.BlockSpec((rows, HEAD_DIM), lambda h, i: (0, 0))
    value = pl.BlockSpec((rows, HEAD_DIM), lambda h, i: (0, 1))
    mine = pl.BlockSpec((tile, HEAD_DIM), lambda h, i: (i, h))
    tab = pl.BlockSpec((tile, HEAD_DIM // 2), lambda h, i: (i, 0))
    back = pl.BlockSpec((rows, 2 * HEAD_DIM), lambda h, i: (0, 0))
    return pl.pallas_call(
        partial(attend_back_kernel, tile),
        grid=(heads, rows // tile),
        out_shape=(
            jax.ShapeDtypeStruct(query.shape, bf16),
            jax.ShapeDtypeStruct((rows, 2 * HEAD_DIM), bf16),
            jax.ShapeDtypeStruct((rows, 2 * HEAD_DIM), bf16),
            jax.ShapeDtypeStruct((rows, 2 * HEAD_DIM), f32),
        ),
        in_specs=[mine, mine]
        + [key] * 3
        + [value] * 3
        + [
            pl.BlockSpec((tile, 1), lambda h, i: (i, 0)),
            pl.BlockSpec((1, tile, 1), lambda h, i: (h, i, 0)),
            tab,
            tab,
        ],
        out_specs=(mine, back, back, back),
        scratch_shapes=[pltpu.VMEM((3, rows, 2 * HEAD_DIM), f32)],
        compiler_params=pltpu.CompilerParams(vmem_limit_bytes=56 << 20),
        cost_estimate=pl.CostEstimate(flops=ATTEND_BACK_COST, bytes_accessed=0, transcendentals=0),
        name="attend_back",
    )(query, d_out, *window, *window, low, lse, cosine, sine_tab)


def pick(array, index, axis=0):
    return lax.dynamic_index_in_dim(array, index, axis, keepdims=False)


class Order:
    def __init__(self, token):
        self.token = token

    def __call__(self, *values):
        values, self.token = lax.optimization_barrier((values, self.token))
        return values[0] if len(values) == 1 else values


def put(buffer, block, index):
    return lax.dynamic_update_index_in_dim(buffer, block, index, 0)


def local(
    inputs,
    seq_lengths,
    gain_attn_in,
    gain_attn_out,
    gain_ffn_in,
    gain_ffn_out,
    w_query,
    w_key,
    w_value,
    w_out,
    w_gate,
    w_up,
    w_down,
    out_grad,
):
    n = lax.axis_size("tok")
    m = n // 4
    width = inputs.shape[1]
    rows = inputs.shape[0]
    part = rows // 4
    tok = lax.axis_index("tok")
    tpi = lax.axis_index("tp")
    z, y = tok // m, tok % m
    zlo, zhi = z % 2, z // 2
    x, core = tpi // 2, tpi % 2
    wrows = w_query.shape[0]
    head_cols = w_query.shape[1]
    kv_cols = w_key.shape[1]
    heads = head_cols // HEAD_DIM
    kv_heads = kv_cols // HEAD_DIM
    units = w_gate.shape[1]
    half = units // 2

    def over_tok(fn):
        pairs = [(t, fn(t)) for t in range(n)]
        return lambda a: lax.ppermute(a, "tok", pairs)

    def over_tp(fn):
        pairs = [(t, fn(t)) for t in range(4)]
        return lambda a: lax.ppermute(a, "tp", pairs)

    def z_shift(a, k):
        return over_tok(lambda t: ((t // m + k) % 4) * m + t % m)(a)

    def y_shift(a, k):
        return over_tok(lambda t: (t // m) * m + (t % m + k) % m)(a)

    to_zlo = over_tok(lambda t: ((t // m) ^ 1) * m + t % m)
    to_zhi = over_tok(lambda t: ((t // m) ^ 2) * m + t % m)
    to_core = over_tp(lambda t: t ^ 1)
    to_x = over_tp(lambda t: t ^ 2)

    def within_quad(a, by):
        pairs = [(t, t + by) for t in range(n) if 0 <= t + by < n and t // QUAD == (t + by) // QUAD]
        return lax.ppermute(a, "tok", pairs)

    def place_of(dz, dy):
        return ((z ^ dz) * m) + (y - dy) % m

    step = Order(seq_lengths)

    def z_line(a, way, at):
        pairs = [
            (zs * m + ys, (zs + way) * m + ys)
            for zs in (range(at - 1, 3) if way > 0 else range(1, 5 - at))
            for ys in range(m)
        ]
        return lax.ppermute(a, "tok", pairs)

    def y_others(a):
        return [y_shift(a, j) for j in range(1, m)]

    def halves(a, index):
        return lax.dynamic_slice_in_dim(a, index * half, half, 1)

    attn_own = jnp.concatenate([w_query, w_key, w_value, w_out], axis=1)
    gains = jnp.concatenate([gain_attn_in, gain_attn_out, gain_ffn_in, gain_ffn_out])
    attn_cols = attn_own.shape[1]
    gains = jnp.pad(gains, (0, attn_cols - gains.shape[0])).reshape(1, attn_cols)
    attn_own = jnp.concatenate([attn_own, jnp.pad(gains, ((0, 7), (0, 0)))], axis=0)
    up1, down1 = z_line(attn_own, 1, 1), z_line(attn_own, -1, 1)
    attn_y = {0: y_others(attn_own)}
    gu_keep = jnp.concatenate([halves(w_gate, zlo), halves(w_up, zlo)], axis=1)
    gu_send = jnp.concatenate([halves(w_gate, 1 - zlo), halves(w_up, 1 - zlo)], axis=1)
    d_keep, d_send = halves(w_down, zlo), halves(w_down, 1 - zlo)
    gu_y = {0: y_others(gu_keep)}
    up1, down1 = step(up1, down1)
    up2, down2 = z_line(up1, 1, 2), z_line(down1, -1, 2)
    up2, down2 = step(up2, down2)
    attn_z = {0: attn_own, 2: jnp.where(z >= 2, up2, down2)}
    up3, down3 = z_line(up2, 1, 3), z_line(down2, -1, 3)
    attn_y[2] = y_others(attn_z[2])
    gu_send, gu_first, d_send = step(gu_send, gu_keep, d_send)
    gu_z = {0: gu_keep, 1: to_zlo(gu_send)}
    gu_z[2] = to_zhi(gu_first)
    d_z = {0: d_keep, 1: to_zlo(d_send)}
    up3, down3 = step(up3, down3)
    attn_z[1] = jnp.where(z >= 1, up1, down3)
    attn_z[3] = jnp.where(z >= 3, up3, down1)
    attn_y[1], attn_y[3] = y_others(attn_z[1]), y_others(attn_z[3])
    gu_z[1] = step(gu_z[1])
    gu_y[1] = y_others(gu_z[1])
    gu_z[3] = to_zhi(gu_z[1])
    attn_y = step(attn_y)

    attn_buf = jnp.zeros((n,) + attn_own.shape, bf16)
    for k in range(4):
        for j, piece in enumerate([attn_z[k]] + attn_y[k]):
            attn_buf = put(attn_buf, piece, ((z - k) % 4) * m + (y - j) % m)
    gains_all = attn_buf[:, wrows, : 4 * wrows].reshape(n, 4, wrows)
    gains_all = gains_all.transpose(1, 0, 2).reshape(4, 1, width).astype(f32)
    gain_one, gain_two, gain_three, gain_four = (gains_all[i] for i in range(4))

    def ffn_matrix(by_z, by_y):
        buffer = jnp.zeros((n,) + by_z[0].shape, bf16)
        for k in range(4):
            for j, piece in enumerate([by_z[k]] + by_y[k]):
                buffer = put(buffer, piece, (z ^ k) * m + (y - j) % m)
        return buffer.reshape(width, -1)

    def own_slice(a):
        return lax.dynamic_slice_in_dim(a, tpi * part, part, 0)

    def gather_tp(a):
        buffer = jnp.zeros((4,) + a.shape, a.dtype)
        low = a.astype(bf16)
        other = to_x(low)
        pair = to_core(jnp.stack([low, other]))
        for k, block in enumerate((a, pair[0], other, pair[1])):
            buffer = put(buffer, block.astype(a.dtype), tpi ^ k)
        return buffer.reshape((-1,) + a.shape[1:])

    def gather_pair(a):
        a_z = to_zlo(a)
        a_x = to_x(a)
        mid = width // 2
        a_xz = jnp.concatenate([to_x(a_z[:, :mid]), to_zlo(a_x[:, mid:])], axis=1)
        side = jnp.concatenate([a, a_z, a_x, a_xz])
        return jnp.concatenate([side, to_core(side)])

    def reduce_pair(compute):
        far = compute(1).astype(bf16)
        near = compute(0) + to_core(far).astype(f32)
        near = near.reshape(2, 2, part, width)
        mid = width // 2
        left, right = near[..., :mid], near[..., mid:]
        left = left[0] + to_x(left[1].astype(bf16)).astype(f32)
        right = right[:, 0] + to_zlo(right[:, 1].astype(bf16)).astype(f32)
        left = left[0] + to_zlo(left[1].astype(bf16)).astype(f32)
        right = right[0] + to_x(right[1].astype(bf16)).astype(f32)
        return jnp.concatenate([left, right], axis=1)

    def reduce_tp(compute):
        far = compute(1 - core).astype(bf16)
        near = compute(core) + to_core(far).astype(f32)
        near = near.reshape(2, part, width)
        return pick(near, x) + to_x(pick(near, 1 - x).astype(bf16)).astype(f32)

    def core_rows(a, c):
        return pick(a.reshape(2, 2, part, a.shape[1]), c, 1).reshape(2 * part, a.shape[1])

    own_index = tok * rows + jnp.arange(rows, dtype=jnp.int32)
    seq_start = sequence_start(seq_lengths, own_index)
    cosine, sine_tab = rope_tables(own_index - seq_start)
    low = (seq_start - (tok - REACH) * rows)[:, None]

    qkv_cols = head_cols + 2 * kv_cols
    qkv_mat = attn_buf[:, :wrows, :qkv_cols].reshape(width, qkv_cols)
    out_mat = attn_buf[:, :wrows, qkv_cols:].reshape(width, head_cols)
    hidden_one, query, key_value = qkv_call(
        inputs, gain_one, qkv_mat, cosine, sine_tab, heads, kv_heads
    )
    key_value = step(key_value)
    window = [within_quad(key_value, by) for by in range(REACH, 0, -1)] + [key_value]
    gu_z[2], d_z[1], d_first = step(gu_z[2], d_z[1], d_keep)
    gu_y[2] = y_others(gu_z[2])
    d_y = {0: y_others(d_first), 1: y_others(d_z[1])}
    d_z[2], d_z[3] = to_zhi(d_first), to_zhi(d_z[1])
    window = step(window)
    attended, lse = attend_call(query, window, low, heads, kv_heads)
    attended = step(attended)
    attn = reduce_tp(lambda c: contract_cols(core_rows(attended, c), out_mat))
    gu_z[3] = step(gu_z[3])
    gu_y[3] = y_others(gu_z[3])
    d_z[2] = step(d_z[2])
    d_y[2] = y_others(d_z[2])
    attn, d_z[3] = step(attn, d_z[3])
    d_y[3] = y_others(d_z[3])

    resid = own_slice(inputs).astype(f32)
    unit_two, inv_two = norm_parts(attn)
    resid_mid = resid + unit_two * gain_two
    unit_three, inv_three = norm_parts(resid_mid)
    hidden_two = gather_pair((unit_three * gain_three).astype(bf16))
    gu_mat, down_mat = ffn_matrix(gu_z, gu_y), ffn_matrix(d_z, d_y)
    gate_up = jnp.dot(hidden_two, gu_mat, preferred_element_type=f32)
    gate_vals, up_vals = gate_up[:, :half], gate_up[:, half:]
    activated, gelu_pull = jax.vjp(partial(jax.nn.gelu, approximate=True), gate_vals)
    inner = (activated * up_vals).astype(bf16)
    ffn = reduce_pair(lambda k: contract_cols(jnp.split(inner, 2)[k], down_mat))
    unit_four, inv_four = norm_parts(ffn)
    layer_out = gather_tp((resid_mid + unit_four * gain_four).astype(bf16))

    grad_out = own_slice(out_grad).astype(f32)
    d_ffn, grad_four = norm_back(grad_out, gain_four, unit_four, inv_four)
    d_ffn_all = gather_pair(d_ffn.astype(bf16))
    d_inner = jnp.dot(d_ffn_all, down_mat, preferred_element_type=f32)

    def y_send(grad):
        blocks = grad.astype(bf16).reshape(4, m, wrows, -1)
        return [pick(blocks, y, 1)] + [y_shift(pick(blocks, (y + j) % m, 1), j) for j in range(1, m)]

    def add_up(terms):
        return sum(t.astype(f32) for t in terms)

    def zhi_send(terms):
        total = add_up(terms).reshape(2, 2, wrows, -1)
        return [pick(total, zhi), to_zhi(pick(total, 1 - zhi).astype(bf16))]

    def zlo_send(terms):
        total = add_up(terms)
        return pick(total, zlo), to_zlo(pick(total, 1 - zlo).astype(bf16)).astype(f32)

    def z_send(terms):
        total = add_up(terms)
        return [pick(total, z)] + [
            z_shift(pick(total, (z + k) % 4).astype(bf16), k) for k in range(1, 4)
        ]

    def sides(own, other):
        return jnp.where(
            zlo == 0,
            jnp.concatenate([own, other], axis=1),
            jnp.concatenate([other, own], axis=1),
        )

    down_s = y_send(contract_rows(d_ffn_all, inner))
    grad_upvals = (d_inner * activated).astype(bf16)
    grad_gatevals = gelu_pull(d_inner * up_vals)[0].astype(bf16)
    grad_gu = jnp.concatenate([grad_gatevals, grad_upvals], axis=1)
    far, near = (contract_cols(jnp.split(grad_gu, 2)[k], gu_mat) for k in (1, 0))
    near = near + to_core(far.astype(bf16)).astype(f32)
    near = near.reshape(2, 2, part, width)
    mid = width // 2
    left, right = near[..., :mid], near[..., mid:]
    left_in, right_in = to_x(left[1].astype(bf16)), to_zlo(right[:, 1].astype(bf16))
    gate_s = y_send(contract_rows(hidden_two, grad_gatevals))
    up_s = y_send(contract_rows(hidden_two, grad_upvals))
    left_in, right_in = step(left_in, right_in)
    left = left[0] + left_in.astype(f32)
    right = right[:, 0] + right_in.astype(f32)
    left_in, right_in = to_zlo(left[1].astype(bf16)), to_x(right[1].astype(bf16))
    down_s = step(down_s)
    left_in, right_in = step(left_in, right_in)
    d_hidden_two = jnp.concatenate(
        [left[0] + left_in.astype(f32), right[0] + right_in.astype(f32)], axis=1
    )
    down_s = zhi_send(down_s)

    mid_add, grad_three = norm_back(d_hidden_two, gain_three, unit_three, inv_three)
    d_mid = grad_out + mid_add

    d_attn, grad_two = norm_back(d_mid, gain_two, unit_two, inv_two)
    d_attn_low = gather_tp(d_attn.astype(bf16))

    d_attn_low = step(d_attn_low)
    wout_s = contract_rows(d_attn_low, attended)
    d_attended = jnp.dot(d_attn_low, out_mat, preferred_element_type=f32).astype(bf16)
    gate_s, down_s = step(gate_s, down_s)
    gate_s = zhi_send(gate_s)
    d_query, *d_window, d_kv = attend_back_call(
        query, d_attended, window, low, lse, cosine, sine_tab, heads
    )
    d_window = [within_quad(d_window[REACH - by], -by) for by in range(1, REACH + 1)]
    q_grad = contract_rows(hidden_one, d_query)
    up_s, wout_s = step(up_s, wout_s)
    up_s, wout_s = zhi_send(up_s), y_send(wout_s)
    out_down = sides(*zlo_send(down_s))
    d_window = step(d_window)
    q_s = y_send(q_grad)
    d_kv = d_kv + add_up(d_window)
    d_key = rotate_in(d_kv[:, :kv_cols], cosine, -sine_tab)
    d_key_value = jnp.concatenate([d_key.astype(bf16), d_kv[:, kv_cols:].astype(bf16)], axis=1)
    d_qkv = jnp.concatenate([d_query, d_key_value], axis=1)
    kv_s = y_send(contract_rows(hidden_one, d_key_value))
    d_hidden_one = reduce_tp(lambda c: contract_cols(core_rows(d_qkv, c), qkv_mat))
    unit_one, inv_one = norm_parts(resid)
    input_add, grad_one = norm_back(d_hidden_one, gain_one, unit_one, inv_one)
    gate_s = step(gate_s)
    out_gate = sides(*zlo_send(gate_s))
    wout_s = z_send(step(wout_s))
    up_s = step(up_s)
    out_up = sides(*zlo_send(up_s))
    q_s = z_send(step(q_s))
    kv_s = z_send(step(kv_s))
    out_wout, out_q, out_kv = add_up(wout_s), add_up(q_s), add_up(kv_s)
    input_grad = gather_tp(d_mid + input_add)

    gain_grads = jnp.stack([grad_one, grad_two, grad_three, grad_four])
    gain_grads = gain_grads + to_core(gain_grads)
    gain_grads = gain_grads + to_x(gain_grads)
    bit = 1
    while bit < n:
        gain_grads = gain_grads + over_tok(lambda t: t ^ bit)(gain_grads)
        bit *= 2
    gain_grads = lax.dynamic_slice_in_dim(gain_grads, tok * wrows, wrows, 1)
    return (
        layer_out,
        input_grad,
        gain_grads[0],
        gain_grads[1],
        gain_grads[2],
        gain_grads[3],
        out_q,
        out_kv[:, :kv_cols],
        out_kv[:, kv_cols:],
        out_wout,
        out_gate,
        out_up,
        out_down,
    )


def solution(mesh):
    weight = P("tok", "tp")
    in_specs = (P("tok", None), P()) + (P("tok"),) * 4 + (weight,) * 7 + (P("tok", None),)
    out_specs = (P("tok", None),) * 2 + (P("tok"),) * 4 + (weight,) * 7
    return jax.shard_map(local, mesh=mesh, in_specs=in_specs, out_specs=out_specs, check_vma=False)
```

time: 1320 us -> 1030 us (0.78)
  blocking collectives: 158 us -> 0 us
  matrix products: 235 us -> 142 us
  waiting for transfers between devices: 589 us -> 513 us
  Pallas kernels: 0 us -> 44.1 us
  other arithmetic: 87.8 us -> 68 us
  starting transfers between devices: 113 us -> 128 us
    all_gather x1 -> x0, blocking collectives: 89.9 us -> none  [local(): gains_all = lax.all_gather(gains, 'tok', axis=1, tiled=True).astype(f32)]
    dot_general x7 -> x0, matrix products: 86.8 us -> none  [the longest x1 29.3 us: local(): jnp.einsum('jqk,qjd->kd', d_raw, query_rot, preferred_element_type=f32)]
    psum x1 -> x0, blocking collectives: 67.9 us -> none  [local(): lax.psum(jnp.stack([grad_one, grad_two, grad_three, grad_four]), ('tok',...]
    ppermute x39 -> x50, waiting for transfers between devices: 382 us -> 314 us  [over_tok(): return lambda a: lax.ppermute(a, 'tok', pairs)]
    ppermute x22 -> x24, waiting for transfers between devices: 148 us -> 84.6 us  [over_tp(): return lambda a: lax.ppermute(a, 'tp', pairs)]
    ppermute x0 -> x6, waiting for transfers between devices: none -> 53.8 us  [z_line(): return lax.ppermute(a, 'tok', pairs)]
    pallas_call x0 -> x3, Pallas kernels: none -> 44.1 us  [the longest x1 22.1 us: attend_back_call(): pl.pallas_call(partial(attend_back_kernel, tile), grid=(heads, rows // ti...]
    dynamic_update_slice x33 -> x29, local copies, waits for them, and re-layouts: 43 us -> 36.3 us  [put(): return lax.dynamic_update_index_in_dim(buffer, block, index, 0)]
  transfers between devices with their start and end apart: 65 -> 84, of which waited for: 27 -> 43; matrix products, arithmetic and copies ran while one was open for 28% -> 21% of each run, Pallas kernels for 0% -> 4%
where the time goes in v2:
time: 1030 us; the launch traced here: 1020 us
  waiting for transfers between devices  513 us (50%)
  matrix products  142 us (14%)
  starting transfers between devices  128 us (12%)
  local copies, waits for them, and re-layouts  126 us (12%)
  other arithmetic  68 us (7%)
  Pallas kernels  44.1 us (4%)
    ppermute x50, waiting for transfers between devices, over_tok(): return lambda a: lax.ppermute(a, 'tok', pairs)  314 us
    ppermute x50, starting transfers between devices, over_tok(): return lambda a: lax.ppermute(a, 'tok', pairs)  85.3 us
    ppermute x24, waiting for transfers between devices, over_tp(): return lambda a: lax.ppermute(a, 'tp', pairs)  84.6 us
    ppermute x4, waiting for transfers between devices, within_quad(): return lax.ppermute(a, 'tok', pairs)  60.1 us
    ppermute x6, waiting for transfers between devices, z_line(): return lax.ppermute(a, 'tok', pairs)  53.8 us
    dot_general x8, matrix products, contract_cols(): lax.dot_general(left, right, (((1,), (1,)), ((), ())), preferred_element_...  53 us
    dot_general x6, matrix products, contract_rows(): lax.dot_general(left, right, (((0,), (0,)), ((), ())), preferred_element_...  48.2 us
    unnamed x154, local copies, waits for them, and re-layouts  36.4 us
  transfers between devices with their start and end apart: 84, of which 43 were waited for; matrix products, arithmetic and copies ran while one was open for 21% of the time, Pallas kernels for 4%

profile of v2, /device:TPU:0, one launch (start us, length us, event | category | flops | bytes accessed | tf_op | source)
XLA Modules:
  0.0 1022.9 jit_solution(13556107373033347873)
XLA Ops:
  16.3 14.0 %collective-permute-done.1 = bf16[296,1536]{1,0:T(8,128)(2,1)} collective-permute-done((bf16[296,1536]{1,0:T(8,128)(2,1)}, bf16[296,1536]{1,0:T(8,128)(2,1)}, u32[]{:S(2)}, u32[]{:S(2)}) %collective-permute-start.1) | collective-permute-done | bytes 909344 | tf_op jit(solution)/shard_map/ppermute | solution.py:341
  43.2 18.2 %collective-permute-done.4 = bf16[296,1536]{1,0:T(8,128)(2,1)} collective-permute-done((bf16[296,1536]{1,0:T(8,128)(2,1)}, bf16[296,1536]{1,0:T(8,128)(2,1)}, u32[]{:S(2)}, u32[]{:S(2)}) %collective-permute-start.4) | collective-permute-done | bytes 909344 | tf_op jit(solution)/shard_map/ppermute | solution.py:341
  67.4 16.6 %collective-permute-done.6 = bf16[296,1536]{1,0:T(8,128)(2,1)S(1)} collective-permute-done((bf16[296,1536]{1,0:T(8,128)(2,1)}, bf16[296,1536]{1,0:T(8,128)(2,1)S(1)}, u32[]{:S(2)}, u32[]{:S(2)}) %collective-permute-start.6) | collective-permute-done | bytes 909344 | tf_op jit(solution)/shard_map/ppermute | solution.py:341
  197.4 14.4 %attend.1 = (bf16[768,512]{1,0:T(8,128)(2,1)S(1)}, f32[2,768,1]{2,1,0:T(8,128)S(1)}) custom-call(bf16[768,512]{1,0:T(8,128)(2,1)S(1)} %copy-done.11, bf16[768,512]{1,0:T(8,128)(2,1)} %collective-permute-done.11.k2_ref.v2_ref, bf16[768,512]{1,0:T(8,128)(2,1)} %collective-permute-done.12.k1_ref.v1_ref, bf16[768,512]{1,0:T(8,128)(2,1)} %get-tuple-element.108.k0_ref.v0_ref, ...), custom_call_target="tpu_custom_call" | custom-call | flops 20000000000 | tf_op jit(solution)/shard_map/attend/pallas_call | solution.py:171
  215.6 56.4 %collective-permute-done.30 = bf16[288,1152]{1,0:T(8,128)(2,1)} collective-permute-done((bf16[288,1152]{1,0:T(8,128)(2,1)S(1)}, bf16[288,1152]{1,0:T(8,128)(2,1)}, u32[]{:S(2)}, u32[]{:S(2)}) %collective-permute-start.30) | collective-permute-done | bytes 663584 | tf_op jit(solution)/shard_map/ppermute | solution.py:309
  295.8 14.3 %collective-permute-done.16 = bf16[192,2304]{1,0:T(8,128)(2,1)} collective-permute-done((bf16[192,2304]{1,0:T(8,128)(2,1)}, bf16[192,2304]{1,0:T(8,128)(2,1)}, u32[]{:S(2)}, u32[]{:S(2)}) %collective-permute-start.16) | collective-permute-done | bytes 884768 | tf_op jit(solution)/shard_map/ppermute | solution.py:313
  383.4 18.8 %fusion.81 = f32[1536,2304]{1,0:T(8,128)S(1)} fusion(bf16[1536,2304]{1,0:T(8,128)(2,1)} %copy-done.51, bf16[2304,2304]{1,0:T(8,128)(2,1)S(1)} %bitcast.284), kind=kOutput, calls=%fused_computation.288 | convolution fusion | flops 16307453952 | bytes 31850496 | tf_op jit(solution)/shard_map/dot_general | solution.py:469
  436.6 18.2 %collective-permute-done.34 = bf16[2,192,1152]{2,1,0:T(8,128)(2,1)S(1)} collective-permute-done((bf16[2,192,1152]{2,1,0:T(8,128)(2,1)S(1)}, bf16[2,192,1152]{2,1,0:T(8,128)(2,1)S(1)}, u32[]{:S(2)}, u32[]{:S(2)}) %collective-permute-start.34) | collective-permute-done | bytes 884768 | tf_op jit(solution)/shard_map/ppermute | solution.py:313
  477.5 15.3 %collective-permute-done.40 = bf16[192,2304]{1,0:T(8,128)(2,1)S(1)} collective-permute-done((bf16[192,2304]{1,0:T(8,128)(2,1)S(1)}, bf16[192,2304]{1,0:T(8,128)(2,1)S(1)}, u32[]{:S(2)}, u32[]{:S(2)}) %collective-permute-start.40) | collective-permute-done | bytes 884768 | tf_op jit(solution)/shard_map/ppermute | solution.py:309
  500.2 15.4 %collective-permute-done.38 = bf16[192,2304]{1,0:T(8,128)(2,1)} collective-permute-done((bf16[192,2304]{1,0:T(8,128)(2,1)}, bf16[192,2304]{1,0:T(8,128)(2,1)}, u32[]{:S(2)}, u32[]{:S(2)}) %collective-permute-start.38) | collective-permute-done | bytes 884768 | tf_op jit(solution)/shard_map/ppermute | solution.py:313
  539.4 14.2 %convolution_convert_fusion = bf16[2304,1152]{1,0:T(8,128)(2,1)} fusion(bf16[1536,2304]{1,0:T(8,128)(2,1)} %constant_dynamic-update-slice_fusion.9, bf16[1536,1152]{1,0:T(8,128)(2,1)S(1)} %copy-done.35), kind=kOutput, calls=%fused_computation | convolution fusion | flops 8156381184 | bytes 15925248 | tf_op jit(solution)/shard_map/dot_general | solution.py:56
  553.6 18.9 %fusion.6 = (bf16[1536,1152]{1,0:T(8,128)(2,1)}, bf16[1536,1152]{1,0:T(8,128)(2,1)}) fusion(f32[1536,2304]{1,0:T(8,128)S(1)} %bitcast.279, bf16[1536,2304]{1,0:T(8,128)(2,1)} %constant_dynamic-update-slice_fusion.9, bf16[2304,1152]{1,0:T(8,128)(2,1)} %bitcast.34), kind=kOutput, calls=%fused_computation.11 | convolution fusion | flops 8196194304 | bytes 33619968 | tf_op jit(solution)/shard_map/dot_general | solution.py:480
  592.4 14.4 %convolution_convert_fusion.3 = bf16[768,2304]{1,0:T(8,128)(2,1)} fusion(bf16[2304,2304]{1,0:T(8,128)(2,1)} %bitcast.282, bf16[1536,1152]{1,0:T(8,128)(2,1)} %get-tuple-element.179, bf16[1536,1152]{1,0:T(8,128)(2,1)} %get-tuple-element.178), kind=kOutput, calls=%fused_computation.24 | convolution fusion | flops 8162574336 | bytes 21233664 | tf_op jit(solution)/shard_map/dot_general | solution.py:62
  607.0 14.7 %convolution_convert_fusion.2 = bf16[2304,1152]{1,0:T(8,128)(2,1)} fusion(bf16[1536,2304]{1,0:T(8,128)(2,1)} %copy-done.51, bf16[1536,1152]{1,0:T(8,128)(2,1)} %get-tuple-element.179), kind=kOutput, calls=%fused_computation.2 | convolution fusion | flops 8156381184 | bytes 15925248 | tf_op jit(solution)/shard_map/dot_general | solution.py:56
  621.6 14.5 %collective-permute-done.77 = bf16[4,288,1152]{2,1,0:T(8,128)(2,1)} collective-permute-done((bf16[4,288,1152]{2,1,0:T(8,128)(2,1)S(1)}, bf16[4,288,1152]{2,1,0:T(8,128)(2,1)}, u32[]{:S(2)}, u32[]{:S(2)}) %collective-permute-start.77) | collective-permute-done | bytes 2654240 | tf_op jit(solution)/shard_map/ppermute | solution.py:309
  642.1 15.7 %convert_add_fusion = f32[768,2304]{1,0:T(8,128)} fusion(bf16[768,2304]{1,0:T(8,128)(2,1)} %collective-permute-done.45, bf16[2304,2304]{1,0:T(8,128)(2,1)} %bitcast.283, bf16[1536,1152]{1,0:T(8,128)(2,1)} %get-tuple-element.178, bf16[1536,1152]{1,0:T(8,128)(2,1)} %get-tuple-element.179), kind=kOutput, calls=%fused_computation.16 | convolution fusion | flops 8164343808 | bytes 28311552 | tf_op jit(solution)/shard_map/dot_general | solution.py:62
  663.0 29.6 %collective-permute-done.76 = bf16[4,288,1152]{2,1,0:T(8,128)(2,1)} collective-permute-done((bf16[4,288,1152]{2,1,0:T(8,128)(2,1)}, bf16[4,288,1152]{2,1,0:T(8,128)(2,1)}, u32[]{:S(2)}, u32[]{:S(2)}) %collective-permute-start.76) | collective-permute-done | bytes 2654240 | tf_op jit(solution)/shard_map/ppermute | solution.py:309
  720.1 23.8 %collective-permute-done.48 = bf16[192,1152]{1,0:T(8,128)(2,1)S(1)} collective-permute-done((bf16[192,1152]{1,0:T(8,128)(2,1)S(1)}, bf16[192,1152]{1,0:T(8,128)(2,1)S(1)}, u32[]{:S(2)}, u32[]{:S(2)}) %collective-permute-start.48) | collective-permute-done | bytes 442400 | tf_op jit(solution)/shard_map/ppermute | solution.py:309
  753.8 19.6 %collective-permute-done.79 = bf16[2,288,1152]{2,1,0:T(8,128)(2,1)S(1)} collective-permute-done((bf16[2,288,1152]{2,1,0:T(8,128)(2,1)}, bf16[2,288,1152]{2,1,0:T(8,128)(2,1)S(1)}, u32[]{:S(2)}, u32[]{:S(2)}) %collective-permute-start.79) | collective-permute-done | bytes 1327136 | tf_op jit(solution)/shard_map/ppermute | solution.py:309
  776.0 15.4 %collective-permute-done.80 = bf16[288,1152]{1,0:T(8,128)(2,1)S(1)} collective-permute-done((bf16[288,1152]{1,0:T(8,128)(2,1)S(1)}, bf16[288,1152]{1,0:T(8,128)(2,1)S(1)}, u32[]{:S(2)}, u32[]{:S(2)}) %collective-permute-start.80) | collective-permute-done | bytes 663584 | tf_op jit(solution)/shard_map/ppermute | solution.py:309
  813.0 22.1 %attend_back.1 = (bf16[768,512]{1,0:T(8,128)(2,1)}, bf16[768,512]{1,0:T(8,128)(2,1)}, bf16[768,512]{1,0:T(8,128)(2,1)}, f32[768,512]{1,0:T(8,128)}) custom-call(bf16[768,512]{1,0:T(8,128)(2,1)} %copy-done.10, bf16[768,512]{1,0:T(8,128)(2,1)} %convolution_convert_fusion.9.do_ref, bf16[768,512]{1,0:T(8,128)(2,1)} %collective-permute-done.11.k2_ref.v2_ref, ...), custom_call_target="tpu_custom_call" | custom-call | flops 40000000000 | tf_op jit(solution)/shard_map/attend_back/pallas_call | solution.py:230
  857.7 40.9 %collective-permute-done.53 = bf16[768,512]{1,0:T(8,128)(2,1)S(1)} collective-permute-done((bf16[768,512]{1,0:T(8,128)(2,1)}, bf16[768,512]{1,0:T(8,128)(2,1)S(1)}, u32[]{:S(2)}, u32[]{:S(2)}) %collective-permute-start.53) | collective-permute-done | bytes 786464 | tf_op jit(solution)/shard_map/ppermute | solution.py:328
  939.6 13.9 %collective-permute-start.82 = (bf16[288,1152]{1,0:T(8,128)(2,1)S(1)}, bf16[288,1152]{1,0:T(8,128)(2,1)S(1)}, u32[]{:S(2)}, u32[]{:S(2)}) collective-permute-start(bf16[288,1152]{1,0:T(8,128)(2,1)S(1)} %fusion.49), channel_id=1, source_target_pairs={{0,8},{4,12},{8,0},{12,4},{16,24},{20,28},{24,16},{28,20},{1,9},{5... | collective-permute-start | bytes 1990664 | tf_op jit(solution)/shard_map/ppermute | solution.py:309
  986.4 18.5 %collective-permute-done.56 = bf16[192,2304]{1,0:T(8,128)(2,1)S(1)} collective-permute-done((bf16[192,2304]{1,0:T(8,128)(2,1)S(1)}, bf16[192,2304]{1,0:T(8,128)(2,1)S(1)}, u32[]{:S(2)}, u32[]{:S(2)}) %collective-permute-start.56) | collective-permute-done | bytes 884768 | tf_op jit(solution)/shard_map/ppermute | solution.py:313
  (496 shorter events, 542.5 us)
Async XLA Ops:
  12.8 85.2 %collective-permute-start = (bf16[296,1536]{1,0:T(8,128)(2,1)}, bf16[296,1536]{1,0:T(8,128)(2,1)}, u32[]{:S(2)}, u32[]{:S(2)}) collective-permute-start(bf16[296,1536]{1,0:T(8,128)(2,1)} %fusion.36), channel_id=1, source_target_pairs={{0,4},{4,0},{8,12},{12,8},{16,20},{20,16},{24,28},{28,24},{1,5},{5... | collective-permute-start | bytes 2727944 | tf_op jit(solution)/shard_map/ppermute | solution.py:309
  39.4 136.4 %collective-permute-start.23 = (bf16[288,2304]{1,0:T(8,128)(2,1)}, bf16[288,2304]{1,0:T(8,128)(2,1)}, u32[]{:S(2)}, u32[]{:S(2)}) collective-permute-start(bf16[288,2304]{1,0:T(8,128)(2,1)} %pad_maximum_fusion.9), channel_id=1, source_target_pairs={{0,4},{4,0},{8,12},{12,8},{16,20},{20,16},{24,28},{28,24},{1,5},{5... | collective-permute-start | bytes 3981320 | tf_op jit(solution)/shard_map/ppermute | solution.py:309
  98.0 67.2 %collective-permute-start.10 = (bf16[288,2304]{1,0:T(8,128)(2,1)}, bf16[288,2304]{1,0:T(8,128)(2,1)}, u32[]{:S(2)}, u32[]{:S(2)}) collective-permute-start(bf16[288,2304]{1,0:T(8,128)(2,1)} %pad_maximum_fusion.8), channel_id=1, source_target_pairs={{0,8},{4,12},{8,0},{12,4},{16,24},{20,28},{24,16},{28,20},{1,9},{5... | collective-permute-start | bytes 3981320 | tf_op jit(solution)/shard_map/ppermute | solution.py:309
  98.9 75.4 %collective-permute-start.13 = (bf16[288,2304]{1,0:T(8,128)(2,1)}, bf16[288,2304]{1,0:T(8,128)(2,1)}, u32[]{:S(2)}, u32[]{:S(2)}) collective-permute-start(bf16[288,2304]{1,0:T(8,128)(2,1)} %pad_maximum_fusion.9), channel_id=1, source_target_pairs={{0,16},{4,20},{8,24},{12,28},{16,0},{20,4},{24,8},{28,12},{1,17},{... | collective-permute-start | bytes 3981320 | tf_op jit(solution)/shard_map/ppermute | solution.py:309
  110.8 63.5 %collective-permute-start.14 = (bf16[288,1152]{1,0:T(8,128)(2,1)}, bf16[288,1152]{1,0:T(8,128)(2,1)}, u32[]{:S(2)}, u32[]{:S(2)}) collective-permute-start(bf16[288,1152]{1,0:T(8,128)(2,1)} %constant_dynamic-slice_fusion.7), channel_id=1, source_target_pairs={{0,8},{4,12},{8,0},{12,4},{16,24},{20,28},{24,16},{28,20},{1,9},{5... | collective-permute-start | bytes 1990664 | tf_op jit(solution)/shard_map/ppermute | solution.py:309
  174.3 139.7 %collective-permute-start.24 = (bf16[288,2304]{1,0:T(8,128)(2,1)}, bf16[288,2304]{1,0:T(8,128)(2,1)}, u32[]{:S(2)}, u32[]{:S(2)}) collective-permute-start(bf16[288,2304]{1,0:T(8,128)(2,1)} %collective-permute-done.10), channel_id=1, source_target_pairs={{0,4},{4,0},{8,12},{12,8},{16,20},{20,16},{24,28},{28,24},{1,5},{5... | collective-permute-start | bytes 3981320 | tf_op jit(solution)/shard_map/ppermute | solution.py:309
  174.3 120.0 %collective-permute-start.26 = (bf16[288,2304]{1,0:T(8,128)(2,1)}, bf16[288,2304]{1,0:T(8,128)(2,1)}, u32[]{:S(2)}, u32[]{:S(2)}) collective-permute-start(bf16[288,2304]{1,0:T(8,128)(2,1)} %collective-permute-done.10), channel_id=1, source_target_pairs={{0,16},{4,20},{8,24},{12,28},{16,0},{20,4},{24,8},{28,12},{1,17},{... | collective-permute-start | bytes 3981320 | tf_op jit(solution)/shard_map/ppermute | solution.py:309
  175.9 96.1 %collective-permute-start.28 = (bf16[288,1152]{1,0:T(8,128)(2,1)}, bf16[288,1152]{1,0:T(8,128)(2,1)S(1)}, u32[]{:S(2)}, u32[]{:S(2)}) collective-permute-start(bf16[288,1152]{1,0:T(8,128)(2,1)} %get-tuple-element.118), channel_id=1, source_target_pairs={{0,4},{4,0},{8,12},{12,8},{16,20},{20,16},{24,28},{28,24},{1,5},{5... | collective-permute-start | bytes 1990664 | tf_op jit(solution)/shard_map/ppermute | solution.py:309
  188.0 84.0 %collective-permute-start.30 = (bf16[288,1152]{1,0:T(8,128)(2,1)S(1)}, bf16[288,1152]{1,0:T(8,128)(2,1)}, u32[]{:S(2)}, u32[]{:S(2)}) collective-permute-start(bf16[288,1152]{1,0:T(8,128)(2,1)S(1)} %copy-done.42), channel_id=1, source_target_pairs={{0,16},{4,20},{8,24},{12,28},{16,0},{20,4},{24,8},{28,12},{1,17},{... | collective-permute-start | bytes 1990664 | tf_op jit(solution)/shard_map/ppermute | solution.py:309
  213.0 61.9 %collective-permute-start.15 = (bf16[384,2304]{1,0:T(8,128)(2,1)S(1)}, bf16[384,2304]{1,0:T(8,128)(2,1)S(1)}, u32[]{:S(2)}, u32[]{:S(2)}) collective-permute-start(bf16[384,2304]{1,0:T(8,128)(2,1)S(1)} %convolution_convert_fusion.8), channel_id=1, source_target_pairs={{0,1},{1,0},{2,3},{3,2},{4,5},{5,4},{6,7},{7,6},{8,9},{9,8},{10,11... | collective-permute-start | bytes 5308424 | tf_op jit(solution)/shard_map/ppermute | solution.py:313
  274.9 61.8 %collective-permute-start.25 = (bf16[288,2304]{1,0:T(8,128)(2,1)}, bf16[288,2304]{1,0:T(8,128)(2,1)}, u32[]{:S(2)}, u32[]{:S(2)}) collective-permute-start(bf16[288,2304]{1,0:T(8,128)(2,1)} %collective-permute-done.13), channel_id=1, source_target_pairs={{0,4},{4,0},{8,12},{12,8},{16,20},{20,16},{24,28},{28,24},{1,5},{5... | collective-permute-start | bytes 3981320 | tf_op jit(solution)/shard_map/ppermute | solution.py:309
  294.3 62.1 %collective-permute-start.31 = (bf16[288,1152]{1,0:T(8,128)(2,1)}, bf16[288,1152]{1,0:T(8,128)(2,1)}, u32[]{:S(2)}, u32[]{:S(2)}) collective-permute-start(bf16[288,1152]{1,0:T(8,128)(2,1)} %collective-permute-done.30), channel_id=1, source_target_pairs={{0,4},{4,0},{8,12},{12,8},{16,20},{20,16},{24,28},{28,24},{1,5},{5... | collective-permute-start | bytes 1990664 | tf_op jit(solution)/shard_map/ppermute | solution.py:309
  575.6 60.5 %collective-permute-start.77 = (bf16[4,288,1152]{2,1,0:T(8,128)(2,1)S(1)}, bf16[4,288,1152]{2,1,0:T(8,128)(2,1)}, u32[]{:S(2)}, u32[]{:S(2)}) collective-permute-start(bf16[4,288,1152]{2,1,0:T(8,128)(2,1)S(1)} %get-tuple-element.184), channel_id=1, source_target_pairs={{0,4},{4,0},{8,12},{12,8},{16,20},{20,16},{24,28},{28,24},{1,5},{5... | collective-permute-start | bytes 7962632 | tf_op jit(solution)/shard_map/ppermute | solution.py:309
  591.9 100.7 %collective-permute-start.76 = (bf16[4,288,1152]{2,1,0:T(8,128)(2,1)}, bf16[4,288,1152]{2,1,0:T(8,128)(2,1)}, u32[]{:S(2)}, u32[]{:S(2)}) collective-permute-start(bf16[4,288,1152]{2,1,0:T(8,128)(2,1)} %get-tuple-element.186), channel_id=1, source_target_pairs={{0,4},{4,0},{8,12},{12,8},{16,20},{20,16},{24,28},{28,24},{1,5},{5... | collective-permute-start | bytes 7962632 | tf_op jit(solution)/shard_map/ppermute | solution.py:309
  639.6 60.0 %collective-permute-start.78 = (bf16[2,288,1152]{2,1,0:T(8,128)(2,1)}, bf16[2,288,1152]{2,1,0:T(8,128)(2,1)S(1)}, u32[]{:S(2)}, u32[]{:S(2)}) collective-permute-start(bf16[2,288,1152]{2,1,0:T(8,128)(2,1)} %fusion.33), channel_id=1, source_target_pairs={{0,16},{4,20},{8,24},{12,28},{16,0},{20,4},{24,8},{28,12},{1,17},{... | collective-permute-start | bytes 3981320 | tf_op jit(solution)/shard_map/ppermute | solution.py:309
  661.4 50.3 %collective-permute-start.47 = (bf16[2,192,1152]{2,1,0:T(8,128)(2,1)S(1)}, bf16[2,192,1152]{2,1,0:T(8,128)(2,1)S(1)}, u32[]{:S(2)}, u32[]{:S(2)}) collective-permute-start(bf16[2,192,1152]{2,1,0:T(8,128)(2,1)S(1)} %slice_bitcast_fusion.6), channel_id=1, source_target_pairs={{0,8},{4,12},{8,0},{12,4},{16,24},{20,28},{24,16},{28,20},{1,9},{5... | collective-permute-start | bytes 2654216 | tf_op jit(solution)/shard_map/ppermute | solution.py:309
  699.9 52.6 %collective-permute-start.83 = (bf16[288,1152]{1,0:T(8,128)(2,1)S(1)}, bf16[288,1152]{1,0:T(8,128)(2,1)}, u32[]{:S(2)}, u32[]{:S(2)}) collective-permute-start(bf16[288,1152]{1,0:T(8,128)(2,1)S(1)} %fusion.50), channel_id=1, source_target_pairs={{0,8},{4,12},{8,0},{12,4},{16,24},{20,28},{24,16},{28,20},{1,9},{5... | collective-permute-start | bytes 1990664 | tf_op jit(solution)/shard_map/ppermute | solution.py:309
  717.5 55.9 %collective-permute-start.79 = (bf16[2,288,1152]{2,1,0:T(8,128)(2,1)}, bf16[2,288,1152]{2,1,0:T(8,128)(2,1)S(1)}, u32[]{:S(2)}, u32[]{:S(2)}) collective-permute-start(bf16[2,288,1152]{2,1,0:T(8,128)(2,1)} %fusion.34), channel_id=1, source_target_pairs={{0,16},{4,20},{8,24},{12,28},{16,0},{20,4},{24,8},{28,12},{1,17},{... | collective-permute-start | bytes 3981320 | tf_op jit(solution)/shard_map/ppermute | solution.py:309
  751.1 57.1 %collective-permute-start.71 = (bf16[4,288,1152]{2,1,0:T(8,128)(2,1)S(1)}, bf16[4,288,1152]{2,1,0:T(8,128)(2,1)S(1)}, u32[]{:S(2)}, u32[]{:S(2)}) collective-permute-start(bf16[4,288,1152]{2,1,0:T(8,128)(2,1)S(1)} %get-tuple-element.188), channel_id=1, source_target_pairs={{0,4},{4,0},{8,12},{12,8},{16,20},{20,16},{24,28},{28,24},{1,5},{5... | collective-permute-start | bytes 7962632 | tf_op jit(solution)/shard_map/ppermute | solution.py:309
  810.0 99.1 %collective-permute-start.81 = (bf16[2,288,1152]{2,1,0:T(8,128)(2,1)}, bf16[2,288,1152]{2,1,0:T(8,128)(2,1)S(1)}, u32[]{:S(2)}, u32[]{:S(2)}) collective-permute-start(bf16[2,288,1152]{2,1,0:T(8,128)(2,1)} %fusion.35), channel_id=1, source_target_pairs={{0,16},{4,20},{8,24},{12,28},{16,0},{20,4},{24,8},{28,12},{1,17},{... | collective-permute-start | bytes 3981320 | tf_op jit(solution)/shard_map/ppermute | solution.py:309
  811.8 94.8 %collective-permute-start.72 = (bf16[4,288,512]{2,1,0:T(8,128)(2,1)}, bf16[4,288,512]{2,1,0:T(8,128)(2,1)}, u32[]{:S(2)}, u32[]{:S(2)}) collective-permute-start(bf16[4,288,512]{2,1,0:T(8,128)(2,1)} %get-tuple-element.194), channel_id=1, source_target_pairs={{0,4},{4,0},{8,12},{12,8},{16,20},{20,16},{24,28},{28,24},{1,5},{5... | collective-permute-start | bytes 3538952 | tf_op jit(solution)/shard_map/ppermute | solution.py:309
  836.4 62.2 %collective-permute-start.53 = (bf16[768,512]{1,0:T(8,128)(2,1)}, bf16[768,512]{1,0:T(8,128)(2,1)S(1)}, u32[]{:S(2)}, u32[]{:S(2)}) collective-permute-start(bf16[768,512]{1,0:T(8,128)(2,1)} %get-tuple-element.128), channel_id=1, source_target_pairs={{8,0},{12,4},{24,16},{28,20},{9,1},{13,5},{25,17},{29,21},{10,2},{... | collective-permute-start | bytes 2359304 | tf_op jit(solution)/shard_map/ppermute | solution.py:328
  841.3 67.2 %collective-permute-start.63 = (bf16[4,288,512]{2,1,0:T(8,128)(2,1)S(1)}, bf16[4,288,512]{2,1,0:T(8,128)(2,1)S(1)}, u32[]{:S(2)}, u32[]{:S(2)}) collective-permute-start(bf16[4,288,512]{2,1,0:T(8,128)(2,1)S(1)} %get-tuple-element.204), channel_id=1, source_target_pairs={{0,4},{4,0},{8,12},{12,8},{16,20},{20,16},{24,28},{28,24},{1,5},{5... | collective-permute-start | bytes 3538952 | tf_op jit(solution)/shard_map/ppermute | solution.py:309
  904.3 54.0 %collective-permute-start.67 = (bf16[4,288,512]{2,1,0:T(8,128)(2,1)S(1)}, bf16[4,288,512]{2,1,0:T(8,128)(2,1)S(1)}, u32[]{:S(2)}, u32[]{:S(2)}) collective-permute-start(bf16[4,288,512]{2,1,0:T(8,128)(2,1)S(1)} %get-tuple-element.199), channel_id=1, source_target_pairs={{0,4},{4,0},{8,12},{12,8},{16,20},{20,16},{24,28},{28,24},{1,5},{5... | collective-permute-start | bytes 3538952 | tf_op jit(solution)/shard_map/ppermute | solution.py:309
  (133 other events, 2319.3 us)

commit v3 on v2

--- a/solution.py
+++ b/solution.py
@@ -62,6 +62,387 @@
     return lax.dot_general(
         left, right, (((1,), (1,)), ((), ())), preferred_element_type=f32
     )
+
+
+def gather_kernel(
+    m, attn_ref, guk_ref, gus_ref, dk_ref, ds_ref, attn_buf, gu_buf, d_buf, send_sem, recv_sem, own_sem
+):
+    tok, tp = lax.axis_index("tok"), lax.axis_index("tp")
+    z, y = tok // m, tok % m
+    flip1 = z + 1 - 2 * (z % 2)
+    flip2 = (z + 2) % 4
+    flip3 = 3 - z
+    slot = lambda zs, ys: zs * m + ys
+    others = range(1, m)
+    used = iter(range(9 + 8 * (m - 1)))
+
+    def hop(src, dst, number, target):
+        return pltpu.make_async_remote_copy(
+            src_ref=src,
+            dst_ref=dst,
+            send_sem=send_sem.at[number],
+            recv_sem=recv_sem.at[number],
+            device_id=(target, tp),
+            device_id_type=pl.DeviceIdType.MESH,
+        )
+
+    barrier = pltpu.get_barrier_semaphore()
+    peers = [slot(f, y) for f in (flip1, flip2, flip3)] + [slot(z, (y + j) % m) for j in others]
+    for peer in peers:
+        pl.semaphore_signal(barrier, inc=1, device_id=(peer, tp), device_id_type=pl.DeviceIdType.MESH)
+    pl.semaphore_wait(barrier, len(peers))
+
+    own = [
+        pltpu.make_async_copy(src, dst.at[tok], own_sem.at[i])
+        for i, (src, dst) in enumerate(((attn_ref, attn_buf), (guk_ref, gu_buf), (dk_ref, d_buf)))
+    ]
+    ups = [next(used) for _ in range(3)]
+    downs = [next(used) for _ in range(3)]
+    y_own = {j: next(used) for j in others}
+    y_gu = {j: next(used) for j in others}
+    y_up = {(s, j): next(used) for s in (1, 2, 3) for j in others}
+    y_down = {(s, j): next(used) for s in (1, 2, 3) for j in others}
+    n_gu1, n_d1, n_gu2 = next(used), next(used), next(used)
+
+    def line(step, way):
+        at = slot(z - way * (step - 1), y)
+        src = attn_ref if step == 1 else attn_buf.at[at]
+        return hop(src, attn_buf.at[at], (ups if way > 0 else downs)[step - 1], slot(z + way, y))
+
+    def can_send(step, way):
+        return (z >= step - 1) & (z <= 2) if way > 0 else (z <= 4 - step) & (z >= 1)
+
+    def can_take(step, way):
+        return z >= step if way > 0 else z <= 3 - step
+
+    def taken(step, way):
+        at = slot(z - way * step, y)
+        return hop(attn_buf.at[at], attn_buf.at[at], (ups if way > 0 else downs)[step - 1], tok)
+
+    def relay(step, way, j, back):
+        at = slot(z - way * step, (y - j) % m if back else y)
+        number = (y_up if way > 0 else y_down)[step, j]
+        return hop(attn_buf.at[at], attn_buf.at[at], number, slot(z, (y + j) % m))
+
+    y_own_hops = [hop(attn_ref, attn_buf.at[tok], y_own[j], slot(z, (y + j) % m)) for j in others]
+    y_gu_hops = [hop(guk_ref, gu_buf.at[tok], y_gu[j], slot(z, (y + j) % m)) for j in others]
+    z_hops = [
+        hop(gus_ref, gu_buf.at[tok], n_gu1, slot(flip1, y)),
+        hop(guk_ref, gu_buf.at[tok], n_gu2, slot(flip2, y)),
+        hop(ds_ref, d_buf.at[tok], n_d1, slot(flip1, y)),
+    ]
+
+    for way in (1, -1):
+        pl.when(can_send(1, way))(line(1, way).start)
+    for c in y_own_hops + y_gu_hops + own:
+        c.start()
+    for step in (1, 2, 3):
+        for way in (1, -1):
+
+            @pl.when(can_take(step, way))
+            def _(step=step, way=way):
+                taken(step, way).wait_recv()
+                if step < 3:
+                    pl.when(can_send(step + 1, way))(line(step + 1, way).start)
+                for j in others:
+                    relay(step, way, j, False).start()
+
+        if step == 2:
+            for c in z_hops:
+                c.start()
+    for j in others:
+        at = slot(z, (y - j) % m)
+        hop(attn_buf.at[at], attn_buf.at[at], y_own[j], tok).wait_recv()
+        hop(gu_buf.at[at], gu_buf.at[at], y_gu[j], tok).wait_recv()
+    for step in (1, 2, 3):
+        for way in (1, -1):
+
+            @pl.when(can_take(step, way))
+            def _(step=step, way=way):
+                for j in others:
+                    relay(step, way, j, True).wait_recv()
+                    relay(step, way, j, False).wait_send()
+
+            pl.when(can_send(step, way))(line(step, way).wait_send)
+    for number, ref, f in ((n_gu1, gu_buf, flip1), (n_d1, d_buf, flip1), (n_gu2, gu_buf, flip2)):
+        at = slot(f, y)
+        hop(ref.at[at], ref.at[at], number, tok).wait_recv()
+    for c in y_own_hops + y_gu_hops + z_hops:
+        c.wait_send()
+    for c in own:
+        c.wait()
+
+
+def gather_call(n, attn, gu_keep, gu_send, d_keep, d_send):
+    m = n // 4
+    count = 9 + 8 * (m - 1)
+    hbm = pl.BlockSpec(memory_space=pltpu.HBM)
+    return pl.pallas_call(
+        partial(gather_kernel, m),
+        out_shape=tuple(jax.ShapeDtypeStruct((n,) + a.shape, bf16) for a in (attn, gu_keep, d_keep)),
+        in_specs=[hbm] * 5,
+        out_specs=(hbm,) * 3,
+        scratch_shapes=[
+            pltpu.SemaphoreType.DMA((count,)),
+            pltpu.SemaphoreType.DMA((count,)),
+            pltpu.SemaphoreType.DMA((3,)),
+        ],
+        compiler_params=pltpu.CompilerParams(collective_id=0, has_side_effects=True),
+        name="gather_first",
+    )(attn, gu_keep, gu_send, d_keep, d_send)
+
+
+def tie_kernel(*refs):
+    del refs
+
+
+def tie(values, *earlier):
+    leaves, tree = jax.tree.flatten(values)
+    earlier = jax.tree.leaves(earlier)
+    anywhere = pl.BlockSpec(memory_space=pl.ANY)
+    found = pl.pallas_call(
+        tie_kernel,
+        out_shape=tuple(jax.ShapeDtypeStruct(v.shape, v.dtype) for v in leaves),
+        in_specs=[anywhere] * (len(leaves) + len(earlier)),
+        out_specs=(anywhere,) * len(leaves),
+        input_output_aliases={i: i for i in range(len(leaves))},
+        name="tie",
+    )(*leaves, *earlier)
+    return jax.tree.unflatten(tree, found)
+
+
+def add_rows(total_ref, arrived_ref):
+    block = 32 if total_ref.shape[0] % 32 == 0 else total_ref.shape[0]
+
+    def body(i, carry):
+        at = pl.ds(pl.multiple_of(i * block, block), block)
+        total_ref[at, :] = total_ref[at, :] + arrived_ref[at, :].astype(f32)
+        return carry
+
+    lax.fori_loop(0, total_ref.shape[0] // block, body, 0)
+
+
+def round_rows(out_ref, value_ref):
+    block = 32 if out_ref.shape[0] % 32 == 0 else out_ref.shape[0]
+
+    def body(i, carry):
+        at = pl.ds(pl.multiple_of(i * block, block), block)
+        out_ref[at, :] = value_ref[at, :].astype(out_ref.dtype)
+        return carry
+
+    lax.fori_loop(0, out_ref.shape[0] // block, body, 0)
+
+
+def comm_kernel(m, chain, kinds, *refs):
+    count = {"gather_pair": 1, "gather_tp": 1, "reduce_pair": 2, "reduce_tp": 2}[chain]
+    ins, refs = refs[:count], refs[count:]
+    sent, refs = refs[: len(kinds)], refs[len(kinds) :]
+    out_ref, refs = refs[0], refs[1:]
+    landed, refs = refs[: len(kinds)], refs[len(kinds) :]
+    send_sem, recv_sem, own_sem = refs[:3]
+    scratch = refs[3:]
+    tok, tp = lax.axis_index("tok"), lax.axis_index("tp")
+    z, y = tok // m, tok % m
+    x, c = tp // 2, tp % 2
+    others = range(1, m)
+    zlo = ((z + 1 - 2 * (z % 2)) * m + y, tp)
+    zhi = (((z + 2) % 4) * m + y, tp)
+    over_x, over_core = (tok, (tp + 2) % 4), (tok, tp + 1 - 2 * c)
+    used = iter(range(8 + len(kinds)))
+
+    def hop(src, dst, target):
+        number = next(used)
+        return pltpu.make_async_remote_copy(
+            src_ref=src,
+            dst_ref=dst,
+            send_sem=send_sem.at[number],
+            recv_sem=recv_sem.at[number],
+            device_id=target,
+            device_id_type=pl.DeviceIdType.MESH,
+        )
+
+    def target(kind):
+        if kind[0] == "y":
+            return (z * m + (y + kind[1]) % m, tp)
+        return {"zlo": zlo, "zhi": zhi}[kind[0]]
+
+    peers = [over_x, over_core]
+    if chain in ("gather_pair", "reduce_pair") or ("zlo",) in kinds:
+        peers.append(zlo)
+    if ("zhi",) in kinds:
+        peers.append(zhi)
+    if any(kind[0] == "y" for kind in kinds):
+        peers += [(z * m + (y + j) % m, tp) for j in others]
+    barrier = pltpu.get_barrier_semaphore()
+    for peer in peers:
+        pl.semaphore_signal(barrier, inc=1, device_id=peer, device_id_type=pl.DeviceIdType.MESH)
+    pl.semaphore_wait(barrier, len(peers))
+
+    beside = [hop(a, b, target(kind)) for a, b, kind in zip(sent, landed, kinds)]
+    waits = []
+
+    def start_beside():
+        for b in beside:
+            b.start()
+
+    if chain == "gather_tp":
+        (a_ref,) = ins
+        own = pltpu.make_async_copy(a_ref, out_ref.at[tp], own_sem)
+        there = (tp + 2) % 4
+        first = hop(a_ref, out_ref.at[tp], over_x)
+        near = hop(a_ref, out_ref.at[tp], over_core)
+        far = hop(out_ref.at[there], out_ref.at[there], over_core)
+        first.start()
+        start_beside()
+        near.start()
+        own.start()
+        first.wait_recv()
+        far.start()
+        near.wait_recv()
+        far.wait_recv()
+        own.wait()
+        waits = [first, near, far]
+    elif chain == "gather_pair":
+        (a_ref,) = ins
+        half = a_ref.shape[0] // 2
+        top, low = pl.ds(0, half), pl.ds(half, half)
+        own = pltpu.make_async_copy(a_ref, out_ref.at[0], own_sem)
+        first_z = hop(a_ref, out_ref.at[1], zlo)
+        first_x = hop(a_ref, out_ref.at[2], over_x)
+        next_x = hop(out_ref.at[1, top], out_ref.at[3, top], over_x)
+        next_z = hop(out_ref.at[2, low], out_ref.at[3, low], zlo)
+        core = [
+            hop(a_ref if k == 0 else out_ref.at[k], out_ref.at[4 + k], over_core) for k in range(4)
+        ]
+        first_z.start()
+        first_x.start()
+        own.start()
+        core[0].start()
+        start_beside()
+        first_z.wait_recv()
+        next_x.start()
+        core[1].start()
+        first_x.wait_recv()
+        next_z.start()
+        core[2].start()
+        next_x.wait_recv()
+        next_z.wait_recv()
+        core[3].start()
+        for each in core:
+            each.wait_recv()
+        own.wait()
+        waits = [first_z, first_x, next_x, next_z] + core
+    elif chain == "reduce_tp":
+        far_ref, near_ref = ins
+        near, from_core, to_go, from_x = scratch
+        part = out_ref.shape[0]
+        own = pltpu.make_async_copy(near_ref, near, own_sem)
+        core = hop(far_ref, from_core, over_core)
+        over = hop(to_go, from_x, over_x)
+        core.start()
+        own.start()
+        start_beside()
+        own.wait()
+        core.wait_recv()
+        away = pl.ds(pl.multiple_of((1 - x) * part, part), part)
+        here = pl.ds(pl.multiple_of(x * part, part), part)
+        add_rows(near.at[away], from_core.at[away])
+        round_rows(to_go, near.at[away])
+        over.start()
+        add_rows(near.at[here], from_core.at[here])
+        round_rows(out_ref, near.at[here])
+        over.wait_recv()
+        add_rows(out_ref, from_x)
+        waits = [core, over]
+    else:
+        far_ref, near_ref = ins
+        near, from_core, left_go, left_in, right_go, right_in = scratch
+        part, width = out_ref.shape
+        mid = width // 2
+        left, right = pl.ds(0, mid), pl.ds(mid, mid)
+        rows = lambda k, count=1: pl.ds(k * part, count * part)
+        own = pltpu.make_async_copy(near_ref, near, own_sem)
+        core = hop(far_ref, from_core, over_core)
+        left_x = hop(left_go.at[rows(0, 2)], left_in.at[rows(0, 2)], over_x)
+        right_z = hop(right_go.at[rows(0, 2)], right_in.at[rows(0, 2)], zlo)
+        left_z = hop(left_go.at[rows(2)], left_in.at[rows(2)], zlo)
+        right_x = hop(right_go.at[rows(2)], right_in.at[rows(2)], over_x)
+        core.start()
+        own.start()
+        start_beside()
+        own.wait()
+        core.wait_recv()
+        add_rows(near.at[rows(1, 3)], from_core.at[rows(1, 3)])
+        round_rows(left_go.at[rows(0, 2)], near.at[rows(2, 2), left])
+        left_x.start()
+        round_rows(right_go.at[rows(0)], near.at[rows(1), right])
+        round_rows(right_go.at[rows(1)], near.at[rows(3), right])
+        right_z.start()
+        add_rows(near.at[rows(0)], from_core.at[rows(0)])
+        left_x.wait_recv()
+        add_rows(near.at[rows(0, 2), left], left_in.at[rows(0, 2)])
+        round_rows(left_go.at[rows(2)], near.at[rows(1), left])
+        left_z.start()
+        right_z.wait_recv()
+        add_rows(near.at[rows(0), right], right_in.at[rows(0)])
+        add_rows(near.at[rows(2), right], right_in.at[rows(1)])
+        round_rows(right_go.at[rows(2)], near.at[rows(2), right])
+        right_x.start()
+        round_rows(out_ref, near.at[rows(0)])
+        left_z.wait_recv()
+        add_rows(out_ref.at[:, left], left_in.at[rows(2)])
+        right_x.wait_recv()
+        add_rows(out_ref.at[:, right], right_in.at[rows(2)])
+        waits = [core, left_x, right_z, left_z, right_x]
+    for each in waits:
+        each.wait_send()
+    for b in beside:
+        b.wait_recv()
+        b.wait_send()
+
+
+def comm_call(n, number, chain, ins, beside=()):
+    m = n // 4
+    kinds = tuple(kind for _, kind in beside)
+    arrays = [a for a, _ in beside]
+    hbm = pl.BlockSpec(memory_space=pltpu.HBM)
+    vmem = pl.BlockSpec(memory_space=pltpu.VMEM)
+    rows, width = ins[-1].shape
+    scratch = []
+    if chain == "gather_tp":
+        out = jax.ShapeDtypeStruct((4, rows, width), bf16)
+    elif chain == "gather_pair":
+        out = jax.ShapeDtypeStruct((8, rows, width), bf16)
+    elif chain == "reduce_tp":
+        out = jax.ShapeDtypeStruct((rows // 2, width), f32)
+        scratch = [
+            pltpu.VMEM((rows, width), f32),
+            pltpu.VMEM((rows, width), bf16),
+            pltpu.VMEM((rows // 2, width), bf16),
+            pltpu.VMEM((rows // 2, width), bf16),
+        ]
+    else:
+        out = jax.ShapeDtypeStruct((rows // 4, width), f32)
+        scratch = [pltpu.VMEM((rows, width), f32), pltpu.VMEM((rows, width), bf16)]
+        scratch += [pltpu.VMEM((rows // 4 * 3, width // 2), bf16)] * 4
+    found = pl.pallas_call(
+        partial(comm_kernel, m, chain, kinds),
+        out_shape=(out,) + tuple(jax.ShapeDtypeStruct(a.shape, a.dtype) for a in arrays),
+        in_specs=[hbm] * (len(ins) + len(arrays)),
+        out_specs=(vmem if scratch else hbm,) + (hbm,) * len(arrays),
+        scratch_shapes=[
+            pltpu.SemaphoreType.DMA((8 + len(kinds),)),
+            pltpu.SemaphoreType.DMA((8 + len(kinds),)),
+            pltpu.SemaphoreType.DMA,
+        ]
+        + scratch,
+        compiler_params=pltpu.CompilerParams(
+            collective_id=number, has_side_effects=True, vmem_limit_bytes=32 << 20
+        ),
+        name=chain,
+    )(*ins, *arrays)
+    first = found[0].reshape(-1, width) if not scratch else found[0]
+    return (first,) + tuple(found[1:])
 
 
 def rotate_in(values, cosine, sine_tab):
@@ -332,14 +713,6 @@
 
     step = Order(seq_lengths)
 
-    def z_line(a, way, at):
-        pairs = [
-            (zs * m + ys, (zs + way) * m + ys)
-            for zs in (range(at - 1, 3) if way > 0 else range(1, 5 - at))
-            for ys in range(m)
-        ]
-        return lax.ppermute(a, "tok", pairs)
-
     def y_others(a):
         return [y_shift(a, j) for j in range(1, m)]
 
@@ -350,46 +723,22 @@
     gains = jnp.concatenate([gain_attn_in, gain_attn_out, gain_ffn_in, gain_ffn_out])
     attn_cols = attn_own.shape[1]
     gains = jnp.pad(gains, (0, attn_cols - gains.shape[0])).reshape(1, attn_cols)
-    attn_own = jnp.concatenate([attn_own, jnp.pad(gains, ((0, 7), (0, 0)))], axis=0)
-    up1, down1 = z_line(attn_own, 1, 1), z_line(attn_own, -1, 1)
-    attn_y = {0: y_others(attn_own)}
+    attn_own = jnp.concatenate([attn_own, jnp.pad(gains, ((0, 15), (0, 0)))], axis=0)
     gu_keep = jnp.concatenate([halves(w_gate, zlo), halves(w_up, zlo)], axis=1)
     gu_send = jnp.concatenate([halves(w_gate, 1 - zlo), halves(w_up, 1 - zlo)], axis=1)
     d_keep, d_send = halves(w_down, zlo), halves(w_down, 1 - zlo)
-    gu_y = {0: y_others(gu_keep)}
-    up1, down1 = step(up1, down1)
-    up2, down2 = z_line(up1, 1, 2), z_line(down1, -1, 2)
-    up2, down2 = step(up2, down2)
-    attn_z = {0: attn_own, 2: jnp.where(z >= 2, up2, down2)}
-    up3, down3 = z_line(up2, 1, 3), z_line(down2, -1, 3)
-    attn_y[2] = y_others(attn_z[2])
-    gu_send, gu_first, d_send = step(gu_send, gu_keep, d_send)
-    gu_z = {0: gu_keep, 1: to_zlo(gu_send)}
-    gu_z[2] = to_zhi(gu_first)
-    d_z = {0: d_keep, 1: to_zlo(d_send)}
-    up3, down3 = step(up3, down3)
-    attn_z[1] = jnp.where(z >= 1, up1, down3)
-    attn_z[3] = jnp.where(z >= 3, up3, down1)
-    attn_y[1], attn_y[3] = y_others(attn_z[1]), y_others(attn_z[3])
-    gu_z[1] = step(gu_z[1])
-    gu_y[1] = y_others(gu_z[1])
-    gu_z[3] = to_zhi(gu_z[1])
-    attn_y = step(attn_y)
-
-    attn_buf = jnp.zeros((n,) + attn_own.shape, bf16)
-    for k in range(4):
-        for j, piece in enumerate([attn_z[k]] + attn_y[k]):
-            attn_buf = put(attn_buf, piece, ((z - k) % 4) * m + (y - j) % m)
+    own_index = tok * rows + jnp.arange(rows, dtype=jnp.int32)
+    seq_start = sequence_start(seq_lengths, own_index)
+    cosine, sine_tab = rope_tables(own_index - seq_start)
+    low = (seq_start - (tok - REACH) * rows)[:, None]
+    attn_own, cosine, sine_tab, low = step(attn_own, cosine, sine_tab, low)
+    attn_buf, gu_buf, d_buf = gather_call(n, attn_own, gu_keep, gu_send, d_keep, d_send)
+    gu_z = {k: pick(gu_buf, (z ^ k) * m + y) for k in (1, 2)}
+    d_z = {0: d_keep, 1: pick(d_buf, (z ^ 1) * m + y)}
+
     gains_all = attn_buf[:, wrows, : 4 * wrows].reshape(n, 4, wrows)
     gains_all = gains_all.transpose(1, 0, 2).reshape(4, 1, width).astype(f32)
     gain_one, gain_two, gain_three, gain_four = (gains_all[i] for i in range(4))
-
-    def ffn_matrix(by_z, by_y):
-        buffer = jnp.zeros((n,) + by_z[0].shape, bf16)
-        for k in range(4):
-            for j, piece in enumerate([by_z[k]] + by_y[k]):
-                buffer = put(buffer, piece, (z ^ k) * m + (y - j) % m)
-        return buffer.reshape(width, -1)
 
     def own_slice(a):
         return lax.dynamic_slice_in_dim(a, tpi * part, part, 0)
@@ -403,26 +752,6 @@
             buffer = put(buffer, block.astype(a.dtype), tpi ^ k)
         return buffer.reshape((-1,) + a.shape[1:])
 
-    def gather_pair(a):
-        a_z = to_zlo(a)
-        a_x = to_x(a)
-        mid = width // 2
-        a_xz = jnp.concatenate([to_x(a_z[:, :mid]), to_zlo(a_x[:, mid:])], axis=1)
-        side = jnp.concatenate([a, a_z, a_x, a_xz])
-        return jnp.concatenate([side, to_core(side)])
-
-    def reduce_pair(compute):
-        far = compute(1).astype(bf16)
-        near = compute(0) + to_core(far).astype(f32)
-        near = near.reshape(2, 2, part, width)
-        mid = width // 2
-        left, right = near[..., :mid], near[..., mid:]
-        left = left[0] + to_x(left[1].astype(bf16)).astype(f32)
-        right = right[:, 0] + to_zlo(right[:, 1].astype(bf16)).astype(f32)
-        left = left[0] + to_zlo(left[1].astype(bf16)).astype(f32)
-        right = right[0] + to_x(right[1].astype(bf16)).astype(f32)
-        return jnp.concatenate([left, right], axis=1)
-
     def reduce_tp(compute):
         far = compute(1 - core).astype(bf16)
         near = compute(core) + to_core(far).astype(f32)
@@ -432,51 +761,64 @@
     def core_rows(a, c):
         return pick(a.reshape(2, 2, part, a.shape[1]), c, 1).reshape(2 * part, a.shape[1])
 
-    own_index = tok * rows + jnp.arange(rows, dtype=jnp.int32)
-    seq_start = sequence_start(seq_lengths, own_index)
-    cosine, sine_tab = rope_tables(own_index - seq_start)
-    low = (seq_start - (tok - REACH) * rows)[:, None]
-
     qkv_cols = head_cols + 2 * kv_cols
     qkv_mat = attn_buf[:, :wrows, :qkv_cols].reshape(width, qkv_cols)
     out_mat = attn_buf[:, :wrows, qkv_cols:].reshape(width, head_cols)
     hidden_one, query, key_value = qkv_call(
         inputs, gain_one, qkv_mat, cosine, sine_tab, heads, kv_heads
     )
-    key_value = step(key_value)
     window = [within_quad(key_value, by) for by in range(REACH, 0, -1)] + [key_value]
-    gu_z[2], d_z[1], d_first = step(gu_z[2], d_z[1], d_keep)
-    gu_y[2] = y_others(gu_z[2])
-    d_y = {0: y_others(d_first), 1: y_others(d_z[1])}
-    d_z[2], d_z[3] = to_zhi(d_first), to_zhi(d_z[1])
-    window = step(window)
     attended, lse = attend_call(query, window, low, heads, kv_heads)
-    attended = step(attended)
-    attn = reduce_tp(lambda c: contract_cols(core_rows(attended, c), out_mat))
-    gu_z[3] = step(gu_z[3])
-    gu_y[3] = y_others(gu_z[3])
-    d_z[2] = step(d_z[2])
-    d_y[2] = y_others(d_z[2])
-    attn, d_z[3] = step(attn, d_z[3])
-    d_y[3] = y_others(d_z[3])
+    far, near = (contract_cols(core_rows(attended, c), out_mat) for c in (1 - core, core))
+    def over_y(a):
+        return [(a, ("y", j)) for j in range(1, m)]
+
+    attn, gu3, *arrived = comm_call(
+        n, 1, "reduce_tp", (far.astype(bf16), near), [(gu_z[1], ("zhi",))] + over_y(gu_z[1]) + over_y(gu_z[2])
+    )
+    gu_z[3] = gu3
+    gu_y = {1: arrived[: m - 1], 2: arrived[m - 1 :]}
 
     resid = own_slice(inputs).astype(f32)
     unit_two, inv_two = norm_parts(attn)
     resid_mid = resid + unit_two * gain_two
     unit_three, inv_three = norm_parts(resid_mid)
-    hidden_two = gather_pair((unit_three * gain_three).astype(bf16))
-    gu_mat, down_mat = ffn_matrix(gu_z, gu_y), ffn_matrix(d_z, d_y)
+    def fill(buffer, by_z, by_y):
+        for k in by_z:
+            buffer = put(buffer, by_z[k], (z ^ k) * m + y)
+        for k in by_y:
+            for j, piece in enumerate(by_y[k]):
+                buffer = put(buffer, piece, (z ^ k) * m + (y - j - 1) % m)
+        return buffer
+
+    hidden_two = (unit_three * gain_three).astype(bf16)
+    hidden_two, d2, d3, *arrived = comm_call(
+        n,
+        2,
+        "gather_pair",
+        (hidden_two,),
+        [(d_z[0], ("zhi",)), (d_z[1], ("zhi",))] + over_y(gu_z[3]) + over_y(d_z[0]) + over_y(d_z[1]),
+    )
+    gu_y[3] = arrived[: m - 1]
+    d_y = {0: arrived[m - 1 : 2 * m - 2], 1: arrived[2 * m - 2 :]}
+    d_z[2], d_z[3] = d2, d3
+    d_y[2], d_y[3] = y_others(d2), y_others(d3)
+    gu_mat = fill(gu_buf, {3: gu_z[3]}, gu_y).reshape(width, -1)
+    down_mat = fill(d_buf, {2: d_z[2], 3: d_z[3]}, d_y).reshape(width, -1)
     gate_up = jnp.dot(hidden_two, gu_mat, preferred_element_type=f32)
     gate_vals, up_vals = gate_up[:, :half], gate_up[:, half:]
     activated, gelu_pull = jax.vjp(partial(jax.nn.gelu, approximate=True), gate_vals)
     inner = (activated * up_vals).astype(bf16)
-    ffn = reduce_pair(lambda k: contract_cols(jnp.split(inner, 2)[k], down_mat))
+    inner_far, inner_near = inner[2 * rows // 2 :], inner[: 2 * rows // 2]
+    (ffn,) = comm_call(
+        n, 3, "reduce_pair", (contract_cols(inner_far, down_mat).astype(bf16), contract_cols(inner_near, down_mat))
+    )
     unit_four, inv_four = norm_parts(ffn)
     layer_out = gather_tp((resid_mid + unit_four * gain_four).astype(bf16))
 
     grad_out = own_slice(out_grad).astype(f32)
     d_ffn, grad_four = norm_back(grad_out, gain_four, unit_four, inv_four)
-    d_ffn_all = gather_pair(d_ffn.astype(bf16))
+    (d_ffn_all,) = comm_call(n, 4, "gather_pair", (d_ffn.astype(bf16),))
     d_inner = jnp.dot(d_ffn_all, down_mat, preferred_element_type=f32)
 
     def y_send(grad):

time: 1030 us -> 980 us (0.951)
  Pallas kernels: 44.1 us -> 399 us
  waiting for transfers between devices: 513 us -> 249 us
  starting transfers between devices: 128 us -> 67.6 us
  local copies, waits for them, and re-layouts: 126 us -> 81.8 us
  other arithmetic: 68 us -> 42 us
    pallas_call x0 -> x5, Pallas kernels: none -> 355 us  [the longest x4 215 us: comm_call(): pl.pallas_call(partial(comm_kernel, m, chain, kinds), out_shape=(out,) +...]
    ppermute x50 -> x28, waiting for transfers between devices: 314 us -> 166 us  [over_tok(): return lambda a: lax.ppermute(a, 'tok', pairs)]
    ppermute x24 -> x13, waiting for transfers between devices: 84.6 us -> 22 us  [over_tp(): return lambda a: lax.ppermute(a, 'tp', pairs)]
    ppermute x6 -> x0, waiting for transfers between devices: 53.8 us -> none  [z_line(): return lax.ppermute(a, 'tok', pairs)]
    ppermute x50 -> x28, starting transfers between devices: 85.3 us -> 50.6 us  [over_tok(): return lambda a: lax.ppermute(a, 'tok', pairs)]
    dynamic_update_slice x29 -> x17, local copies, waits for them, and re-layouts: 36.3 us -> 11.8 us  [put(): return lax.dynamic_update_index_in_dim(buffer, block, index, 0)]
    unnamed x154 -> x122, local copies, waits for them, and re-layouts: 36.4 us -> 19.8 us
    concatenate x3 -> x1, other arithmetic: 17.4 us -> 2.18 us  [local(): jnp.concatenate([attn_own, jnp.pad(gains, ((0, 15), (0, 0)))], axis=0)]
  transfers between devices with their start and end apart: 84 -> 45, of which waited for: 43 -> 21; matrix products, arithmetic and copies ran while one was open for 21% -> 16% of each run, Pallas kernels for 4% -> 2%
where the time goes in v3:
time: 980 us; the launch traced here: 974 us
  Pallas kernels  399 us (41%)
  waiting for transfers between devices  249 us (25%)
  matrix products  132 us (13%)
  local copies, waits for them, and re-layouts  81.8 us (8%)
  starting transfers between devices  67.6 us (7%)
  other arithmetic  42 us (4%)
    pallas_call x4, Pallas kernels, comm_call(): pl.pallas_call(partial(comm_kernel, m, chain, kinds), out_shape=(out,) +...  215 us
    ppermute x28, waiting for transfers between devices, over_tok(): return lambda a: lax.ppermute(a, 'tok', pairs)  166 us
    pallas_call x1, Pallas kernels, gather_call(): pl.pallas_call(partial(gather_kernel, m), out_shape=tuple((jax.ShapeDtype...  140 us
    ppermute x4, waiting for transfers between devices, within_quad(): return lax.ppermute(a, 'tok', pairs)  61.3 us
    ppermute x28, starting transfers between devices, over_tok(): return lambda a: lax.ppermute(a, 'tok', pairs)  50.6 us
    dot_general x8, matrix products, contract_cols(): lax.dot_general(left, right, (((1,), (1,)), ((), ())), preferred_element_...  49.4 us
    dot_general x6, matrix products, contract_rows(): lax.dot_general(left, right, (((0,), (0,)), ((), ())), preferred_element_...  41.2 us
    pallas_call x1, Pallas kernels, attend_back_call(): pl.pallas_call(partial(attend_back_kernel, tile), grid=(heads, rows // ti...  22.1 us
  transfers between devices with their start and end apart: 45, of which 21 were waited for; matrix products, arithmetic and copies ran while one was open for 16% of the time, Pallas kernels for 2%

profile of v3, /device:TPU:0, one launch (start us, length us, event | category | flops | bytes accessed | tf_op | source)
XLA Modules:
  0.0 974.1 jit_solution(1587876646335418323)
XLA Ops:
  14.3 139.5 %gather_first.1 = (bf16[8,304,1536]{2,1,0:T(8,128)(2,1)}, bf16[8,288,2304]{2,1,0:T(8,128)(2,1)}, bf16[8,288,1152]{2,1,0:T(8,128)(2,1)}) custom-call(bf16[304,1536]{1,0:T(8,128)(2,1)} %fusion.37.attn_ref, bf16[288,2304]{1,0:T(8,128)(2,1)} %pad_maximum_fusion.7.guk_ref, bf16[288,2304]{1,0:T(8,128)(2,1)} %pad_maximum_fusion.8.gus_ref, ...), custom_call_target="tpu_custom_call" | custom-call | tf_op jit(solution)/shard_map/gather_first/pallas_call | solution.py:180
  200.9 14.6 %attend.1 = (bf16[768,512]{1,0:T(8,128)(2,1)S(1)}, f32[2,768,1]{2,1,0:T(8,128)S(1)}) custom-call(bf16[768,512]{1,0:T(8,128)(2,1)S(1)} %copy-done.17, bf16[768,512]{1,0:T(8,128)(2,1)} %collective-permute-done.k2_ref.v2_ref, bf16[768,512]{1,0:T(8,128)(2,1)} %collective-permute-done.1.k1_ref.v1_ref, bf16[768,512]{1,0:T(8,128)(2,1)} %get-tuple-element.69.k0_ref.v0_ref, ...), custom_call_target="tpu_custom_call" | custom-call | flops 20000000000 | tf_op jit(solution)/shard_map/attend/pallas_call | solution.py:552
  218.0 75.8 %reduce_tp.1 = (f32[192,2304]{1,0:T(8,128)S(1)}, bf16[288,2304]{1,0:T(8,128)(2,1)S(1)}, bf16[288,2304]{1,0:T(8,128)(2,1)S(1)}, bf16[288,2304]{1,0:T(8,128)(2,1)S(1)}) custom-call(bf16[384,2304]{1,0:T(8,128)(2,1)S(1)} %convolution_convert_fusion.8.refs_0_, f32[384,2304]{1,0:T(8,128)S(1)} %fusion.75.refs_1_, ...), custom_call_target="tpu_custom_call" | custom-call | tf_op jit(solution)/shard_map/reduce_tp/pallas_call | solution.py:428
  295.5 60.5 %gather_pair.2 = (bf16[8,192,2304]{2,1,0:T(8,128)(2,1)S(1)}, bf16[288,1152]{1,0:T(8,128)(2,1)S(1)}, bf16[288,1152]{1,0:T(8,128)(2,1)S(1)}, bf16[288,2304]{1,0:T(...) custom-call(bf16[192,2304]{1,0:T(8,128)(2,1)S(1)} %multiply_convert_fusion.3.refs_0_, ...), custom_call_target="tpu_custom_call" | custom-call | tf_op jit(solution)/shard_map/gather_pair/pallas_call | solution.py:428
  363.3 19.6 %fusion.76 = f32[1536,2304]{1,0:T(8,128)S(1)} fusion(bf16[1536,2304]{1,0:T(8,128)(2,1)S(1)} %bitcast.224, bf16[2304,2304]{1,0:T(8,128)(2,1)} %bitcast.266), kind=kOutput, calls=%fused_computation.240 | convolution fusion | flops 16307453952 | bytes 31850496 | tf_op jit(solution)/shard_map/dot_general | solution.py:808
  415.8 44.5 %reduce_pair.1 = f32[192,2304]{1,0:T(8,128)S(1)} custom-call(bf16[768,2304]{1,0:T(8,128)(2,1)S(1)} %convolution_convert_fusion.4.refs_0_, f32[768,2304]{1,0:T(8,128)S(1)} %fusion.31.refs_1_), custom_call_target="tpu_custom_call" | custom-call | tf_op jit(solution)/shard_map/reduce_pair/pallas_call | solution.py:428
  461.6 34.2 %gather_pair.3 = bf16[8,192,2304]{2,1,0:T(8,128)(2,1)S(1)} custom-call(bf16[192,2304]{1,0:T(8,128)(2,1)S(1)} %fusion.21.refs_0_), custom_call_target="tpu_custom_call" | custom-call | tf_op jit(solution)/shard_map/gather_pair/pallas_call | solution.py:428
  507.0 19.2 %fusion.6 = (bf16[1536,1152]{1,0:T(8,128)(2,1)}, bf16[1536,1152]{1,0:T(8,128)(2,1)}) fusion(f32[1536,2304]{1,0:T(8,128)} %copy-done.23, bf16[1536,2304]{1,0:T(8,128)(2,1)S(1)} %bitcast.217, bf16[2304,1152]{1,0:T(8,128)(2,1)} %bitcast.272), kind=kOutput, calls=%fused_computation.11 | convolution fusion | flops 8196194304 | bytes 33619968 | tf_op jit(solution)/shard_map/dot_general | solution.py:822
  531.8 11.3 %convolution_convert_fusion.1 = bf16[2304,1152]{1,0:T(8,128)(2,1)} fusion(bf16[1536,2304]{1,0:T(8,128)(2,1)S(1)} %bitcast.227, bf16[1536,1152]{1,0:T(8,128)(2,1)S(1)} %copy-done.53), kind=kOutput, calls=%fused_computation.1 | convolution fusion | flops 8156381184 | bytes 15925248 | tf_op jit(solution)/shard_map/dot_general | solution.py:56
  543.1 11.4 %convolution_convert_fusion.2 = bf16[2304,1152]{1,0:T(8,128)(2,1)} fusion(bf16[1536,2304]{1,0:T(8,128)(2,1)S(1)} %bitcast.228, bf16[1536,1152]{1,0:T(8,128)(2,1)S(1)} %copy-done.54), kind=kOutput, calls=%fused_computation.2 | convolution fusion | flops 8156381184 | bytes 15925248 | tf_op jit(solution)/shard_map/dot_general | solution.py:56
  556.7 14.6 %convolution_convert_fusion.3 = bf16[768,2304]{1,0:T(8,128)(2,1)} fusion(bf16[2304,2304]{1,0:T(8,128)(2,1)} %bitcast.267, bf16[1536,1152]{1,0:T(8,128)(2,1)} %get-tuple-element.137, bf16[1536,1152]{1,0:T(8,128)(2,1)} %get-tuple-element.136), kind=kOutput, calls=%fused_computation.22 | convolution fusion | flops 8162574336 | bytes 21233664 | tf_op jit(solution)/shard_map/dot_general | solution.py:62
  600.1 15.9 %convert_add_fusion = f32[768,2304]{1,0:T(8,128)} fusion(bf16[768,2304]{1,0:T(8,128)(2,1)} %collective-permute-done.6, bf16[2304,2304]{1,0:T(8,128)(2,1)} %bitcast.268, bf16[1536,1152]{1,0:T(8,128)(2,1)} %get-tuple-element.136, bf16[1536,1152]{1,0:T(8,128)(2,1)} %get-tuple-element.137), kind=kOutput, calls=%fused_computation.15 | convolution fusion | flops 8164343808 | bytes 28311552 | tf_op jit(solution)/shard_map/dot_general | solution.py:62
  621.4 27.1 %collective-permute-done.37 = bf16[4,288,1152]{2,1,0:T(8,128)(2,1)} collective-permute-done((bf16[4,288,1152]{2,1,0:T(8,128)(2,1)}, bf16[4,288,1152]{2,1,0:T(8,128)(2,1)}, u32[]{:S(2)}, u32[]{:S(2)}) %collective-permute-start.37) | collective-permute-done | bytes 2654240 | tf_op jit(solution)/shard_map/ppermute | solution.py:690
  657.1 13.7 %collective-permute-done.8 = bf16[2,192,1152]{2,1,0:T(8,128)(2,1)S(1)} collective-permute-done((bf16[2,192,1152]{2,1,0:T(8,128)(2,1)S(1)}, bf16[2,192,1152]{2,1,0:T(8,128)(2,1)S(1)}, u32[]{:S(2)}, u32[]{:S(2)}) %collective-permute-start.8) | collective-permute-done | bytes 884768 | tf_op jit(solution)/shard_map/ppermute | solution.py:690
  679.6 22.6 %collective-permute-done.9 = bf16[192,1152]{1,0:T(8,128)(2,1)S(1)} collective-permute-done((bf16[192,1152]{1,0:T(8,128)(2,1)S(1)}, bf16[192,1152]{1,0:T(8,128)(2,1)S(1)}, u32[]{:S(2)}, u32[]{:S(2)}) %collective-permute-start.9) | collective-permute-done | bytes 442400 | tf_op jit(solution)/shard_map/ppermute | solution.py:690
  709.4 21.2 %collective-permute-done.40 = bf16[2,288,1152]{2,1,0:T(8,128)(2,1)S(1)} collective-permute-done((bf16[2,288,1152]{2,1,0:T(8,128)(2,1)S(1)}, bf16[2,288,1152]{2,1,0:T(8,128)(2,1)S(1)}, u32[]{:S(2)}, u32[]{:S(2)}) %collective-permute-start.40) | collective-permute-done | bytes 1327136 | tf_op jit(solution)/shard_map/ppermute | solution.py:690
  733.2 15.4 %collective-permute-done.41 = bf16[288,1152]{1,0:T(8,128)(2,1)S(1)} collective-permute-done((bf16[288,1152]{1,0:T(8,128)(2,1)S(1)}, bf16[288,1152]{1,0:T(8,128)(2,1)S(1)}, u32[]{:S(2)}, u32[]{:S(2)}) %collective-permute-start.41) | collective-permute-done | bytes 663584 | tf_op jit(solution)/shard_map/ppermute | solution.py:690
  763.0 22.1 %attend_back.1 = (bf16[768,512]{1,0:T(8,128)(2,1)}, bf16[768,512]{1,0:T(8,128)(2,1)}, bf16[768,512]{1,0:T(8,128)(2,1)}, f32[768,512]{1,0:T(8,128)}) custom-call(bf16[768,512]{1,0:T(8,128)(2,1)} %copy-done.16, bf16[768,512]{1,0:T(8,128)(2,1)} %convolution_convert_fusion.9.do_ref, bf16[768,512]{1,0:T(8,128)(2,1)} %collective-permute-done.k2_ref.v2_ref, ...), custom_call_target="tpu_custom_call" | custom-call | flops 40000000000 | tf_op jit(solution)/shard_map/attend_back/pallas_call | solution.py:611
  794.1 13.6 %collective-permute-done.13 = bf16[768,512]{1,0:T(8,128)(2,1)S(1)} collective-permute-done((bf16[768,512]{1,0:T(8,128)(2,1)}, bf16[768,512]{1,0:T(8,128)(2,1)S(1)}, u32[]{:S(2)}, u32[]{:S(2)}) %collective-permute-start.13) | collective-permute-done | bytes 786464 | tf_op jit(solution)/shard_map/ppermute | solution.py:709
  807.6 44.1 %collective-permute-done.14 = bf16[768,512]{1,0:T(8,128)(2,1)S(1)} collective-permute-done((bf16[768,512]{1,0:T(8,128)(2,1)}, bf16[768,512]{1,0:T(8,128)(2,1)S(1)}, u32[]{:S(2)}, u32[]{:S(2)}) %collective-permute-start.14) | collective-permute-done | bytes 786464 | tf_op jit(solution)/shard_map/ppermute | solution.py:709
  871.6 11.7 %collective-permute-done.35 = bf16[288,512]{1,0:T(8,128)(2,1)S(1)} collective-permute-done((bf16[288,512]{1,0:T(8,128)(2,1)S(1)}, bf16[288,512]{1,0:T(8,128)(2,1)S(1)}, u32[]{:S(2)}, u32[]{:S(2)}) %collective-permute-start.35) | collective-permute-done | bytes 294944 | tf_op jit(solution)/shard_map/ppermute | solution.py:690
  890.9 14.1 %collective-permute-start.43 = (bf16[288,1152]{1,0:T(8,128)(2,1)S(1)}, bf16[288,1152]{1,0:T(8,128)(2,1)S(1)}, u32[]{:S(2)}, u32[]{:S(2)}) collective-permute-start(bf16[288,1152]{1,0:T(8,128)(2,1)S(1)} %fusion.47), channel_id=1, source_target_pairs={{0,8},{4,12},{8,0},{12,4},{16,24},{20,28},{24,16},{28,20},{1,9},{5... | collective-permute-start | bytes 1990664 | tf_op jit(solution)/shard_map/ppermute | solution.py:690
  919.2 12.9 %collective-permute-done.43 = bf16[288,1152]{1,0:T(8,128)(2,1)S(1)} collective-permute-done((bf16[288,1152]{1,0:T(8,128)(2,1)S(1)}, bf16[288,1152]{1,0:T(8,128)(2,1)S(1)}, u32[]{:S(2)}, u32[]{:S(2)}) %collective-permute-start.43) | collective-permute-done | bytes 663584 | tf_op jit(solution)/shard_map/ppermute | solution.py:690
  937.8 18.5 %collective-permute-done.17 = bf16[192,2304]{1,0:T(8,128)(2,1)S(1)} collective-permute-done((bf16[192,2304]{1,0:T(8,128)(2,1)S(1)}, bf16[192,2304]{1,0:T(8,128)(2,1)S(1)}, u32[]{:S(2)}, u32[]{:S(2)}) %collective-permute-start.17) | collective-permute-done | bytes 884768 | tf_op jit(solution)/shard_map/ppermute | solution.py:694
  (357 shorter events, 273.6 us)
Async XLA Ops:
  357.0 35.2 %collective-permute-start.2 = (bf16[288,1152]{1,0:T(8,128)(2,1)S(1)}, bf16[288,1152]{1,0:T(8,128)(2,1)S(1)}, u32[]{:S(2)}, u32[]{:S(2)}) collective-permute-start(bf16[288,1152]{1,0:T(8,128)(2,1)S(1)} %get-tuple-element.80), channel_id=1, source_target_pairs={{0,4},{4,0},{8,12},{12,8},{16,20},{20,16},{24,28},{28,24},{1,5},{5... | collective-permute-start | bytes 1990664 | tf_op jit(solution)/shard_map/ppermute | solution.py:690
  530.9 60.7 %collective-permute-start.38 = (bf16[4,288,1152]{2,1,0:T(8,128)(2,1)}, bf16[4,288,1152]{2,1,0:T(8,128)(2,1)}, u32[]{:S(2)}, u32[]{:S(2)}) collective-permute-start(bf16[4,288,1152]{2,1,0:T(8,128)(2,1)} %get-tuple-element.142), channel_id=1, source_target_pairs={{0,4},{4,0},{8,12},{12,8},{16,20},{20,16},{24,28},{28,24},{1,5},{5... | collective-permute-start | bytes 7962632 | tf_op jit(solution)/shard_map/ppermute | solution.py:690
  577.2 71.3 %collective-permute-start.37 = (bf16[4,288,1152]{2,1,0:T(8,128)(2,1)}, bf16[4,288,1152]{2,1,0:T(8,128)(2,1)}, u32[]{:S(2)}, u32[]{:S(2)}) collective-permute-start(bf16[4,288,1152]{2,1,0:T(8,128)(2,1)} %get-tuple-element.144), channel_id=1, source_target_pairs={{0,4},{4,0},{8,12},{12,8},{16,20},{20,16},{24,28},{28,24},{1,5},{5... | collective-permute-start | bytes 7962632 | tf_op jit(solution)/shard_map/ppermute | solution.py:690
  582.7 173.9 %collective-permute-start.32 = (bf16[4,288,1152]{2,1,0:T(8,128)(2,1)}, bf16[4,288,1152]{2,1,0:T(8,128)(2,1)}, u32[]{:S(2)}, u32[]{:S(2)}) collective-permute-start(bf16[4,288,1152]{2,1,0:T(8,128)(2,1)} %get-tuple-element.146), channel_id=1, source_target_pairs={{0,4},{4,0},{8,12},{12,8},{16,20},{20,16},{24,28},{28,24},{1,5},{5... | collective-permute-start | bytes 7962632 | tf_op jit(solution)/shard_map/ppermute | solution.py:690
  595.1 60.1 %collective-permute-start.39 = (bf16[2,288,1152]{2,1,0:T(8,128)(2,1)}, bf16[2,288,1152]{2,1,0:T(8,128)(2,1)}, u32[]{:S(2)}, u32[]{:S(2)}) collective-permute-start(bf16[2,288,1152]{2,1,0:T(8,128)(2,1)} %fusion.34), channel_id=1, source_target_pairs={{0,16},{4,20},{8,24},{12,28},{16,0},{20,4},{24,8},{28,12},{1,17},{... | collective-permute-start | bytes 3981320 | tf_op jit(solution)/shard_map/ppermute | solution.py:690
  617.6 39.5 %collective-permute-start.7 = (bf16[2,192,1152]{2,1,0:T(8,128)(2,1)S(1)}, bf16[2,192,1152]{2,1,0:T(8,128)(2,1)S(1)}, u32[]{:S(2)}, u32[]{:S(2)}) collective-permute-start(bf16[2,192,1152]{2,1,0:T(8,128)(2,1)S(1)} %slice_bitcast_fusion.5), channel_id=1, source_target_pairs={{0,2},{1,3},{2,0},{3,1},{4,6},{5,7},{6,4},{7,5},{8,10},{9,11},{10,... | collective-permute-start | bytes 2654216 | tf_op jit(solution)/shard_map/ppermute | solution.py:694
  620.2 50.6 %collective-permute-start.8 = (bf16[2,192,1152]{2,1,0:T(8,128)(2,1)S(1)}, bf16[2,192,1152]{2,1,0:T(8,128)(2,1)S(1)}, u32[]{:S(2)}, u32[]{:S(2)}) collective-permute-start(bf16[2,192,1152]{2,1,0:T(8,128)(2,1)S(1)} %slice_bitcast_fusion.4), channel_id=1, source_target_pairs={{0,8},{4,12},{8,0},{12,4},{16,24},{20,28},{24,16},{28,20},{1,9},{5... | collective-permute-start | bytes 2654216 | tf_op jit(solution)/shard_map/ppermute | solution.py:690
  656.9 52.4 %collective-permute-start.44 = (bf16[288,1152]{1,0:T(8,128)(2,1)S(1)}, bf16[288,1152]{1,0:T(8,128)(2,1)S(1)}, u32[]{:S(2)}, u32[]{:S(2)}) collective-permute-start(bf16[288,1152]{1,0:T(8,128)(2,1)S(1)} %fusion.48), channel_id=1, source_target_pairs={{0,8},{4,12},{8,0},{12,4},{16,24},{20,28},{24,16},{28,20},{1,9},{5... | collective-permute-start | bytes 1990664 | tf_op jit(solution)/shard_map/ppermute | solution.py:690
  672.3 29.9 %collective-permute-start.9 = (bf16[192,1152]{1,0:T(8,128)(2,1)S(1)}, bf16[192,1152]{1,0:T(8,128)(2,1)S(1)}, u32[]{:S(2)}, u32[]{:S(2)}) collective-permute-start(bf16[192,1152]{1,0:T(8,128)(2,1)S(1)} %fusion.55), channel_id=1, source_target_pairs={{0,8},{4,12},{8,0},{12,4},{16,24},{20,28},{24,16},{28,20},{1,9},{5... | collective-permute-start | bytes 1327112 | tf_op jit(solution)/shard_map/ppermute | solution.py:690
  675.0 55.5 %collective-permute-start.40 = (bf16[2,288,1152]{2,1,0:T(8,128)(2,1)S(1)}, bf16[2,288,1152]{2,1,0:T(8,128)(2,1)S(1)}, u32[]{:S(2)}, u32[]{:S(2)}) collective-permute-start(bf16[2,288,1152]{2,1,0:T(8,128)(2,1)S(1)} %fusion.35), channel_id=1, source_target_pairs={{0,16},{4,20},{8,24},{12,28},{16,0},{20,4},{24,8},{28,12},{1,17},{... | collective-permute-start | bytes 3981320 | tf_op jit(solution)/shard_map/ppermute | solution.py:690
  760.2 100.3 %collective-permute-start.42 = (bf16[2,288,1152]{2,1,0:T(8,128)(2,1)}, bf16[2,288,1152]{2,1,0:T(8,128)(2,1)S(1)}, u32[]{:S(2)}, u32[]{:S(2)}) collective-permute-start(bf16[2,288,1152]{2,1,0:T(8,128)(2,1)} %fusion.36), channel_id=1, source_target_pairs={{0,16},{4,20},{8,24},{12,28},{16,0},{20,4},{24,8},{28,12},{1,17},{... | collective-permute-start | bytes 3981320 | tf_op jit(solution)/shard_map/ppermute | solution.py:690
  762.0 96.1 %collective-permute-start.33 = (bf16[4,288,512]{2,1,0:T(8,128)(2,1)}, bf16[4,288,512]{2,1,0:T(8,128)(2,1)}, u32[]{:S(2)}, u32[]{:S(2)}) collective-permute-start(bf16[4,288,512]{2,1,0:T(8,128)(2,1)} %get-tuple-element.152), channel_id=1, source_target_pairs={{0,4},{4,0},{8,12},{12,8},{16,20},{20,16},{24,28},{28,24},{1,5},{5... | collective-permute-start | bytes 3538952 | tf_op jit(solution)/shard_map/ppermute | solution.py:690
  786.4 65.4 %collective-permute-start.14 = (bf16[768,512]{1,0:T(8,128)(2,1)}, bf16[768,512]{1,0:T(8,128)(2,1)S(1)}, u32[]{:S(2)}, u32[]{:S(2)}) collective-permute-start(bf16[768,512]{1,0:T(8,128)(2,1)} %get-tuple-element.92), channel_id=1, source_target_pairs={{8,0},{12,4},{24,16},{28,20},{9,1},{13,5},{25,17},{29,21},{10,2},{... | collective-permute-start | bytes 2359304 | tf_op jit(solution)/shard_map/ppermute | solution.py:709
  791.2 68.7 %collective-permute-start.24 = (bf16[4,288,512]{2,1,0:T(8,128)(2,1)S(1)}, bf16[4,288,512]{2,1,0:T(8,128)(2,1)S(1)}, u32[]{:S(2)}, u32[]{:S(2)}) collective-permute-start(bf16[4,288,512]{2,1,0:T(8,128)(2,1)S(1)} %get-tuple-element.162), channel_id=1, source_target_pairs={{0,4},{4,0},{8,12},{12,8},{16,20},{20,16},{24,28},{28,24},{1,5},{5... | collective-permute-start | bytes 3538952 | tf_op jit(solution)/shard_map/ppermute | solution.py:690
  855.7 54.0 %collective-permute-start.28 = (bf16[4,288,512]{2,1,0:T(8,128)(2,1)S(1)}, bf16[4,288,512]{2,1,0:T(8,128)(2,1)S(1)}, u32[]{:S(2)}, u32[]{:S(2)}) collective-permute-start(bf16[4,288,512]{2,1,0:T(8,128)(2,1)S(1)} %get-tuple-element.157), channel_id=1, source_target_pairs={{0,4},{4,0},{8,12},{12,8},{16,20},{20,16},{24,28},{28,24},{1,5},{5... | collective-permute-start | bytes 3538952 | tf_op jit(solution)/shard_map/ppermute | solution.py:690
  860.5 28.4 %collective-permute-start.36 = (bf16[288,512]{1,0:T(8,128)(2,1)S(1)}, bf16[288,512]{1,0:T(8,128)(2,1)S(1)}, u32[]{:S(2)}, u32[]{:S(2)}) collective-permute-start(bf16[288,512]{1,0:T(8,128)(2,1)S(1)} %get-tuple-element.150), channel_id=1, source_target_pairs={{0,24},{4,28},{8,0},{12,4},{16,8},{20,12},{24,16},{28,20},{1,25},{... | collective-permute-start | bytes 884744 | tf_op jit(solution)/shard_map/ppermute | solution.py:690
  864.8 26.0 %collective-permute-start.25 = (bf16[288,512]{1,0:T(8,128)(2,1)S(1)}, bf16[288,512]{1,0:T(8,128)(2,1)S(1)}, u32[]{:S(2)}, u32[]{:S(2)}) collective-permute-start(bf16[288,512]{1,0:T(8,128)(2,1)S(1)} %get-tuple-element.159), channel_id=1, source_target_pairs={{0,8},{4,12},{8,16},{12,20},{16,24},{20,28},{24,0},{28,4},{1,9},{5... | collective-permute-start | bytes 884744 | tf_op jit(solution)/shard_map/ppermute | solution.py:690
  871.6 37.1 %collective-permute-start.26 = (bf16[288,512]{1,0:T(8,128)(2,1)S(1)}, bf16[288,512]{1,0:T(8,128)(2,1)S(1)}, u32[]{:S(2)}, u32[]{:S(2)}) collective-permute-start(bf16[288,512]{1,0:T(8,128)(2,1)S(1)} %get-tuple-element.161), channel_id=1, source_target_pairs={{0,16},{4,20},{8,24},{12,28},{16,0},{20,4},{24,8},{28,12},{1,17},{... | collective-permute-start | bytes 884744 | tf_op jit(solution)/shard_map/ppermute | solution.py:690
  883.4 25.3 %collective-permute-start.27 = (bf16[288,512]{1,0:T(8,128)(2,1)S(1)}, bf16[288,512]{1,0:T(8,128)(2,1)S(1)}, u32[]{:S(2)}, u32[]{:S(2)}) collective-permute-start(bf16[288,512]{1,0:T(8,128)(2,1)S(1)} %get-tuple-element.160), channel_id=1, source_target_pairs={{0,24},{4,28},{8,0},{12,4},{16,8},{20,12},{24,16},{28,20},{1,25},{... | collective-permute-start | bytes 884744 | tf_op jit(solution)/shard_map/ppermute | solution.py:690
  888.9 43.3 %collective-permute-start.16 = (bf16[192,2304]{1,0:T(8,128)(2,1)S(1)}, bf16[192,2304]{1,0:T(8,128)(2,1)S(1)}, u32[]{:S(2)}, u32[]{:S(2)}) collective-permute-start(bf16[192,2304]{1,0:T(8,128)(2,1)S(1)} %fusion.38), channel_id=1, source_target_pairs={{0,2},{1,3},{2,0},{3,1},{4,6},{5,7},{6,4},{7,5},{8,10},{9,11},{10,... | collective-permute-start | bytes 2654216 | tf_op jit(solution)/shard_map/ppermute | solution.py:694
  890.9 41.2 %collective-permute-start.43 = (bf16[288,1152]{1,0:T(8,128)(2,1)S(1)}, bf16[288,1152]{1,0:T(8,128)(2,1)S(1)}, u32[]{:S(2)}, u32[]{:S(2)}) collective-permute-start(bf16[288,1152]{1,0:T(8,128)(2,1)S(1)} %fusion.47), channel_id=1, source_target_pairs={{0,8},{4,12},{8,0},{12,4},{16,24},{20,28},{24,16},{28,20},{1,9},{5... | collective-permute-start | bytes 1990664 | tf_op jit(solution)/shard_map/ppermute | solution.py:690
  910.2 48.7 %collective-permute-start.29 = (bf16[288,512]{1,0:T(8,128)(2,1)S(1)}, bf16[288,512]{1,0:T(8,128)(2,1)S(1)}, u32[]{:S(2)}, u32[]{:S(2)}) collective-permute-start(bf16[288,512]{1,0:T(8,128)(2,1)S(1)} %get-tuple-element.154), channel_id=1, source_target_pairs={{0,8},{4,12},{8,16},{12,20},{16,24},{20,28},{24,0},{28,4},{1,9},{5... | collective-permute-start | bytes 884744 | tf_op jit(solution)/shard_map/ppermute | solution.py:690
  916.7 42.1 %collective-permute-start.30 = (bf16[288,512]{1,0:T(8,128)(2,1)S(1)}, bf16[288,512]{1,0:T(8,128)(2,1)S(1)}, u32[]{:S(2)}, u32[]{:S(2)}) collective-permute-start(bf16[288,512]{1,0:T(8,128)(2,1)S(1)} %get-tuple-element.156), channel_id=1, source_target_pairs={{0,16},{4,20},{8,24},{12,28},{16,0},{20,4},{24,8},{28,12},{1,17},{... | collective-permute-start | bytes 884744 | tf_op jit(solution)/shard_map/ppermute | solution.py:690
  916.7 42.1 %collective-permute-start.31 = (bf16[288,512]{1,0:T(8,128)(2,1)S(1)}, bf16[288,512]{1,0:T(8,128)(2,1)S(1)}, u32[]{:S(2)}, u32[]{:S(2)}) collective-permute-start(bf16[288,512]{1,0:T(8,128)(2,1)S(1)} %get-tuple-element.155), channel_id=1, source_target_pairs={{0,24},{4,28},{8,0},{12,4},{16,8},{20,12},{24,16},{28,20},{1,25},{... | collective-permute-start | bytes 884744 | tf_op jit(solution)/shard_map/ppermute | solution.py:690
  (82 other events, 1343.7 us)

commit v4 on v3

--- a/solution.py
+++ b/solution.py
@@ -463,7 +463,7 @@
         hidden_ref[...] = (values * inverse * gain_ref[...]).astype(bf16)
 
     product = jnp.dot(
-        hidden_ref[...], w_ref[...], preferred_element_type=f32
+        hidden_ref[...], w_ref[...].reshape(-1, HEAD_DIM), preferred_element_type=f32
     )
 
     @pl.when(which < heads)
@@ -481,6 +481,7 @@
 
 def qkv_call(inputs, gain, mat, cosine, sine_tab, heads, kv_heads):
     rows, width = inputs.shape
+    n = mat.shape[0]
     whole = lambda a: pl.BlockSpec(a.shape, lambda j: (0, 0))
     return pl.pallas_call(
         partial(qkv_kernel, heads, kv_heads),
@@ -493,7 +494,7 @@
         in_specs=[
             whole(inputs),
             whole(gain),
-            pl.BlockSpec((width, HEAD_DIM), lambda j: (0, j)),
+            pl.BlockSpec((n, width // n, HEAD_DIM), lambda j: (0, 0, j)),
             whole(cosine),
             whole(sine_tab),
         ],
@@ -765,7 +766,13 @@
     qkv_mat = attn_buf[:, :wrows, :qkv_cols].reshape(width, qkv_cols)
     out_mat = attn_buf[:, :wrows, qkv_cols:].reshape(width, head_cols)
     hidden_one, query, key_value = qkv_call(
-        inputs, gain_one, qkv_mat, cosine, sine_tab, heads, kv_heads
+        inputs,
+        gain_one,
+        attn_buf if wrows % 16 == 0 else qkv_mat[None],
+        cosine,
+        sine_tab,
+        heads,
+        kv_heads,
     )
     window = [within_quad(key_value, by) for by in range(REACH, 0, -1)] + [key_value]
     attended, lse = attend_call(query, window, low, heads, kv_heads)
@@ -856,21 +863,13 @@
     far, near = (contract_cols(jnp.split(grad_gu, 2)[k], gu_mat) for k in (1, 0))
     near = near + to_core(far.astype(bf16)).astype(f32)
     near = near.reshape(2, 2, part, width)
-    mid = width // 2
-    left, right = near[..., :mid], near[..., mid:]
-    left_in, right_in = to_x(left[1].astype(bf16)), to_zlo(right[:, 1].astype(bf16))
+    ahead_in, own_in = to_x(near[1, 1].astype(bf16)), to_x(near[1, 0].astype(bf16))
     gate_s = y_send(contract_rows(hidden_two, grad_gatevals))
     up_s = y_send(contract_rows(hidden_two, grad_upvals))
-    left_in, right_in = step(left_in, right_in)
-    left = left[0] + left_in.astype(f32)
-    right = right[:, 0] + right_in.astype(f32)
-    left_in, right_in = to_zlo(left[1].astype(bf16)), to_x(right[1].astype(bf16))
-    down_s = step(down_s)
-    left_in, right_in = step(left_in, right_in)
-    d_hidden_two = jnp.concatenate(
-        [left[0] + left_in.astype(f32), right[0] + right_in.astype(f32)], axis=1
-    )
+    z_in = to_zlo((near[0, 1] + ahead_in.astype(f32)).astype(bf16))
+    d_hidden_two = near[0, 0] + own_in.astype(f32) + z_in.astype(f32)
     down_s = zhi_send(down_s)
+    gate_s[1:] = tie(gate_s[1:], z_in)
 
     mid_add, grad_three = norm_back(d_hidden_two, gain_three, unit_three, inv_three)
     d_mid = grad_out + mid_add
@@ -901,7 +900,7 @@
     d_hidden_one = reduce_tp(lambda c: contract_cols(core_rows(d_qkv, c), qkv_mat))
     unit_one, inv_one = norm_parts(resid)
     input_add, grad_one = norm_back(d_hidden_one, gain_one, unit_one, inv_one)
-    gate_s = step(gate_s)
+    gate_s[1:] = tie(gate_s[1:], d_window)
     out_gate = sides(*zlo_send(gate_s))
     wout_s = z_send(step(wout_s))
     up_s = step(up_s)
@@ -909,11 +908,11 @@
     q_s = z_send(step(q_s))
     kv_s = z_send(step(kv_s))
     out_wout, out_q, out_kv = add_up(wout_s), add_up(q_s), add_up(kv_s)
-    input_grad = gather_tp(d_mid + input_add)
-
     gain_grads = jnp.stack([grad_one, grad_two, grad_three, grad_four])
     gain_grads = gain_grads + to_core(gain_grads)
     gain_grads = gain_grads + to_x(gain_grads)
+    input_grad = gather_tp(tie(d_mid + input_add, gain_grads))
+
     bit = 1
     while bit < n:
         gain_grads = gain_grads + over_tok(lambda t: t ^ bit)(gain_grads)

time: 980 us -> 967 us (0.987)
  waiting for transfers between devices: 249 us -> 146 us
  starting transfers between devices: 67.6 us -> 132 us
  other arithmetic: 42 us -> 61.5 us
    ppermute x28 -> x27, waiting for transfers between devices: 166 us -> 67.7 us  [over_tok(): return lambda a: lax.ppermute(a, 'tok', pairs)]
    ppermute x28 -> x27, starting transfers between devices: 50.6 us -> 116 us  [over_tok(): return lambda a: lax.ppermute(a, 'tok', pairs)]
    ppermute x4, waiting for transfers between devices: 61.3 us -> 24.9 us  [within_quad(): return lax.ppermute(a, 'tok', pairs)]
    ppermute x13, waiting for transfers between devices: 22 us -> 53.2 us  [over_tp(): return lambda a: lax.ppermute(a, 'tp', pairs)]
    unnamed x122 -> x176, local copies, waits for them, and re-layouts: 19.8 us -> 27.2 us
  transfers between devices with their start and end apart: 45 -> 44, of which waited for: 21 -> 20; matrix products, arithmetic and copies ran while one was open for 16% -> 19% of each run, Pallas kernels for 2% -> 2%
where the time goes in v4:
time: 967 us; the launch traced here: 961 us
  Pallas kernels  398 us (41%)
  waiting for transfers between devices  146 us (15%)
  starting transfers between devices  132 us (14%)
  matrix products  132 us (14%)
  local copies, waits for them, and re-layouts  89.7 us (9%)
  other arithmetic  61.5 us (6%)
    pallas_call x4, Pallas kernels, comm_call(): pl.pallas_call(partial(comm_kernel, m, chain, kinds), out_shape=(out,) +...  214 us
    pallas_call x1, Pallas kernels, gather_call(): pl.pallas_call(partial(gather_kernel, m), out_shape=tuple((jax.ShapeDtype...  140 us
    ppermute x27, starting transfers between devices, over_tok(): return lambda a: lax.ppermute(a, 'tok', pairs)  116 us
    ppermute x27, waiting for transfers between devices, over_tok(): return lambda a: lax.ppermute(a, 'tok', pairs)  67.7 us
    ppermute x13, waiting for transfers between devices, over_tp(): return lambda a: lax.ppermute(a, 'tp', pairs)  53.2 us
    dot_general x8, matrix products, contract_cols(): lax.dot_general(left, right, (((1,), (1,)), ((), ())), preferred_element_...  49.4 us
    dot_general x6, matrix products, contract_rows(): lax.dot_general(left, right, (((0,), (0,)), ((), ())), preferred_element_...  39.1 us
    unnamed x176, local copies, waits for them, and re-layouts  27.2 us
  transfers between devices with their start and end apart: 44, of which 20 were waited for; matrix products, arithmetic and copies ran while one was open for 19% of the time, Pallas kernels for 2%

profile of v4, /device:TPU:0, one launch (start us, length us, event | category | flops | bytes accessed | tf_op | source)
XLA Modules:
  0.0 961.3 jit_solution(17489660114269252736)
XLA Ops:
  14.3 139.5 %gather_first.1 = (bf16[8,304,1536]{2,1,0:T(8,128)(2,1)}, bf16[8,288,2304]{2,1,0:T(8,128)(2,1)}, bf16[8,288,1152]{2,1,0:T(8,128)(2,1)}) custom-call(bf16[304,1536]{1,0:T(8,128)(2,1)} %fusion.39.attn_ref, bf16[288,2304]{1,0:T(8,128)(2,1)} %pad_maximum_fusion.6.guk_ref, bf16[288,2304]{1,0:T(8,128)(2,1)} %pad_maximum_fusion.7.gus_ref, ...), custom_call_target="tpu_custom_call" | custom-call | tf_op jit(solution)/shard_map/gather_first/pallas_call | solution.py:180
  161.1 8.4 qkv.1
  195.4 14.8 %attend.1 = (bf16[768,512]{1,0:T(8,128)(2,1)S(1)}, f32[2,768,1]{2,1,0:T(8,128)S(1)}) custom-call(bf16[768,512]{1,0:T(8,128)(2,1)S(1)} %copy-done.16, bf16[768,512]{1,0:T(8,128)(2,1)} %collective-permute-done.k2_ref.v2_ref, bf16[768,512]{1,0:T(8,128)(2,1)} %collective-permute-done.1.k1_ref.v1_ref, bf16[768,512]{1,0:T(8,128)(2,1)} %get-tuple-element.61.k0_ref.v0_ref, ...), custom_call_target="tpu_custom_call" | custom-call | flops 20000000000 | tf_op jit(solution)/shard_map/attend/pallas_call | solution.py:553
  213.4 74.5 %reduce_tp.1 = (f32[192,2304]{1,0:T(8,128)S(1)}, bf16[288,2304]{1,0:T(8,128)(2,1)S(1)}, bf16[288,2304]{1,0:T(8,128)(2,1)S(1)}, bf16[288,2304]{1,0:T(8,128)(2,1)S(1)}) custom-call(bf16[384,2304]{1,0:T(8,128)(2,1)S(1)} %convolution_convert_fusion.8.refs_0_, f32[384,2304]{1,0:T(8,128)S(1)} %fusion.71.refs_1_, ...), custom_call_target="tpu_custom_call" | custom-call | tf_op jit(solution)/shard_map/reduce_tp/pallas_call | solution.py:428
  289.6 60.5 %gather_pair.2 = (bf16[8,192,2304]{2,1,0:T(8,128)(2,1)S(1)}, bf16[288,1152]{1,0:T(8,128)(2,1)S(1)}, bf16[288,1152]{1,0:T(8,128)(2,1)S(1)}, bf16[288,2304]{1,0:T(...) custom-call(bf16[192,2304]{1,0:T(8,128)(2,1)S(1)} %multiply_convert_fusion.3.refs_0_, ...), custom_call_target="tpu_custom_call" | custom-call | tf_op jit(solution)/shard_map/gather_pair/pallas_call | solution.py:428
  357.3 19.6 %fusion.72 = f32[1536,2304]{1,0:T(8,128)S(1)} fusion(bf16[1536,2304]{1,0:T(8,128)(2,1)S(1)} %bitcast.225, bf16[2304,2304]{1,0:T(8,128)(2,1)} %bitcast.276), kind=kOutput, calls=%fused_computation.229 | convolution fusion | flops 16307453952 | bytes 31850496 | tf_op jit(solution)/shard_map/dot_general | solution.py:815
  387.2 9.2 collective-permute-done.3
  409.9 44.4 %reduce_pair.1 = f32[192,2304]{1,0:T(8,128)S(1)} custom-call(bf16[768,2304]{1,0:T(8,128)(2,1)S(1)} %convolution_convert_fusion.4.refs_0_, f32[768,2304]{1,0:T(8,128)S(1)} %fusion.33.refs_1_), custom_call_target="tpu_custom_call" | custom-call | tf_op jit(solution)/shard_map/reduce_pair/pallas_call | solution.py:428
  455.6 34.2 %gather_pair.3 = bf16[8,192,2304]{2,1,0:T(8,128)(2,1)S(1)} custom-call(bf16[192,2304]{1,0:T(8,128)(2,1)S(1)} %fusion.21.refs_0_), custom_call_target="tpu_custom_call" | custom-call | tf_op jit(solution)/shard_map/gather_pair/pallas_call | solution.py:428
  489.9 9.7 %convolution_convert_fusion = bf16[2304,1152]{1,0:T(8,128)(2,1)S(1)} fusion(bf16[1536,2304]{1,0:T(8,128)(2,1)S(1)} %bitcast.222, bf16[1536,1152]{1,0:T(8,128)(2,1)S(1)} %copy-done.47), kind=kOutput, calls=%fused_computation | convolution fusion | flops 8156381184 | bytes 15925248 | tf_op jit(solution)/shard_map/dot_general | solution.py:56
  499.7 20.8 %fusion.6 = (bf16[1536,1152]{1,0:T(8,128)(2,1)}, bf16[1536,1152]{1,0:T(8,128)(2,1)}) fusion(f32[1536,2304]{1,0:T(8,128)} %copy-done.27, bf16[1536,2304]{1,0:T(8,128)(2,1)S(1)} %bitcast.223, bf16[2304,1152]{1,0:T(8,128)(2,1)} %bitcast.282), kind=kOutput, calls=%fused_computation.11 | convolution fusion | flops 8196194304 | bytes 33619968 | tf_op jit(solution)/shard_map/dot_general | solution.py:829
  523.4 13.4 %convolution_convert_fusion.1 = bf16[2304,1152]{1,0:T(8,128)(2,1)} fusion(bf16[1536,2304]{1,0:T(8,128)(2,1)} %bitcast.226, bf16[1536,1152]{1,0:T(8,128)(2,1)S(1)} %copy-done.76), kind=kOutput, calls=%fused_computation.1 | convolution fusion | flops 8156381184 | bytes 15925248 | tf_op jit(solution)/shard_map/dot_general | solution.py:56
  536.8 14.9 %convolution_convert_fusion.3 = bf16[768,2304]{1,0:T(8,128)(2,1)} fusion(bf16[2304,2304]{1,0:T(8,128)(2,1)} %bitcast.277, bf16[1536,1152]{1,0:T(8,128)(2,1)} %get-tuple-element.119, bf16[1536,1152]{1,0:T(8,128)(2,1)} %get-tuple-element.118), kind=kOutput, calls=%fused_computation.21 | convolution fusion | flops 8162574336 | bytes 21233664 | tf_op jit(solution)/shard_map/dot_general | solution.py:62
  556.6 9.9 %convolution_convert_fusion.2 = bf16[2304,1152]{1,0:T(8,128)(2,1)S(1)} fusion(bf16[1536,2304]{1,0:T(8,128)(2,1)S(1)} %bitcast.229, bf16[1536,1152]{1,0:T(8,128)(2,1)S(1)} %copy-done.77), kind=kOutput, calls=%fused_computation.2 | convolution fusion | flops 8156381184 | bytes 15925248 | tf_op jit(solution)/shard_map/dot_general | solution.py:56
  592.0 15.7 %convert_add_fusion = f32[768,2304]{1,0:T(8,128)} fusion(bf16[768,2304]{1,0:T(8,128)(2,1)} %collective-permute-done.6, bf16[2304,2304]{1,0:T(8,128)(2,1)} %bitcast.278, bf16[1536,1152]{1,0:T(8,128)(2,1)} %get-tuple-element.118, bf16[1536,1152]{1,0:T(8,128)(2,1)} %get-tuple-element.119), kind=kOutput, calls=%fused_computation.14 | convolution fusion | flops 8164343808 | bytes 28311552 | tf_op jit(solution)/shard_map/dot_general | solution.py:62
  617.3 17.5 %collective-permute-done.8 = bf16[192,2304]{1,0:T(8,128)(2,1)S(1)} collective-permute-done((bf16[192,2304]{1,0:T(8,128)(2,1)S(1)}, bf16[192,2304]{1,0:T(8,128)(2,1)S(1)}, u32[]{:S(2)}, u32[]{:S(2)}) %collective-permute-start.8) | collective-permute-done | bytes 884768 | tf_op jit(solution)/shard_map/ppermute | solution.py:695
  640.4 27.4 %collective-permute-done.9.refs_1_ = bf16[192,2304]{1,0:T(8,128)(2,1)S(1)} collective-permute-done((bf16[192,2304]{1,0:T(8,128)(2,1)S(1)}, bf16[192,2304]{1,0:T(8,128)(2,1)S(1)}, u32[]{:S(2)}, u32[]{:S(2)}) %collective-permute-start.9) | collective-permute-done | bytes 884768 | tf_op jit(solution)/shard_map/ppermute | solution.py:691
  679.4 18.7 %collective-permute-done.10 = bf16[192,2304]{1,0:T(8,128)(2,1)S(1)} collective-permute-done((bf16[192,2304]{1,0:T(8,128)(2,1)S(1)}, bf16[192,2304]{1,0:T(8,128)(2,1)S(1)}, u32[]{:S(2)}, u32[]{:S(2)}) %collective-permute-start.10) | collective-permute-done | bytes 884768 | tf_op jit(solution)/shard_map/ppermute | solution.py:695
  719.0 22.0 %attend_back.1 = (bf16[768,512]{1,0:T(8,128)(2,1)}, bf16[768,512]{1,0:T(8,128)(2,1)}, bf16[768,512]{1,0:T(8,128)(2,1)}, f32[768,512]{1,0:T(8,128)}) custom-call(bf16[768,512]{1,0:T(8,128)(2,1)} %copy-done.15, bf16[768,512]{1,0:T(8,128)(2,1)} %convolution_convert_fusion.9.do_ref, bf16[768,512]{1,0:T(8,128)(2,1)} %collective-permute-done.k2_ref.v2_ref, ...), custom_call_target="tpu_custom_call" | custom-call | flops 40000000000 | tf_op jit(solution)/shard_map/attend_back/pallas_call | solution.py:612
  753.5 10.3 %collective-permute-done.12.refs_1_ = bf16[768,512]{1,0:T(8,128)(2,1)S(1)} collective-permute-done((bf16[768,512]{1,0:T(8,128)(2,1)}, bf16[768,512]{1,0:T(8,128)(2,1)S(1)}, u32[]{:S(2)}, u32[]{:S(2)}) %collective-permute-start.12) | collective-permute-done | bytes 786464 | tf_op jit(solution)/shard_map/ppermute | solution.py:710
  763.8 58.1 %collective-permute-start.23 = (bf16[4,288,512]{2,1,0:T(8,128)(2,1)}, bf16[4,288,512]{2,1,0:T(8,128)(2,1)}, u32[]{:S(2)}, u32[]{:S(2)}) collective-permute-start(bf16[4,288,512]{2,1,0:T(8,128)(2,1)} %get-tuple-element.142), channel_id=1, source_target_pairs={{0,4},{4,0},{8,12},{12,8},{16,20},{20,16},{24,28},{28,24},{1,5},{5... | collective-permute-start | bytes 3538952 | tf_op jit(solution)/shard_map/ppermute | solution.py:691
  821.9 14.6 %collective-permute-done.13.refs_2_ = bf16[768,512]{1,0:T(8,128)(2,1)S(1)} collective-permute-done((bf16[768,512]{1,0:T(8,128)(2,1)}, bf16[768,512]{1,0:T(8,128)(2,1)S(1)}, u32[]{:S(2)}, u32[]{:S(2)}) %collective-permute-start.13) | collective-permute-done | bytes 786464 | tf_op jit(solution)/shard_map/ppermute | solution.py:710
  888.9 9.1 collective-permute-start.42
  913.4 10.7 %collective-permute-start.28 = (bf16[288,512]{1,0:T(8,128)(2,1)S(1)}, bf16[288,512]{1,0:T(8,128)(2,1)S(1)}, u32[]{:S(2)}, u32[]{:S(2)}) collective-permute-start(bf16[288,512]{1,0:T(8,128)(2,1)S(1)} %get-tuple-element.134), channel_id=1, source_target_pairs={{0,8},{4,12},{8,16},{12,20},{16,24},{20,28},{24,0},{28,4},{1,9},{5... | collective-permute-start | bytes 884744 | tf_op jit(solution)/shard_map/ppermute | solution.py:691
  (411 shorter events, 280.7 us)
Async XLA Ops:
  172.1 23.2 %collective-permute-start = (bf16[768,512]{1,0:T(8,128)(2,1)}, bf16[768,512]{1,0:T(8,128)(2,1)}, u32[]{:S(2)}, u32[]{:S(2)}) collective-permute-start(bf16[768,512]{1,0:T(8,128)(2,1)} %get-tuple-element.61.k0_ref.v0_ref), channel_id=1, source_target_pairs={{0,8},{4,12},{16,24},{20,28},{1,9},{5,13},{17,25},{21,29},{2,10},{... | collective-permute-start | bytes 2359304 | tf_op jit(solution)/shard_map/ppermute | solution.py:710
  351.1 35.2 %collective-permute-start.2 = (bf16[288,1152]{1,0:T(8,128)(2,1)S(1)}, bf16[288,1152]{1,0:T(8,128)(2,1)S(1)}, u32[]{:S(2)}, u32[]{:S(2)}) collective-permute-start(bf16[288,1152]{1,0:T(8,128)(2,1)S(1)} %get-tuple-element.72), channel_id=1, source_target_pairs={{0,4},{4,0},{8,12},{12,8},{16,20},{20,16},{24,28},{28,24},{1,5},{5... | collective-permute-start | bytes 1990664 | tf_op jit(solution)/shard_map/ppermute | solution.py:691
  522.2 60.7 %collective-permute-start.37 = (bf16[4,288,1152]{2,1,0:T(8,128)(2,1)}, bf16[4,288,1152]{2,1,0:T(8,128)(2,1)}, u32[]{:S(2)}, u32[]{:S(2)}) collective-permute-start(bf16[4,288,1152]{2,1,0:T(8,128)(2,1)} %dynamic-slice_bitcast_fusion.2), channel_id=1, source_target_pairs={{0,4},{4,0},{8,12},{12,8},{16,20},{20,16},{24,28},{28,24},{1,5},{5... | collective-permute-start | bytes 7962632 | tf_op jit(solution)/shard_map/ppermute | solution.py:691
  551.8 40.2 %collective-permute-start.6 = (bf16[768,2304]{1,0:T(8,128)(2,1)}, bf16[768,2304]{1,0:T(8,128)(2,1)}, u32[]{:S(2)}, u32[]{:S(2)}) collective-permute-start(bf16[768,2304]{1,0:T(8,128)(2,1)} %convolution_convert_fusion.3), channel_id=1, source_target_pairs={{0,1},{1,0},{2,3},{3,2},{4,5},{5,4},{6,7},{7,6},{8,9},{9,8},{10,11... | collective-permute-start | bytes 10616840 | tf_op jit(solution)/shard_map/ppermute | solution.py:695
  568.4 72.0 %collective-permute-start.36 = (bf16[4,288,1152]{2,1,0:T(8,128)(2,1)S(1)}, bf16[4,288,1152]{2,1,0:T(8,128)(2,1)}, u32[]{:S(2)}, u32[]{:S(2)}) collective-permute-start(bf16[4,288,1152]{2,1,0:T(8,128)(2,1)S(1)} %get-tuple-element.122), channel_id=1, source_target_pairs={{0,4},{4,0},{8,12},{12,8},{16,20},{20,16},{24,28},{28,24},{1,5},{5... | collective-permute-start | bytes 7962632 | tf_op jit(solution)/shard_map/ppermute | solution.py:691
  572.3 139.2 %collective-permute-start.31 = (bf16[4,288,1152]{2,1,0:T(8,128)(2,1)}, bf16[4,288,1152]{2,1,0:T(8,128)(2,1)}, u32[]{:S(2)}, u32[]{:S(2)}) collective-permute-start(bf16[4,288,1152]{2,1,0:T(8,128)(2,1)} %get-tuple-element.124), channel_id=1, source_target_pairs={{0,4},{4,0},{8,12},{12,8},{16,20},{20,16},{24,28},{28,24},{1,5},{5... | collective-permute-start | bytes 7962632 | tf_op jit(solution)/shard_map/ppermute | solution.py:691
  578.8 35.8 %collective-permute-start.5 = (bf16[2,192,2304]{2,1,0:T(8,128)(2,1)}, bf16[2,192,2304]{2,1,0:T(8,128)(2,1)}, u32[]{:S(2)}, u32[]{:S(2)}) collective-permute-start(bf16[2,192,2304]{2,1,0:T(8,128)(2,1)} %pad_maximum_fusion.2), channel_id=1, source_target_pairs={{0,1},{1,0},{2,3},{3,2},{4,5},{5,4},{6,7},{7,6},{8,9},{9,8},{10,11... | collective-permute-start | bytes 5308424 | tf_op jit(solution)/shard_map/ppermute | solution.py:695
  588.9 80.0 %collective-permute-start.38 = (bf16[2,288,1152]{2,1,0:T(8,128)(2,1)}, bf16[2,288,1152]{2,1,0:T(8,128)(2,1)}, u32[]{:S(2)}, u32[]{:S(2)}) collective-permute-start(bf16[2,288,1152]{2,1,0:T(8,128)(2,1)} %fusion.36), channel_id=1, source_target_pairs={{0,16},{4,20},{8,24},{12,28},{16,0},{20,4},{24,8},{28,12},{1,17},{... | collective-permute-start | bytes 3981320 | tf_op jit(solution)/shard_map/ppermute | solution.py:691
  615.9 52.9 %collective-permute-start.7 = (bf16[192,2304]{1,0:T(8,128)(2,1)}, bf16[192,2304]{1,0:T(8,128)(2,1)}, u32[]{:S(2)}, u32[]{:S(2)}) collective-permute-start(bf16[192,2304]{1,0:T(8,128)(2,1)} %get-tuple-element.127), channel_id=1, source_target_pairs={{0,2},{1,3},{2,0},{3,1},{4,6},{5,7},{6,4},{7,5},{8,10},{9,11},{10,... | collective-permute-start | bytes 2654216 | tf_op jit(solution)/shard_map/ppermute | solution.py:695
  636.4 31.4 %collective-permute-start.9 = (bf16[192,2304]{1,0:T(8,128)(2,1)S(1)}, bf16[192,2304]{1,0:T(8,128)(2,1)S(1)}, u32[]{:S(2)}, u32[]{:S(2)}) collective-permute-start(bf16[192,2304]{1,0:T(8,128)(2,1)S(1)} %fusion.30), channel_id=1, source_target_pairs={{0,8},{4,12},{8,0},{12,4},{16,24},{20,28},{24,16},{28,20},{1,9},{5... | collective-permute-start | bytes 2654216 | tf_op jit(solution)/shard_map/ppermute | solution.py:691
  679.3 24.2 %collective-permute-start.43 = (bf16[288,1152]{1,0:T(8,128)(2,1)S(1)}, bf16[288,1152]{1,0:T(8,128)(2,1)S(1)}, u32[]{:S(2)}, u32[]{:S(2)}) collective-permute-start(bf16[288,1152]{1,0:T(8,128)(2,1)S(1)} %fusion.48), channel_id=1, source_target_pairs={{0,8},{4,12},{8,0},{12,4},{16,24},{20,28},{24,16},{28,20},{1,9},{5... | collective-permute-start | bytes 1990664 | tf_op jit(solution)/shard_map/ppermute | solution.py:691
  700.8 138.1 %collective-permute-start.39 = (bf16[2,288,1152]{2,1,0:T(8,128)(2,1)S(1)}, bf16[2,288,1152]{2,1,0:T(8,128)(2,1)}, u32[]{:S(2)}, u32[]{:S(2)}) collective-permute-start(bf16[2,288,1152]{2,1,0:T(8,128)(2,1)S(1)} %fusion.37), channel_id=1, source_target_pairs={{0,16},{4,20},{8,24},{12,28},{16,0},{20,4},{24,8},{28,12},{1,17},{... | collective-permute-start | bytes 3981320 | tf_op jit(solution)/shard_map/ppermute | solution.py:691
  717.5 137.1 %collective-permute-start.41 = (bf16[2,288,1152]{2,1,0:T(8,128)(2,1)}, bf16[2,288,1152]{2,1,0:T(8,128)(2,1)}, u32[]{:S(2)}, u32[]{:S(2)}) collective-permute-start(bf16[2,288,1152]{2,1,0:T(8,128)(2,1)} %fusion.38), channel_id=1, source_target_pairs={{0,16},{4,20},{8,24},{12,28},{16,0},{20,4},{24,8},{28,12},{1,17},{... | collective-permute-start | bytes 3981320 | tf_op jit(solution)/shard_map/ppermute | solution.py:691
  741.0 22.8 %collective-permute-start.12 = (bf16[768,512]{1,0:T(8,128)(2,1)}, bf16[768,512]{1,0:T(8,128)(2,1)S(1)}, u32[]{:S(2)}, u32[]{:S(2)}) collective-permute-start(bf16[768,512]{1,0:T(8,128)(2,1)} %get-tuple-element.79), channel_id=1, source_target_pairs={{4,0},{8,4},{12,8},{20,16},{24,20},{28,24},{5,1},{9,5},{13,9},{21,... | collective-permute-start | bytes 2359304 | tf_op jit(solution)/shard_map/ppermute | solution.py:710
  742.6 93.9 %collective-permute-start.13 = (bf16[768,512]{1,0:T(8,128)(2,1)}, bf16[768,512]{1,0:T(8,128)(2,1)S(1)}, u32[]{:S(2)}, u32[]{:S(2)}) collective-permute-start(bf16[768,512]{1,0:T(8,128)(2,1)} %get-tuple-element.80), channel_id=1, source_target_pairs={{8,0},{12,4},{24,16},{28,20},{9,1},{13,5},{25,17},{29,21},{10,2},{... | collective-permute-start | bytes 2359304 | tf_op jit(solution)/shard_map/ppermute | solution.py:710
  745.4 101.9 %collective-permute-start.32 = (bf16[4,288,512]{2,1,0:T(8,128)(2,1)}, bf16[4,288,512]{2,1,0:T(8,128)(2,1)}, u32[]{:S(2)}, u32[]{:S(2)}) collective-permute-start(bf16[4,288,512]{2,1,0:T(8,128)(2,1)} %get-tuple-element.132), channel_id=1, source_target_pairs={{0,4},{4,0},{8,12},{12,8},{16,20},{20,16},{24,28},{28,24},{1,5},{5... | collective-permute-start | bytes 3538952 | tf_op jit(solution)/shard_map/ppermute | solution.py:691
  763.8 86.6 %collective-permute-start.23 = (bf16[4,288,512]{2,1,0:T(8,128)(2,1)}, bf16[4,288,512]{2,1,0:T(8,128)(2,1)}, u32[]{:S(2)}, u32[]{:S(2)}) collective-permute-start(bf16[4,288,512]{2,1,0:T(8,128)(2,1)} %get-tuple-element.142), channel_id=1, source_target_pairs={{0,4},{4,0},{8,12},{12,8},{16,20},{20,16},{24,28},{28,24},{1,5},{5... | collective-permute-start | bytes 3538952 | tf_op jit(solution)/shard_map/ppermute | solution.py:691
  841.5 22.7 %collective-permute-start.40 = (bf16[288,1152]{1,0:T(8,128)(2,1)S(1)}, bf16[288,1152]{1,0:T(8,128)(2,1)S(1)}, u32[]{:S(2)}, u32[]{:S(2)}) collective-permute-start(bf16[288,1152]{1,0:T(8,128)(2,1)S(1)} %fusion.46), channel_id=1, source_target_pairs={{0,8},{4,12},{8,0},{12,4},{16,24},{20,28},{24,16},{28,20},{1,9},{5... | collective-permute-start | bytes 1990664 | tf_op jit(solution)/shard_map/ppermute | solution.py:691
  844.0 56.0 %collective-permute-start.27 = (bf16[4,288,512]{2,1,0:T(8,128)(2,1)S(1)}, bf16[4,288,512]{2,1,0:T(8,128)(2,1)S(1)}, u32[]{:S(2)}, u32[]{:S(2)}) collective-permute-start(bf16[4,288,512]{2,1,0:T(8,128)(2,1)S(1)} %get-tuple-element.137), channel_id=1, source_target_pairs={{0,4},{4,0},{8,12},{12,8},{16,20},{20,16},{24,28},{28,24},{1,5},{5... | collective-permute-start | bytes 3538952 | tf_op jit(solution)/shard_map/ppermute | solution.py:691
  864.4 24.6 %collective-permute-start.24 = (bf16[288,512]{1,0:T(8,128)(2,1)S(1)}, bf16[288,512]{1,0:T(8,128)(2,1)S(1)}, u32[]{:S(2)}, u32[]{:S(2)}) collective-permute-start(bf16[288,512]{1,0:T(8,128)(2,1)S(1)} %get-tuple-element.139), channel_id=1, source_target_pairs={{0,8},{4,12},{8,16},{12,20},{16,24},{20,28},{24,0},{28,4},{1,9},{5... | collective-permute-start | bytes 884744 | tf_op jit(solution)/shard_map/ppermute | solution.py:691
  868.6 30.4 %collective-permute-start.25 = (bf16[288,512]{1,0:T(8,128)(2,1)S(1)}, bf16[288,512]{1,0:T(8,128)(2,1)S(1)}, u32[]{:S(2)}, u32[]{:S(2)}) collective-permute-start(bf16[288,512]{1,0:T(8,128)(2,1)S(1)} %get-tuple-element.141), channel_id=1, source_target_pairs={{0,16},{4,20},{8,24},{12,28},{16,0},{20,4},{24,8},{28,12},{1,17},{... | collective-permute-start | bytes 884744 | tf_op jit(solution)/shard_map/ppermute | solution.py:691
  875.3 23.7 %collective-permute-start.26 = (bf16[288,512]{1,0:T(8,128)(2,1)S(1)}, bf16[288,512]{1,0:T(8,128)(2,1)S(1)}, u32[]{:S(2)}, u32[]{:S(2)}) collective-permute-start(bf16[288,512]{1,0:T(8,128)(2,1)S(1)} %get-tuple-element.140), channel_id=1, source_target_pairs={{0,24},{4,28},{8,0},{12,4},{16,8},{20,12},{24,16},{28,20},{1,25},{... | collective-permute-start | bytes 884744 | tf_op jit(solution)/shard_map/ppermute | solution.py:691
  888.9 37.6 %collective-permute-start.42 = (bf16[288,1152]{1,0:T(8,128)(2,1)S(1)}, bf16[288,1152]{1,0:T(8,128)(2,1)}, u32[]{:S(2)}, u32[]{:S(2)}) collective-permute-start(bf16[288,1152]{1,0:T(8,128)(2,1)S(1)} %fusion.47), channel_id=1, source_target_pairs={{0,8},{4,12},{8,0},{12,4},{16,24},{20,28},{24,16},{28,20},{1,9},{5... | collective-permute-start | bytes 1990664 | tf_op jit(solution)/shard_map/ppermute | solution.py:691
  934.2 23.4 %collective-permute-start.19 = (bf16[2,192,2304]{2,1,0:T(8,128)(2,1)S(1)}, bf16[2,192,2304]{2,1,0:T(8,128)(2,1)S(1)}, u32[]{:S(2)}, u32[]{:S(2)}) collective-permute-start(bf16[2,192,2304]{2,1,0:T(8,128)(2,1)S(1)} %pad_maximum_fusion.4), channel_id=1, source_target_pairs={{0,1},{1,0},{2,3},{3,2},{4,5},{5,4},{6,7},{7,6},{8,9},{9,8},{10,11... | collective-permute-start | bytes 5308424 | tf_op jit(solution)/shard_map/ppermute | solution.py:695
  (108 other events, 1524.5 us)
